TPU v7x, 128 devices: a whole 4x4x4 slice. The times are simulated.
128 devices in a mesh: pole: 4 (over z_hi, core), snode: 32 (over x, z_lo, y).
Axes of the slice: x: 4, y: 4, z: 4 (z_hi: 2, z_lo: 2; z = z_hi * 2 + z_lo), core: 2. Of those that a mesh axis runs over, the one named last changes fastest.
Arguments:
- root_inverse: bfloat16 [4, 2, 96, 12288, 128], P('pole', None, None, 'snode'), may hold values from -6 to 6
- factor_columns: bfloat16 [4, 32, 2, 1024, 128], P('pole', 'snode'), may hold values from -0.1875 to 0.1875
- diagonal_inverse: bfloat16 [4, 32, 2, 128, 128], P('pole', 'snode'), may hold values from -6 to 6
- pattern: int32 [32, 8], replicated, may hold values from 0 to 95, all different within a row
- pole_weights: float32 [4, 2], P('pole'), may hold values from -4 to 4
- pole_shifts: float32 [4, 2], P('pole'), may hold values from -2 to 2
Outputs:
- density_rows: float32 [2, 32, 32, 384, 128], P(None, 'snode', None, 'pole')
- density_diagonal: float32 [2, 32, 128, 128], P(None, 'snode', 'pole')
Inputs may be any that keep to these rules, and one draw needn't show every extreme that they name: Each row of pattern lists 8 different root blocks; every root block is listed by some row.
All inputs are finite; a program needn't handle non-finite values.
Results may differ from a plain program's by a relative error of at most 0.0029.
Values may be sent and summed in bfloat16 or wider, within the bound.
No kernel may reach another device: no remote copies, remote signals or barrier semaphores. Data moves between devices by JAX's collectives and lax.ppermute only.
A program may use at most 448 MiB of HBM per device.

v0:
```python
import jax
import jax.numpy as jnp
from jax import lax
from jax.experimental import pallas as pl
from jax.experimental.pallas import tpu as pltpu
from jax.sharding import PartitionSpec as P

B = 128
M = 8
ROWS = 384
PART = 96
DIAG = 32
SX, SZ, SY = 4, 2, 4
COST = pl.CostEstimate(flops=0, bytes_accessed=1, transcendentals=0)
AHEAD = 4
RING = (0, 1, -1, 2)
CORE = [(p, p ^ 1) for p in range(4)]
Z_HI = [(p, p ^ 2) for p in range(4)]
PLANES = [[(x * SZ + z) * SY + y for x in range(SX) for y in range(SY)] for z in range(SZ)]
ALL = [(a, b) for a in range(4) for b in range(4)]
INNER = [(a, b) for a in range(3) for b in range(3)]
OUTER = [(a, 3) for a in range(4)] + [(3, b) for b in range(3)]


def shift(dx=0, dz=0, dy=0):
    return [
        (
            (x * SZ + z) * SY + y,
            (((x + dx) % SX) * SZ + (z + dz) % SZ) * SY + (y + dy) % SY,
        )
        for x in range(SX)
        for z in range(SZ)
        for y in range(SY)
    ]


def across():
    nodes = SX * SZ * SY
    return [
        (p * nodes + a, (p ^ 2) * nodes + b) for p in range(4) for a, b in shift(dz=1)
    ]


def send(value, **by):
    return lax.ppermute(value, "snode", shift(**by))


def copies_body(plan, n_in, n_out, *refs):
    ins, outs = refs[:n_in], refs[n_in : n_in + n_out]
    stages, sems = refs[n_in + n_out : -1], refs[-1]
    first, second = [], []
    for n, (source, targets) in enumerate(plan):
        first.append(pltpu.make_async_copy(source(ins), stages[n], sems.at[n]))
        first[-1].start()
    for n, (source, targets) in enumerate(plan):
        first[n].wait()
        for target in targets:
            at = len(plan) + len(second)
            second.append(pltpu.make_async_copy(stages[n], target(outs), sems.at[at]))
            second[-1].start()
    for copy in second:
        copy.wait()


def copied(name, plan, piece, arrays, shapes):
    n_copies = len(plan) + sum(len(targets) for _, targets in plan)
    return pl.pallas_call(
        lambda *refs: copies_body(plan, len(arrays), len(shapes), *refs),
        out_shape=[jax.ShapeDtypeStruct(shape, jnp.bfloat16) for shape in shapes],
        in_specs=[pl.BlockSpec(memory_space=pl.ANY)] * len(arrays),
        out_specs=[pl.BlockSpec(memory_space=pltpu.HBM)] * len(shapes),
        scratch_shapes=[pltpu.VMEM(piece, jnp.bfloat16)] * len(plan)
        + [pltpu.SemaphoreType.DMA((n_copies,))],
        compiler_params=pltpu.CompilerParams(vmem_limit_bytes=8 * 2**20),
        cost_estimate=COST,
        name=name,
    )(*arrays)


CROSS = (2, 4, 2, 2 * B, B)


def own_rings(factor):
    parts = factor.reshape(2, 2, 2, 2 * B, B).transpose(1, 2, 0, 3, 4)
    arrays = [parts[0]] + [send(parts[0], dx=-d) for d in RING[1:]]
    arrays += [parts[1]] + [send(parts[1], dy=-d) for d in RING[1:]]
    plan = []
    for n in range(8):
        side, at = n // 4, n % 4
        targets = [
            lambda outs, s=side, at=at: outs[s].at[:, at],
            lambda outs, s=side, at=at: outs[2].at[s, :, at],
        ]
        plan.append((lambda ins, n=n: ins[n], targets))
    return copied("own_rings", plan, CROSS[:1] + CROSS[2:], arrays, [CROSS, CROSS, (2,) + CROSS])


def crossed(left, right):
    found = [
        (send(left, dy=-1), send(left, dy=1)),
        (send(right, dx=-1), send(right, dx=1)),
    ]
    arrays = [*found[0], *found[1]]
    plan = [
        (lambda ins, n=n: ins[n].at[1 - n % 2], [lambda outs, n=n: outs[n]]) for n in range(4)
    ]
    halves = copied("halves", plan, CROSS[1:], arrays, [CROSS[1:]] * 4)
    far = [
        (send(halves[1], dy=1), send(halves[0], dy=-1)),
        (send(halves[3], dx=1), send(halves[2], dx=-1)),
    ]
    return [left, *found[0], *far[0]], [right, *found[1], *far[1]]


def factor_copies(places, left, right, factors):
    dys = sorted({a for a, _ in places})
    dxs = sorted({b for _, b in places})
    found = []
    for side, ours, others in ((1, dxs, dys), (0, dys, dxs)):
        sources = (left, right)[side]
        for one in ours:
            far = [o for o in others if ((o, one) if side else (one, o)) in places]
            span = pl.ds(far[0], len(far))
            for h in range(2):
                ref = sources[one].at[h, span] if one < 3 else sources[3 + h].at[span]
                if side:
                    found.append((ref, factors.at[span, one, 2 + h]))
                else:
                    found.append((ref, factors.at[one, span, h]))
    return found


def column_body(places, with_own, meta, root, diag_inv, *refs):
    count = len(places)
    left, right = refs[:5], refs[5:10]
    keep, give, blocks, factors, column, total, root_sems, sems = refs[-8:]

    def fetch(j, i):
        slot = j % AHEAD
        for h in range(2):
            pltpu.make_async_copy(
                root.at[0, h, meta[j * M + i]],
                blocks.at[slot, i, :, pl.ds(h * B, B)],
                root_sems.at[slot],
            ).start()

    copies = [
        pltpu.make_async_copy(source, target, sems.at[n])
        for n, (source, target) in enumerate(factor_copies(places, left, right, factors))
    ]
    for copy in copies:
        copy.start()

    @pl.loop(0, (AHEAD - 1) * M)
    def _(n):
        fetch(n // M, n % M)

    for copy in copies:
        copy.wait()
    first_block = meta[count * M]
    pole = meta[count * M + 1]

    @pl.loop(0, count)
    def _(j):
        @pl.when(j + AHEAD - 1 < count)
        def _():
            for i in range(M):
                fetch(j + AHEAD - 1, i)

        dy = meta[count * M + 2 + 2 * j]
        dx = meta[count * M + 3 + 2 * j]
        slot = j % AHEAD

        pltpu.make_async_copy(blocks.at[slot], blocks.at[slot], root_sems.at[slot]).wait()

        product = None
        for i in range(M):
            at = pl.ds((i % 2) * B, B)
            real, imag = factors[dy, dx, i // 2, 0, at, :], factors[dy, dx, i // 2, 1, at, :]
            weights = jnp.concatenate(
                [
                    jnp.concatenate([real, imag], axis=1),
                    jnp.concatenate([-imag, real], axis=1),
                ],
                axis=0,
            )
            term = jnp.dot(blocks[slot, i], weights, preferred_element_type=jnp.float32)
            product = term if product is None else product + term
        column[...] = (-product).astype(jnp.bfloat16)
        total[...] = jnp.zeros_like(total)

        @pl.loop(0, M)
        def _(i):
            local = meta[j * M + i] - first_block

            @pl.when((local >= 0) & (local < ROWS // B))
            def _():
                rows = column[pl.ds(pl.multiple_of(local * B, B), B), :]
                real, imag = rows[:, :B], rows[:, B:]
                values = jnp.concatenate(
                    [
                        jnp.concatenate([real, imag], axis=1),
                        jnp.concatenate([-imag, real], axis=1),
                    ],
                    axis=0,
                )
                at = pl.ds(pl.multiple_of((i % 2) * B, B), B)
                factor = jnp.concatenate(
                    [factors[dy, dx, i // 2, 0, at, :], factors[dy, dx, i // 2, 1, at, :]], axis=0
                )
                total[...] += lax.dot_general(
                    factor, values, (((0,), (0,)), ((), ())), preferred_element_type=jnp.float32
                )

        if with_own:

            @pl.when(j == 0)
            def _():
                total[:, :B] -= diag_inv[0].astype(jnp.float32)
                total[:, B:] -= diag_inv[1].astype(jnp.float32)

        for n in range(4):
            out, e = (keep, give)[n >> 1], n & 1
            part = pole ^ ((e << 1) | (n >> 1))
            rows_at = pl.multiple_of(part * PART, PART)
            diag_at = pl.multiple_of(part * DIAG, DIAG)
            for h in range(2):
                lanes = slice(h * B, (h + 1) * B)
                out[e, j, h, :PART, :] = column[pl.ds(rows_at, PART), lanes]
                share = -total[pl.ds(diag_at, DIAG), lanes]
                coarse = share.astype(jnp.bfloat16)
                out[e, j, h, PART : PART + DIAG, :] = coarse
                rest = share - coarse.astype(jnp.float32)
                out[e, j, h, PART + DIAG :, :] = rest.astype(jnp.bfloat16)


def columns_of(places, with_own, left, right, meta, root, diag_inv, after):
    count = len(places)
    piece = jax.ShapeDtypeStruct((2, count, 2, PART + 2 * DIAG, B), jnp.bfloat16)
    n_copies = 2 * (len({a for a, _ in places}) + len({b for _, b in places}))
    return pl.pallas_call(
        lambda *refs: column_body(places, with_own, *refs),
        out_shape=[piece] * 2,
        in_specs=[
            pl.BlockSpec(memory_space=pltpu.SMEM),
            pl.BlockSpec(memory_space=pl.ANY),
            pl.BlockSpec(memory_space=pltpu.VMEM),
        ]
        + [pl.BlockSpec(memory_space=pl.ANY)] * (10 + len(after)),
        out_specs=[pl.BlockSpec(memory_space=pltpu.VMEM)] * 2,
        scratch_shapes=[
            pltpu.VMEM((AHEAD, M, ROWS, 2 * B), jnp.bfloat16),
            pltpu.VMEM((4, 4, 4, 2, 2 * B, B), jnp.bfloat16),
            pltpu.VMEM((ROWS, 2 * B), jnp.bfloat16),
            pltpu.VMEM((B, 2 * B), jnp.float32),
            pltpu.SemaphoreType.DMA((AHEAD,)),
            pltpu.SemaphoreType.DMA((n_copies,)),
        ],
        compiler_params=pltpu.CompilerParams(vmem_limit_bytes=60 * 2**20),
        cost_estimate=pl.CostEstimate(
            flops=2 * count * ROWS * 2 * M * B * 2 * B,
            bytes_accessed=count * (2 * M * B * B * 2 + 2 * M * ROWS * B * 2),
            transcendentals=0,
        ),
        name="columns",
    )(meta, root, diag_inv, *left, *right, *after)


def weighted(coef, which, mine, other):
    own_real, own_imag = mine[0].astype(jnp.float32), mine[1].astype(jnp.float32)
    far_real, far_imag = other[0].astype(jnp.float32), other[1].astype(jnp.float32)
    value = (
        coef[0, 2 * which] * own_imag
        + coef[0, 2 * which + 1] * own_real
        + coef[1, 2 * which] * far_imag
        + coef[1, 2 * which + 1] * far_real
    )
    return value[:PART], value[PART : PART + DIAG] + value[PART + DIAG :]


def pair_body(parts, coef, mine, other, *refs):
    outs = refs[-len(parts) :]

    @pl.loop(0, mine.shape[1])
    def _(j):
        for e, out in zip(parts, outs):
            for which in range(2):
                rows, diag = weighted(coef, which, mine[e, j], other[e, j])
                out[j, which, :PART, :] = rows.astype(jnp.bfloat16)
                out[j, which, PART:, :] = diag.astype(jnp.bfloat16)


def pair_sums(parts, coef, mine, other, after):
    count = mine.shape[1]
    return pl.pallas_call(
        lambda *refs: pair_body(parts, *refs),
        out_shape=[jax.ShapeDtypeStruct((count, 2, PART + DIAG, B), jnp.bfloat16)] * len(parts),
        in_specs=[pl.BlockSpec(memory_space=pltpu.SMEM)]
        + [pl.BlockSpec(memory_space=pltpu.VMEM)] * 2
        + [pl.BlockSpec(memory_space=pl.ANY)] * len(after),
        out_specs=[pl.BlockSpec(memory_space=pltpu.VMEM)] * len(parts),
        compiler_params=pltpu.CompilerParams(vmem_limit_bytes=16 * 2**20),
        cost_estimate=COST,
        name="pair_sums",
    )(coef, mine, other, *after)


def own_body(coef, order, mine, other, far, out):
    @pl.loop(0, far.shape[0])
    def _(j):
        at = order[j]
        for which in range(2):
            rows, diag = weighted(coef, which, mine[0, j], other[0, j])
            rows = rows + far[j, which, :PART, :].astype(jnp.float32)
            diag = diag + far[j, which, PART:, :].astype(jnp.float32)
            out[at, which, :PART, :] = rows.astype(jnp.bfloat16)
            out[at, which, PART:, :] = diag.astype(jnp.bfloat16)


def own_sums(coef, order, mine, other, far):
    return pl.pallas_call(
        own_body,
        out_shape=jax.ShapeDtypeStruct(far.shape, jnp.bfloat16),
        in_specs=[pl.BlockSpec(memory_space=pltpu.SMEM)] * 2
        + [pl.BlockSpec(memory_space=pltpu.VMEM)] * 3,
        out_specs=pl.BlockSpec(memory_space=pltpu.VMEM),
        compiler_params=pltpu.CompilerParams(vmem_limit_bytes=16 * 2**20),
        cost_estimate=COST,
        name="own_sums",
    )(coef, order, mine, other, far)


def next_body(order, *refs):
    out, start = refs[-1], 0
    for near, far in zip(refs[:-1:2], refs[1:-1:2]):

        @pl.loop(0, near.shape[0])
        def _(j, start=start, near=near, far=far):
            value = near[j].astype(jnp.float32) + far[j].astype(jnp.float32)
            out[order[start + j]] = value.astype(jnp.bfloat16)

        start += near.shape[0]


def next_sums(order, pairs):
    return pl.pallas_call(
        next_body,
        out_shape=jax.ShapeDtypeStruct((SX * SY, 2, PART + DIAG, B), jnp.bfloat16),
        in_specs=[pl.BlockSpec(memory_space=pltpu.SMEM)]
        + [pl.BlockSpec(memory_space=pltpu.VMEM)] * (2 * len(pairs)),
        out_specs=pl.BlockSpec(memory_space=pltpu.VMEM),
        compiler_params=pltpu.CompilerParams(vmem_limit_bytes=16 * 2**20),
        cost_estimate=COST,
        name="next_sums",
    )(order, *[piece for pair in pairs for piece in pair])


def place_body(plane, own, other, rows_out, diag_out):
    diag_out[...] = jnp.zeros_like(diag_out)
    for n, pieces in enumerate((own, other)):
        z = plane[n]

        @pl.loop(0, SX * SY)
        def _(j, pieces=pieces, z=z):
            owner = (j // SY * SZ + z) * SY + j % SY
            for which in range(2):
                rows_out[which, owner] = pieces[j, which, :PART, :].astype(jnp.float32)
            diag_out[...] += pieces[j, :, PART:, :].astype(jnp.float32)


def placed(plane, own, other):
    return pl.pallas_call(
        place_body,
        out_shape=[
            jax.ShapeDtypeStruct((2, SX * SZ * SY, PART, B), jnp.float32),
            jax.ShapeDtypeStruct((2, DIAG, B), jnp.float32),
        ],
        in_specs=[pl.BlockSpec(memory_space=pltpu.SMEM)]
        + [pl.BlockSpec(memory_space=pltpu.VMEM)] * 2,
        out_specs=[pl.BlockSpec(memory_space=pltpu.VMEM)] * 2,
        compiler_params=pltpu.CompilerParams(vmem_limit_bytes=16 * 2**20),
        name="placed",
    )(plane, own, other)


def in_plane(value):
    return lax.all_to_all(
        value, "snode", split_axis=0, concat_axis=0, axis_index_groups=PLANES, tiled=True
    )


def on_device(root_inverse, factor_columns, diagonal_inverse, pattern, pole_weights, pole_shifts):
    node = lax.axis_index("snode")
    pole = lax.axis_index("pole")
    x, z, y = node // (SZ * SY), (node // SY) % SZ, node % SY
    weight_real, weight_imag = pole_weights[0, 0], pole_weights[0, 1]
    shift_real, shift_imag = pole_shifts[0, 0], pole_shifts[0, 1]
    own_coef = jnp.stack(
        [
            weight_real,
            weight_imag,
            weight_real * shift_real - weight_imag * shift_imag,
            weight_real * shift_imag + weight_imag * shift_real,
        ]
    )[None]
    coef = jnp.concatenate([own_coef, lax.ppermute(own_coef, "pole", CORE)])
    left, right, both = own_rings(factor_columns[0, 0])
    both = send(both, dz=1)
    left, right = crossed(left, right)
    plan = [(lambda ins, n=n: ins[0].at[n], [lambda outs, n=n: outs[n]]) for n in range(2)]
    next_left, next_right = copied("next_rings", plan, CROSS, [both], [CROSS, CROSS])

    def chunk(dz, places, left, right, after):
        at = [(RING[a], RING[b]) for a, b in places]
        nodes = jnp.stack(
            [((x + dx) % SX * SZ + (z + dz) % SZ) * SY + (y + dy) % SY for dy, dx in at]
        )
        order = jnp.stack([(x + dx) % SX * SY + (y + dy) % SY for dy, dx in at])
        meta = jnp.concatenate(
            [
                pattern[nodes].reshape(-1),
                jnp.stack([node * (ROWS // B), pole]),
                jnp.array(places, jnp.int32).reshape(-1),
            ]
        ).astype(jnp.int32)
        keep, give = columns_of(
            places, dz == 0, left, right, meta, root_inverse, diagonal_inverse[0, 0], after
        )
        return keep, lax.ppermute(give, "pole", CORE), order.astype(jnp.int32)

    keep, got, order = chunk(0, ALL, left, right, (next_left,))
    (away,) = pair_sums((1,), coef, keep, got, ())
    sums = own_sums(coef, order, keep, got, lax.ppermute(away, "pole", Z_HI))
    own = in_plane(sums)
    left, right = crossed(next_left, next_right)
    keep, got, inner = chunk(1, INNER, left, right, (away,))
    near, away = pair_sums((0, 1), coef, keep, got, ())
    keep, got, outer = chunk(1, OUTER, left, right, (away,))
    pairs = [(near, away), pair_sums((0, 1), coef, keep, got, (sums,))]
    pairs = [
        (send(near, dz=1), lax.ppermute(away, ("pole", "snode"), across()))
        for near, away in pairs
    ]
    other = in_plane(next_sums(jnp.concatenate([inner, outer]), pairs))
    rows_out, diag_out = placed(jnp.stack([z, 1 - z]).astype(jnp.int32), own, other)
    return rows_out[:, None], diag_out[:, None]


def solution(mesh):
    in_specs = (
        P("pole", None, None, "snode", None),
        P("pole", "snode", None, None, None),
        P("pole", "snode", None, None, None),
        P(),
        P("pole", None),
        P("pole", None),
    )
    out_specs = (P(None, "snode", None, "pole", None), P(None, "snode", "pole", None))
    return jax.shard_map(
        on_device, mesh=mesh, in_specs=in_specs, out_specs=out_specs, check_vma=False
    )
```

profile of v0, /device:TPU:0, one launch (start us, length us, event | category | flops | bytes accessed | tf_op | source)
XLA Modules:
  0.0 254.7 jit_solution(8657150282282792251)
XLA Ops:
  10.0 5.9 %collective-permute-done.1.refs_1_ = bf16[2,2,256,128]{3,2,1,0:T(8,128)(2,1)S(1)} collective-permute-done((bf16[2,2,256,128]{3,2,1,0:T(8,128)(2,1)S(1)}, bf16[2,2,256,128]{3,2,1,0:T(8,128)(2,1)S(1)}, u32[]{:S(2)}, u32[]{:S(2)}) %collective-permute-start.1) | collective-permute-done | bytes 262176 | tf_op jit(solution)/shard_map/ppermute | solution.py:45
  15.8 3.2 %collective-permute-start.6 = (bf16[2,2,256,128]{3,2,1,0:T(8,128)(2,1)S(1)}, bf16[2,2,256,128]{3,2,1,0:T(8,128)(2,1)S(1)}, u32[]{:S(2)}, u32[]{:S(2)}) collective-permute-start(bf16[2,2,256,128]{3,2,1,0:T(8,128)(2,1)S(1)} %get-tuple-element.56.refs_4_), channel_id=1, source_target_pairs={{0,2},{1,3},{2,0},{3,1},{4,6},{5,7},{6,4},{7,5},{8,10},{9,11},{10,... | collective-permute-start | bytes 786440 | tf_op jit(solution)/shard_map/ppermute | solution.py:45
  27.5 3.1 %collective-permute-start.7 = (bf16[2,4,2,256,128]{4,3,2,1,0:T(8,128)(2,1)S(1)}, bf16[2,4,2,256,128]{4,3,2,1,0:T(8,128)(2,1)S(1)}, u32[]{:S(2)}, u32[]{:S(2)}) collective-permute-start(bf16[2,4,2,256,128]{4,3,2,1,0:T(8,128)(2,1)S(1)} %get-tuple-element.27.refs_3_), channel_id=1, source_target_pairs={{0,3},{1,0},{2,1},{3,2},{4,7},{5,4},{6,5},{7,6},{8,11},{9,8},{10,9... | collective-permute-start | bytes 3145736 | tf_op jit(solution)/shard_map/ppermute | solution.py:45
  30.6 4.4 %collective-permute-start.9 = (bf16[2,4,2,256,128]{4,3,2,1,0:T(8,128)(2,1)S(1)}, bf16[2,4,2,256,128]{4,3,2,1,0:T(8,128)(2,1)S(1)}, u32[]{:S(2)}, u32[]{:S(2)}) collective-permute-start(bf16[2,4,2,256,128]{4,3,2,1,0:T(8,128)(2,1)S(1)} %get-tuple-element.28.refs_8_), channel_id=1, source_target_pairs={{0,24},{1,25},{2,26},{3,27},{4,28},{5,29},{6,30},{7,31},{8,0},{9,1... | collective-permute-start | bytes 3145736 | tf_op jit(solution)/shard_map/ppermute | solution.py:45
  34.9 13.4 %collective-permute-done.7.refs_0_.refs_4_ = bf16[2,4,2,256,128]{4,3,2,1,0:T(8,128)(2,1)S(1)} collective-permute-done((bf16[2,4,2,256,128]{4,3,2,1,0:T(8,128)(2,1)S(1)}, bf16[2,4,2,256,128]{4,3,2,1,0:T(8,128)(2,1)S(1)}, u32[]{:S(2)}, u32[]{:S(2)}) %collective-permute-start.7) | collective-permute-done | bytes 1048608 | tf_op jit(solution)/shard_map/ppermute | solution.py:45
  49.5 5.5 %collective-permute-done.9.refs_2_.refs_9_ = bf16[2,4,2,256,128]{4,3,2,1,0:T(8,128)(2,1)S(1)} collective-permute-done((bf16[2,4,2,256,128]{4,3,2,1,0:T(8,128)(2,1)S(1)}, bf16[2,4,2,256,128]{4,3,2,1,0:T(8,128)(2,1)S(1)}, u32[]{:S(2)}, u32[]{:S(2)}) %collective-permute-start.9) | collective-permute-done | bytes 1048608 | tf_op jit(solution)/shard_map/ppermute | solution.py:45
  55.0 3.4 %collective-permute-done.10.refs_3_.refs_10_ = bf16[2,4,2,256,128]{4,3,2,1,0:T(8,128)(2,1)S(1)} collective-permute-done((bf16[2,4,2,256,128]{4,3,2,1,0:T(8,128)(2,1)S(1)}, bf16[2,4,2,256,128]{4,3,2,1,0:T(8,128)(2,1)S(1)}, u32[]{:S(2)}, u32[]{:S(2)}) %collective-permute-start.10) | collective-permute-done | bytes 1048608 | tf_op jit(solution)/shard_map/ppermute | solution.py:45
  63.5 3.2 %collective-permute-start.14 = (bf16[4,2,256,128]{3,2,1,0:T(8,128)(2,1)}, bf16[4,2,256,128]{3,2,1,0:T(8,128)(2,1)}, u32[]{:S(2)}, u32[]{:S(2)}) collective-permute-start(bf16[4,2,256,128]{3,2,1,0:T(8,128)(2,1)} %get-tuple-element.32), channel_id=1, source_target_pairs={{0,24},{1,25},{2,26},{3,27},{4,28},{5,29},{6,30},{7,31},{8,0},{9,1... | collective-permute-start | bytes 1572872 | tf_op jit(solution)/shard_map/ppermute | solution.py:45
  74.6 21.8 %columns.3 = (bf16[2,16,2,160,128]{4,3,2,1,0:T(8,128)(2,1)}, bf16[2,16,2,160,128]{4,3,2,1,0:T(8,128)(2,1)}) custom-call(s32[162]{0:T(256)} %pad_add_fusion.refs_0_, bf16[1,2,96,384,128]{4,3,2,1,0:T(8,128)(2,1)} %refs_1_.5, bf16[2,128,128]{2,1,0:T(8,128)(2,1)} %bitcast.80, bf16[2,4,2,256,128]{4,3,2,1,0:T(8,128)(2,1)} %copy-done.10, ...), custom_call_target="tpu_custom_call" | custom-call | flops 6442450944 | bytes 33554432 | tf_op jit(solution)/shard_map/columns/pallas_call | solution.py:241
  98.5 3.3 %collective-permute-start.20 = (bf16[2,4,2,256,128]{4,3,2,1,0:T(8,128)(2,1)}, bf16[2,4,2,256,128]{4,3,2,1,0:T(8,128)(2,1)}, u32[]{:S(2)}, u32[]{:S(2)}) collective-permute-start(bf16[2,4,2,256,128]{4,3,2,1,0:T(8,128)(2,1)} %get-tuple-element.37.refs_8_), channel_id=1, source_target_pairs={{0,24},{1,25},{2,26},{3,27},{4,28},{5,29},{6,30},{7,31},{8,0},{9,1... | collective-permute-start | bytes 3145736 | tf_op jit(solution)/shard_map/ppermute | solution.py:45
  109.2 13.1 %collective-permute-done.18.refs_0_.refs_4_ = bf16[2,4,2,256,128]{4,3,2,1,0:T(8,128)(2,1)} collective-permute-done((bf16[2,4,2,256,128]{4,3,2,1,0:T(8,128)(2,1)}, bf16[2,4,2,256,128]{4,3,2,1,0:T(8,128)(2,1)}, u32[]{:S(2)}, u32[]{:S(2)}) %collective-permute-start.18) | collective-permute-done | bytes 1048608 | tf_op jit(solution)/shard_map/ppermute | solution.py:45
  124.9 3.4 %collective-permute-done.21.refs_3_.refs_10_ = bf16[2,4,2,256,128]{4,3,2,1,0:T(8,128)(2,1)} collective-permute-done((bf16[2,4,2,256,128]{4,3,2,1,0:T(8,128)(2,1)}, bf16[2,4,2,256,128]{4,3,2,1,0:T(8,128)(2,1)}, u32[]{:S(2)}, u32[]{:S(2)}) %collective-permute-start.21) | collective-permute-done | bytes 1048608 | tf_op jit(solution)/shard_map/ppermute | solution.py:45
  134.0 3.2 %collective-permute-start.25 = (bf16[4,2,256,128]{3,2,1,0:T(8,128)(2,1)S(1)}, bf16[4,2,256,128]{3,2,1,0:T(8,128)(2,1)}, u32[]{:S(2)}, u32[]{:S(2)}) collective-permute-start(bf16[4,2,256,128]{3,2,1,0:T(8,128)(2,1)S(1)} %get-tuple-element.41), channel_id=1, source_target_pairs={{0,24},{1,25},{2,26},{3,27},{4,28},{5,29},{6,30},{7,31},{8,0},{9,1... | collective-permute-start | bytes 1572872 | tf_op jit(solution)/shard_map/ppermute | solution.py:45
  147.8 13.5 %columns.4 = (bf16[2,9,2,160,128]{4,3,2,1,0:T(8,128)(2,1)}, bf16[2,9,2,160,128]{4,3,2,1,0:T(8,128)(2,1)}) custom-call(s32[92]{0:T(128)} %pad_add_fusion.2.refs_0_, bf16[1,2,96,384,128]{4,3,2,1,0:T(8,128)(2,1)} %refs_1_.5, bf16[2,128,128]{2,1,0:T(8,128)(2,1)} %bitcast.81, bf16[2,4,2,256,128]{4,3,2,1,0:T(8,128)(2,1)} %get-tuple-element.34.refs_13_.refs_3_, ...), custom_call_target="tpu_custom_call" | custom-call | flops 3623878656 | bytes 18874368 | tf_op jit(solution)/shard_map/columns/pallas_call | solution.py:241
  161.7 3.8 %collective-permute-start.17 = (bf16[16,2,128,128]{3,2,1,0:T(8,128)(2,1)}, bf16[16,2,128,128]{3,2,1,0:T(8,128)(2,1)}, u32[]{:S(2)}, u32[]{:S(2)}) collective-permute-start(bf16[16,2,128,128]{3,2,1,0:T(8,128)(2,1)} %copy-done.7), channel_id=1, source_target_pairs={{0,64},{32,96},{64,0},{96,32},{1,65},{33,97},{65,1},{97,33},{2,66}... | collective-permute-start | bytes 3145736 | tf_op jit(solution)/shard_map/ppermute | solution.py:433
  172.3 11.4 %columns.5 = (bf16[2,7,2,160,128]{4,3,2,1,0:T(8,128)(2,1)}, bf16[2,7,2,160,128]{4,3,2,1,0:T(8,128)(2,1)}) custom-call(s32[72]{0:T(128)} %pad_add_fusion.3.refs_0_, bf16[1,2,96,384,128]{4,3,2,1,0:T(8,128)(2,1)} %refs_1_.5, bf16[2,128,128]{2,1,0:T(8,128)(2,1)} %bitcast.82, bf16[2,4,2,256,128]{4,3,2,1,0:T(8,128)(2,1)} %get-tuple-element.34.refs_13_.refs_3_, ...), custom_call_target="tpu_custom_call" | custom-call | flops 2818572288 | bytes 14680064 | tf_op jit(solution)/shard_map/columns/pallas_call | solution.py:241
  184.1 5.5 %collective-permute-done.17.far = bf16[16,2,128,128]{3,2,1,0:T(8,128)(2,1)} collective-permute-done((bf16[16,2,128,128]{3,2,1,0:T(8,128)(2,1)}, bf16[16,2,128,128]{3,2,1,0:T(8,128)(2,1)}, u32[]{:S(2)}, u32[]{:S(2)}) %collective-permute-start.17) | collective-permute-done | bytes 1048608 | tf_op jit(solution)/shard_map/ppermute | solution.py:433
  189.6 3.3 %own_sums.1.refs_3_ = bf16[16,2,128,128]{3,2,1,0:T(8,128)(2,1)S(1)} custom-call(f32[2,4]{1,0:T(2,128)S(1)} %pad_maximum_fusion.refs_0_.coef, s32[16]{0:T(128)S(1)} %stack.222.order, bf16[2,16,2,160,128]{4,3,2,1,0:T(8,128)(2,1)S(1)} %copy-done, bf16[2,16,2,160,128]{4,3,2,1,0:T(8,128)(2,1)} %collective-permute-done.16.refs_2_.other, ...), custom_call_target="tpu_custom_call" | custom-call | bytes 1 | tf_op jit(solution)/shard_map/own_sums/pallas_call | solution.py:321
  193.9 5.3 %all-to-all-start = ((bf16[16,2,128,128]{3,2,1,0:T(8,128)(2,1)}), bf16[16,2,128,128]{3,2,1,0:T(8,128)(2,1)S(1)}, u32[]{:S(2)}, u32[]{:S(2)}) async-start(bf16[16,2,128,128]{3,2,1,0:T(8,128)(2,1)} %copy-done.1), calls=%async_computation | async-start | bytes 2097152 | tf_op jit(solution)/shard_map/all_to_all | solution.py:387
  210.7 5.9 %collective-permute-done.27.refs_0_ = bf16[9,2,128,128]{3,2,1,0:T(8,128)(2,1)S(1)} collective-permute-done((bf16[9,2,128,128]{3,2,1,0:T(8,128)(2,1)}, bf16[9,2,128,128]{3,2,1,0:T(8,128)(2,1)S(1)}, u32[]{:S(2)}, u32[]{:S(2)}) %collective-permute-start.27) | collective-permute-done | bytes 589856 | tf_op jit(solution)/shard_map/ppermute | solution.py:45
  216.5 3.2 %collective-permute-done.28.refs_1_ = bf16[9,2,128,128]{3,2,1,0:T(8,128)(2,1)} collective-permute-done((bf16[9,2,128,128]{3,2,1,0:T(8,128)(2,1)S(1)}, bf16[9,2,128,128]{3,2,1,0:T(8,128)(2,1)}, u32[]{:S(2)}, u32[]{:S(2)}) %collective-permute-start.28) | collective-permute-done | bytes 589856 | tf_op jit(solution)/shard_map/ppermute | solution.py:441
  219.7 5.3 %collective-permute-done.30.refs_2_ = bf16[7,2,128,128]{3,2,1,0:T(8,128)(2,1)S(1)} collective-permute-done((bf16[7,2,128,128]{3,2,1,0:T(8,128)(2,1)}, bf16[7,2,128,128]{3,2,1,0:T(8,128)(2,1)S(1)}, u32[]{:S(2)}, u32[]{:S(2)}) %collective-permute-start.30) | collective-permute-done | bytes 458784 | tf_op jit(solution)/shard_map/ppermute | solution.py:45
  229.9 6.9 %all-to-all-start.1 = ((bf16[16,2,128,128]{3,2,1,0:T(8,128)(2,1)}), bf16[16,2,128,128]{3,2,1,0:T(8,128)(2,1)S(1)}, u32[]{:S(2)}, u32[]{:S(2)}) async-start(bf16[16,2,128,128]{3,2,1,0:T(8,128)(2,1)} %next_sums.1), calls=%async_computation.1 | async-start | bytes 2097152 | tf_op jit(solution)/shard_map/all_to_all | solution.py:387
  236.8 15.1 %all-to-all-done.1.other = bf16[16,2,128,128]{3,2,1,0:T(8,128)(2,1)S(1)} async-done(((bf16[16,2,128,128]{3,2,1,0:T(8,128)(2,1)}), bf16[16,2,128,128]{3,2,1,0:T(8,128)(2,1)S(1)}, u32[]{:S(2)}, u32[]{:S(2)}) %all-to-all-start.1) | async-done | bytes 1048608 | tf_op jit(solution)/shard_map/all_to_all | solution.py:387
  (126 shorter events, 82.6 us)
Async XLA Ops:
  1.8 14.1 %collective-permute-start.1 = (bf16[2,2,256,128]{3,2,1,0:T(8,128)(2,1)S(1)}, bf16[2,2,256,128]{3,2,1,0:T(8,128)(2,1)S(1)}, u32[]{:S(2)}, u32[]{:S(2)}) collective-permute-start(bf16[2,2,256,128]{3,2,1,0:T(8,128)(2,1)S(1)} %get-tuple-element.57.refs_0_), channel_id=1, source_target_pairs={{0,24},{1,25},{2,26},{3,27},{4,28},{5,29},{6,30},{7,31},{8,0},{9,1... | collective-permute-start | bytes 786440 | tf_op jit(solution)/shard_map/ppermute | solution.py:45
  4.7 14.6 %collective-permute-start.2 = (bf16[2,2,256,128]{3,2,1,0:T(8,128)(2,1)S(1)}, bf16[2,2,256,128]{3,2,1,0:T(8,128)(2,1)S(1)}, u32[]{:S(2)}, u32[]{:S(2)}) collective-permute-start(bf16[2,2,256,128]{3,2,1,0:T(8,128)(2,1)S(1)} %get-tuple-element.57.refs_0_), channel_id=1, source_target_pairs={{0,8},{1,9},{2,10},{3,11},{4,12},{5,13},{6,14},{7,15},{8,16},{9,17... | collective-permute-start | bytes 786440 | tf_op jit(solution)/shard_map/ppermute | solution.py:45
  4.7 14.6 %collective-permute-start.3 = (bf16[2,2,256,128]{3,2,1,0:T(8,128)(2,1)S(1)}, bf16[2,2,256,128]{3,2,1,0:T(8,128)(2,1)S(1)}, u32[]{:S(2)}, u32[]{:S(2)}) collective-permute-start(bf16[2,2,256,128]{3,2,1,0:T(8,128)(2,1)S(1)} %get-tuple-element.57.refs_0_), channel_id=1, source_target_pairs={{0,16},{1,17},{2,18},{3,19},{4,20},{5,21},{6,22},{7,23},{8,24},{9,... | collective-permute-start | bytes 786440 | tf_op jit(solution)/shard_map/ppermute | solution.py:45
  25.4 44.1 %collective-permute-start.15 = (bf16[2,2,4,2,256,128]{5,4,3,2,1,0:T(8,128)(2,1)}, bf16[2,2,4,2,256,128]{5,4,3,2,1,0:T(8,128)(2,1)S(1)}, u32[]{:S(2)}, u32[]{:S(2)}) collective-permute-start(bf16[2,2,4,2,256,128]{5,4,3,2,1,0:T(8,128)(2,1)} %get-tuple-element.33), channel_id=1, source_target_pairs={{0,4},{1,5},{2,6},{3,7},{4,0},{5,1},{6,2},{7,3},{8,12},{9,13},{10,... | collective-permute-start | bytes 6291464 | tf_op jit(solution)/shard_map/ppermute | solution.py:45
  27.5 20.8 %collective-permute-start.7 = (bf16[2,4,2,256,128]{4,3,2,1,0:T(8,128)(2,1)S(1)}, bf16[2,4,2,256,128]{4,3,2,1,0:T(8,128)(2,1)S(1)}, u32[]{:S(2)}, u32[]{:S(2)}) collective-permute-start(bf16[2,4,2,256,128]{4,3,2,1,0:T(8,128)(2,1)S(1)} %get-tuple-element.27.refs_3_), channel_id=1, source_target_pairs={{0,3},{1,0},{2,1},{3,2},{4,7},{5,4},{6,5},{7,6},{8,11},{9,8},{10,9... | collective-permute-start | bytes 3145736 | tf_op jit(solution)/shard_map/ppermute | solution.py:45
  30.6 18.9 %collective-permute-start.8 = (bf16[2,4,2,256,128]{4,3,2,1,0:T(8,128)(2,1)S(1)}, bf16[2,4,2,256,128]{4,3,2,1,0:T(8,128)(2,1)S(1)}, u32[]{:S(2)}, u32[]{:S(2)}) collective-permute-start(bf16[2,4,2,256,128]{4,3,2,1,0:T(8,128)(2,1)S(1)} %get-tuple-element.27.refs_3_), channel_id=1, source_target_pairs={{0,1},{1,2},{2,3},{3,0},{4,5},{5,6},{6,7},{7,4},{8,9},{9,10},{10,1... | collective-permute-start | bytes 3145736 | tf_op jit(solution)/shard_map/ppermute | solution.py:45
  30.6 24.4 %collective-permute-start.9 = (bf16[2,4,2,256,128]{4,3,2,1,0:T(8,128)(2,1)S(1)}, bf16[2,4,2,256,128]{4,3,2,1,0:T(8,128)(2,1)S(1)}, u32[]{:S(2)}, u32[]{:S(2)}) collective-permute-start(bf16[2,4,2,256,128]{4,3,2,1,0:T(8,128)(2,1)S(1)} %get-tuple-element.28.refs_8_), channel_id=1, source_target_pairs={{0,24},{1,25},{2,26},{3,27},{4,28},{5,29},{6,30},{7,31},{8,0},{9,1... | collective-permute-start | bytes 3145736 | tf_op jit(solution)/shard_map/ppermute | solution.py:45
  34.9 23.5 %collective-permute-start.10 = (bf16[2,4,2,256,128]{4,3,2,1,0:T(8,128)(2,1)S(1)}, bf16[2,4,2,256,128]{4,3,2,1,0:T(8,128)(2,1)S(1)}, u32[]{:S(2)}, u32[]{:S(2)}) collective-permute-start(bf16[2,4,2,256,128]{4,3,2,1,0:T(8,128)(2,1)S(1)} %get-tuple-element.28.refs_8_), channel_id=1, source_target_pairs={{0,8},{1,9},{2,10},{3,11},{4,12},{5,13},{6,14},{7,15},{8,16},{9,17... | collective-permute-start | bytes 3145736 | tf_op jit(solution)/shard_map/ppermute | solution.py:45
  96.3 42.1 %collective-permute-start.16 = (bf16[2,16,2,160,128]{4,3,2,1,0:T(8,128)(2,1)}, bf16[2,16,2,160,128]{4,3,2,1,0:T(8,128)(2,1)}, u32[]{:S(2)}, u32[]{:S(2)}) collective-permute-start(bf16[2,16,2,160,128]{4,3,2,1,0:T(8,128)(2,1)} %get-tuple-element.36), channel_id=1, source_target_pairs={{0,32},{32,0},{64,96},{96,64},{1,33},{33,1},{65,97},{97,65},{2,34}... | collective-permute-start | bytes 7864328 | tf_op jit(solution)/shard_map/ppermute | solution.py:429
  96.4 25.9 %collective-permute-start.18 = (bf16[2,4,2,256,128]{4,3,2,1,0:T(8,128)(2,1)}, bf16[2,4,2,256,128]{4,3,2,1,0:T(8,128)(2,1)}, u32[]{:S(2)}, u32[]{:S(2)}) collective-permute-start(bf16[2,4,2,256,128]{4,3,2,1,0:T(8,128)(2,1)} %get-tuple-element.34.refs_13_.refs_3_), channel_id=1, source_target_pairs={{0,3},{1,0},{2,1},{3,2},{4,7},{5,4},{6,5},{7,6},{8,11},{9,8},{10,9... | collective-permute-start | bytes 3145736 | tf_op jit(solution)/shard_map/ppermute | solution.py:45
  97.2 26.8 %collective-permute-start.19 = (bf16[2,4,2,256,128]{4,3,2,1,0:T(8,128)(2,1)}, bf16[2,4,2,256,128]{4,3,2,1,0:T(8,128)(2,1)}, u32[]{:S(2)}, u32[]{:S(2)}) collective-permute-start(bf16[2,4,2,256,128]{4,3,2,1,0:T(8,128)(2,1)} %get-tuple-element.34.refs_13_.refs_3_), channel_id=1, source_target_pairs={{0,1},{1,2},{2,3},{3,0},{4,5},{5,6},{6,7},{7,4},{8,9},{9,10},{10,1... | collective-permute-start | bytes 3145736 | tf_op jit(solution)/shard_map/ppermute | solution.py:45
  98.5 26.4 %collective-permute-start.20 = (bf16[2,4,2,256,128]{4,3,2,1,0:T(8,128)(2,1)}, bf16[2,4,2,256,128]{4,3,2,1,0:T(8,128)(2,1)}, u32[]{:S(2)}, u32[]{:S(2)}) collective-permute-start(bf16[2,4,2,256,128]{4,3,2,1,0:T(8,128)(2,1)} %get-tuple-element.37.refs_8_), channel_id=1, source_target_pairs={{0,24},{1,25},{2,26},{3,27},{4,28},{5,29},{6,30},{7,31},{8,0},{9,1... | collective-permute-start | bytes 3145736 | tf_op jit(solution)/shard_map/ppermute | solution.py:45
  101.8 26.5 %collective-permute-start.21 = (bf16[2,4,2,256,128]{4,3,2,1,0:T(8,128)(2,1)}, bf16[2,4,2,256,128]{4,3,2,1,0:T(8,128)(2,1)}, u32[]{:S(2)}, u32[]{:S(2)}) collective-permute-start(bf16[2,4,2,256,128]{4,3,2,1,0:T(8,128)(2,1)} %get-tuple-element.37.refs_8_), channel_id=1, source_target_pairs={{0,8},{1,9},{2,10},{3,11},{4,12},{5,13},{6,14},{7,15},{8,16},{9,17... | collective-permute-start | bytes 3145736 | tf_op jit(solution)/shard_map/ppermute | solution.py:45
  130.7 14.4 %collective-permute-start.22 = (bf16[4,2,256,128]{3,2,1,0:T(8,128)(2,1)}, bf16[4,2,256,128]{3,2,1,0:T(8,128)(2,1)}, u32[]{:S(2)}, u32[]{:S(2)}) collective-permute-start(bf16[4,2,256,128]{3,2,1,0:T(8,128)(2,1)} %get-tuple-element.38), channel_id=1, source_target_pairs={{0,1},{1,2},{2,3},{3,0},{4,5},{5,6},{6,7},{7,4},{8,9},{9,10},{10,1... | collective-permute-start | bytes 1572872 | tf_op jit(solution)/shard_map/ppermute | solution.py:45
  131.2 13.9 %collective-permute-start.23 = (bf16[4,2,256,128]{3,2,1,0:T(8,128)(2,1)}, bf16[4,2,256,128]{3,2,1,0:T(8,128)(2,1)}, u32[]{:S(2)}, u32[]{:S(2)}) collective-permute-start(bf16[4,2,256,128]{3,2,1,0:T(8,128)(2,1)} %get-tuple-element.39), channel_id=1, source_target_pairs={{0,3},{1,0},{2,1},{3,2},{4,7},{5,4},{6,5},{7,6},{8,11},{9,8},{10,9... | collective-permute-start | bytes 1572872 | tf_op jit(solution)/shard_map/ppermute | solution.py:45
  134.0 13.8 %collective-permute-start.24 = (bf16[4,2,256,128]{3,2,1,0:T(8,128)(2,1)}, bf16[4,2,256,128]{3,2,1,0:T(8,128)(2,1)}, u32[]{:S(2)}, u32[]{:S(2)}) collective-permute-start(bf16[4,2,256,128]{3,2,1,0:T(8,128)(2,1)} %get-tuple-element.40), channel_id=1, source_target_pairs={{0,8},{1,9},{2,10},{3,11},{4,12},{5,13},{6,14},{7,15},{8,16},{9,17... | collective-permute-start | bytes 1572872 | tf_op jit(solution)/shard_map/ppermute | solution.py:45
  161.7 27.9 %collective-permute-start.17 = (bf16[16,2,128,128]{3,2,1,0:T(8,128)(2,1)}, bf16[16,2,128,128]{3,2,1,0:T(8,128)(2,1)}, u32[]{:S(2)}, u32[]{:S(2)}) collective-permute-start(bf16[16,2,128,128]{3,2,1,0:T(8,128)(2,1)} %copy-done.7), channel_id=1, source_target_pairs={{0,64},{32,96},{64,0},{96,32},{1,65},{33,97},{65,1},{97,33},{2,66}... | collective-permute-start | bytes 3145736 | tf_op jit(solution)/shard_map/ppermute | solution.py:433
  183.8 20.5 %collective-permute-start.29 = (bf16[2,7,2,160,128]{4,3,2,1,0:T(8,128)(2,1)}, bf16[2,7,2,160,128]{4,3,2,1,0:T(8,128)(2,1)}, u32[]{:S(2)}, u32[]{:S(2)}) collective-permute-start(bf16[2,7,2,160,128]{4,3,2,1,0:T(8,128)(2,1)} %get-tuple-element.47), channel_id=1, source_target_pairs={{0,32},{32,0},{64,96},{96,64},{1,33},{33,1},{65,97},{97,65},{2,34}... | collective-permute-start | bytes 3440648 | tf_op jit(solution)/shard_map/ppermute | solution.py:429
  193.9 36.0 %all-to-all-start = ((bf16[16,2,128,128]{3,2,1,0:T(8,128)(2,1)}), bf16[16,2,128,128]{3,2,1,0:T(8,128)(2,1)S(1)}, u32[]{:S(2)}, u32[]{:S(2)}) async-start(bf16[16,2,128,128]{3,2,1,0:T(8,128)(2,1)} %copy-done.1), calls=%async_computation | async-start | bytes 2097152 | tf_op jit(solution)/shard_map/all_to_all | solution.py:387
  199.2 17.4 %collective-permute-start.27 = (bf16[9,2,128,128]{3,2,1,0:T(8,128)(2,1)}, bf16[9,2,128,128]{3,2,1,0:T(8,128)(2,1)S(1)}, u32[]{:S(2)}, u32[]{:S(2)}) collective-permute-start(bf16[9,2,128,128]{3,2,1,0:T(8,128)(2,1)} %copy-done.14), channel_id=1, source_target_pairs={{0,4},{1,5},{2,6},{3,7},{4,0},{5,1},{6,2},{7,3},{8,12},{9,13},{10,... | collective-permute-start | bytes 1769480 | tf_op jit(solution)/shard_map/ppermute | solution.py:45
  202.1 17.6 %collective-permute-start.28 = (bf16[9,2,128,128]{3,2,1,0:T(8,128)(2,1)S(1)}, bf16[9,2,128,128]{3,2,1,0:T(8,128)(2,1)}, u32[]{:S(2)}, u32[]{:S(2)}) collective-permute-start(bf16[9,2,128,128]{3,2,1,0:T(8,128)(2,1)S(1)} %copy-done.13), channel_id=1, source_target_pairs={{0,68},{1,69},{2,70},{3,71},{4,64},{5,65},{6,66},{7,67},{8,76},{9,... | collective-permute-start | bytes 1769480 | tf_op jit(solution)/shard_map/ppermute | solution.py:441
  208.6 16.4 %collective-permute-start.30 = (bf16[7,2,128,128]{3,2,1,0:T(8,128)(2,1)}, bf16[7,2,128,128]{3,2,1,0:T(8,128)(2,1)S(1)}, u32[]{:S(2)}, u32[]{:S(2)}) collective-permute-start(bf16[7,2,128,128]{3,2,1,0:T(8,128)(2,1)} %get-tuple-element.48), channel_id=1, source_target_pairs={{0,4},{1,5},{2,6},{3,7},{4,0},{5,1},{6,2},{7,3},{8,12},{9,13},{10,... | collective-permute-start | bytes 1376264 | tf_op jit(solution)/shard_map/ppermute | solution.py:45
  209.9 17.6 %collective-permute-start.31 = (bf16[7,2,128,128]{3,2,1,0:T(8,128)(2,1)}, bf16[7,2,128,128]{3,2,1,0:T(8,128)(2,1)S(1)}, u32[]{:S(2)}, u32[]{:S(2)}) collective-permute-start(bf16[7,2,128,128]{3,2,1,0:T(8,128)(2,1)} %get-tuple-element.49), channel_id=1, source_target_pairs={{0,68},{1,69},{2,70},{3,71},{4,64},{5,65},{6,66},{7,67},{8,76},{9,... | collective-permute-start | bytes 1376264 | tf_op jit(solution)/shard_map/ppermute | solution.py:441
  229.9 22.1 %all-to-all-start.1 = ((bf16[16,2,128,128]{3,2,1,0:T(8,128)(2,1)}), bf16[16,2,128,128]{3,2,1,0:T(8,128)(2,1)S(1)}, u32[]{:S(2)}, u32[]{:S(2)}) async-start(bf16[16,2,128,128]{3,2,1,0:T(8,128)(2,1)} %next_sums.1), calls=%async_computation.1 | async-start | bytes 2097152 | tf_op jit(solution)/shard_map/all_to_all | solution.py:387
  (31 other events, 454.9 us)
where the time goes:
time: 255 us
  waiting for transfers between devices  101 us (40%)
  Pallas kernels  70.9 us (28%)
  starting transfers between devices  63 us (25%)
  local copies, waits for them, and re-layouts  10.6 us (4%)
  between operations  6.2 us (2%)
  other arithmetic  3.33 us (1%)
    ppermute x25, waiting for transfers between devices, send(): return lax.ppermute(value, 'snode', shift(**by))  74.4 us
    pallas_call x3, Pallas kernels, columns_of(): pl.pallas_call(lambda *refs: column_body(places, with_own, *refs), out_sh...  46.7 us
    ppermute x25, starting transfers between devices, send(): return lax.ppermute(value, 'snode', shift(**by))  43.7 us
    all_to_all x2, waiting for transfers between devices, in_plane(): lax.all_to_all(value, 'snode', split_axis=0, concat_axis=0, axis_index_gr...  15.1 us
    all_to_all x2, starting transfers between devices, in_plane(): lax.all_to_all(value, 'snode', split_axis=0, concat_axis=0, axis_index_gr...  12.1 us
    pallas_call x3, Pallas kernels, pair_sums(): pl.pallas_call(lambda *refs: pair_body(parts, *refs), out_shape=[jax.Shap...  8.47 us
    pallas_call x4, Pallas kernels, copied(): pl.pallas_call(lambda *refs: copies_body(plan, len(arrays), len(shapes),...  7.27 us
    unnamed x43, local copies, waits for them, and re-layouts  6.41 us
  transfers between devices with their start and end apart: 34, of which 23 were waited for; matrix products, arithmetic and copies ran while one was open for 3% of the time, Pallas kernels for 12%

commit v1 on v0

--- a/solution.py
+++ b/solution.py
@@ -45,6 +45,19 @@
     return lax.ppermute(value, "snode", shift(**by))
 
 
+def ordered(value, *after):
+    return pl.pallas_call(
+        lambda *refs: None,
+        out_shape=jax.ShapeDtypeStruct(value.shape, value.dtype),
+        in_specs=[pl.BlockSpec(memory_space=pl.ANY)] * (1 + len(after)),
+        out_specs=pl.BlockSpec(memory_space=pl.ANY),
+        input_output_aliases={0: 0},
+        compiler_params=pltpu.CompilerParams(vmem_limit_bytes=2**20),
+        cost_estimate=COST,
+        name="ordered",
+    )(value, *after)
+
+
 def copies_body(plan, n_in, n_out, *refs):
     ins, outs = refs[:n_in], refs[n_in : n_in + n_out]
     stages, sems = refs[n_in + n_out : -1], refs[-1]
@@ -109,7 +122,7 @@
         (send(halves[1], dy=1), send(halves[0], dy=-1)),
         (send(halves[3], dx=1), send(halves[2], dx=-1)),
     ]
-    return [left, *found[0], *far[0]], [right, *found[1], *far[1]]
+    return [left, *found[0], *far[0]], [right, *found[1], *far[1]], halves
 
 
 def factor_copies(places, left, right, factors):
@@ -132,7 +145,8 @@
 
 def column_body(places, with_own, meta, root, diag_inv, *refs):
     count = len(places)
-    left, right = refs[:5], refs[5:10]
+    n_side = 3 if places is INNER else 5
+    left, right = refs[:n_side], refs[n_side : 2 * n_side]
     keep, give, blocks, factors, column, total, root_sems, sems = refs[-8:]
 
     def fetch(j, i):
@@ -238,6 +252,8 @@
     count = len(places)
     piece = jax.ShapeDtypeStruct((2, count, 2, PART + 2 * DIAG, B), jnp.bfloat16)
     n_copies = 2 * (len({a for a, _ in places}) + len({b for _, b in places}))
+    n_side = 3 if places is INNER else 5
+    sources = [*left[:n_side], *right[:n_side], *after]
     return pl.pallas_call(
         lambda *refs: column_body(places, with_own, *refs),
         out_shape=[piece] * 2,
@@ -246,7 +262,7 @@
             pl.BlockSpec(memory_space=pl.ANY),
             pl.BlockSpec(memory_space=pltpu.VMEM),
         ]
-        + [pl.BlockSpec(memory_space=pl.ANY)] * (10 + len(after)),
+        + [pl.BlockSpec(memory_space=pl.ANY)] * len(sources),
         out_specs=[pl.BlockSpec(memory_space=pltpu.VMEM)] * 2,
         scratch_shapes=[
             pltpu.VMEM((AHEAD, M, ROWS, 2 * B), jnp.bfloat16),
@@ -263,7 +279,7 @@
             transcendentals=0,
         ),
         name="columns",
-    )(meta, root, diag_inv, *left, *right, *after)
+    )(meta, root, diag_inv, *sources)
 
 
 def weighted(coef, which, mine, other):
@@ -406,7 +422,7 @@
     coef = jnp.concatenate([own_coef, lax.ppermute(own_coef, "pole", CORE)])
     left, right, both = own_rings(factor_columns[0, 0])
     both = send(both, dz=1)
-    left, right = crossed(left, right)
+    left, right, _ = crossed(left, right)
     plan = [(lambda ins, n=n: ins[0].at[n], [lambda outs, n=n: outs[n]]) for n in range(2)]
     next_left, next_right = copied("next_rings", plan, CROSS, [both], [CROSS, CROSS])
 
@@ -426,17 +442,25 @@
         keep, give = columns_of(
             places, dz == 0, left, right, meta, root_inverse, diagonal_inverse[0, 0], after
         )
-        return keep, lax.ppermute(give, "pole", CORE), order.astype(jnp.int32)
-
-    keep, got, order = chunk(0, ALL, left, right, (next_left,))
-    (away,) = pair_sums((1,), coef, keep, got, ())
-    sums = own_sums(coef, order, keep, got, lax.ppermute(away, "pole", Z_HI))
-    own = in_plane(sums)
-    left, right = crossed(next_left, next_right)
-    keep, got, inner = chunk(1, INNER, left, right, (away,))
-    near, away = pair_sums((0, 1), coef, keep, got, ())
-    keep, got, outer = chunk(1, OUTER, left, right, (away,))
-    pairs = [(near, away), pair_sums((0, 1), coef, keep, got, (sums,))]
+        return keep, give, order.astype(jnp.int32)
+
+    def swapped(give, *after):
+        return lax.ppermute(ordered(give, *after), "pole", CORE)
+
+    own_keep, own_give, own_order = chunk(0, ALL, left, right, (next_left,))
+    left, right, halves = crossed(next_left, next_right)
+    own_got = swapped(own_give, halves[0])
+    inner_keep, inner_give, inner = chunk(1, INNER, left, right, ())
+    inner_got = swapped(inner_give, left[3], left[4], right[3], right[4])
+    (own_away,) = pair_sums((1,), coef, own_keep, own_got, ())
+    own_far = lax.ppermute(own_away, "pole", Z_HI)
+    outer_keep, outer_give, outer = chunk(1, OUTER, left, right, (own_away,))
+    outer_got = swapped(outer_give, inner_got)
+    pairs = [
+        pair_sums((0, 1), coef, inner_keep, inner_got, (outer_give,)),
+        pair_sums((0, 1), coef, outer_keep, outer_got, ()),
+    ]
+    own = in_plane(own_sums(coef, own_order, own_keep, own_got, ordered(own_far, pairs[1][1])))
     pairs = [
         (send(near, dz=1), lax.ppermute(away, ("pole", "snode"), across()))
         for near, away in pairs

time: 255 us -> 256 us (level)
  local copies, waits for them, and re-layouts: 10.6 us -> 18.3 us
  waiting for transfers between devices: 101 us -> 95.9 us
    ppermute x25, waiting for transfers between devices: 74.4 us -> 54.2 us  [send(): return lax.ppermute(value, 'snode', shift(**by))]
    ppermute x4, waiting for transfers between devices: 5.48 us -> 20.5 us  [the longest x1 20.5 us: on_device(): own_far = lax.ppermute(own_away, 'pole', Z_HI)]
    unnamed x43 -> x67, local copies, waits for them, and re-layouts: 6.41 us -> 14.1 us
  transfers between devices with their start and end apart: 34 -> 34, of which waited for: 23 -> 15; matrix products, arithmetic and copies ran while one was open for 3% -> 3% of each run, Pallas kernels for 12% -> 22%
where the time goes in v1:
time: 256 us; the launch traced here: 255 us
  waiting for transfers between devices  95.9 us (37%)
  Pallas kernels  70.4 us (28%)
  starting transfers between devices  60.6 us (24%)
  local copies, waits for them, and re-layouts  18.3 us (7%)
  between operations  6.23 us (2%)
  other arithmetic  3.25 us (1%)
    ppermute x25, waiting for transfers between devices, send(): return lax.ppermute(value, 'snode', shift(**by))  54.2 us
    pallas_call x3, Pallas kernels, columns_of(): pl.pallas_call(lambda *refs: column_body(places, with_own, *refs), out_sh...  46 us
    ppermute x25, starting transfers between devices, send(): return lax.ppermute(value, 'snode', shift(**by))  43.1 us
    ppermute x1, waiting for transfers between devices, on_device(): own_far = lax.ppermute(own_away, 'pole', Z_HI)  20.5 us
    all_to_all x2, waiting for transfers between devices, in_plane(): lax.all_to_all(value, 'snode', split_axis=0, concat_axis=0, axis_index_gr...  15.4 us
    unnamed x67, local copies, waits for them, and re-layouts  14.1 us
    all_to_all x2, starting transfers between devices, in_plane(): lax.all_to_all(value, 'snode', split_axis=0, concat_axis=0, axis_index_gr...  10.5 us
    pallas_call x3, Pallas kernels, pair_sums(): pl.pallas_call(lambda *refs: pair_body(parts, *refs), out_shape=[jax.Shap...  9.38 us
  transfers between devices with their start and end apart: 34, of which 15 were waited for; matrix products, arithmetic and copies ran while one was open for 3% of the time, Pallas kernels for 22%

profile of v1, /device:TPU:0, one launch (start us, length us, event | category | flops | bytes accessed | tf_op | source)
XLA Modules:
  0.0 254.8 jit_solution(14469247192078720761)
XLA Ops:
  1.8 3.4 %collective-permute-start.6 = (bf16[2,2,256,128]{3,2,1,0:T(8,128)(2,1)S(1)}, bf16[2,2,256,128]{3,2,1,0:T(8,128)(2,1)S(1)}, u32[]{:S(2)}, u32[]{:S(2)}) collective-permute-start(bf16[2,2,256,128]{3,2,1,0:T(8,128)(2,1)S(1)} %get-tuple-element.56.refs_4_), channel_id=1, source_target_pairs={{0,2},{1,3},{2,0},{3,1},{4,6},{5,7},{6,4},{7,5},{8,10},{9,11},{10,... | collective-permute-start | bytes 786440 | tf_op jit(solution)/shard_map/ppermute | solution.py:45
  8.3 3.0 %collective-permute-start.3 = (bf16[2,2,256,128]{3,2,1,0:T(8,128)(2,1)S(1)}, bf16[2,2,256,128]{3,2,1,0:T(8,128)(2,1)S(1)}, u32[]{:S(2)}, u32[]{:S(2)}) collective-permute-start(bf16[2,2,256,128]{3,2,1,0:T(8,128)(2,1)S(1)} %get-tuple-element.57.refs_0_), channel_id=1, source_target_pairs={{0,16},{1,17},{2,18},{3,19},{4,20},{5,21},{6,22},{7,23},{8,24},{9,... | collective-permute-start | bytes 786440 | tf_op jit(solution)/shard_map/ppermute | solution.py:45
  12.6 2.8 %collective-permute-start.1 = (bf16[2,2,256,128]{3,2,1,0:T(8,128)(2,1)S(1)}, bf16[2,2,256,128]{3,2,1,0:T(8,128)(2,1)S(1)}, u32[]{:S(2)}, u32[]{:S(2)}) collective-permute-start(bf16[2,2,256,128]{3,2,1,0:T(8,128)(2,1)S(1)} %get-tuple-element.57.refs_0_), channel_id=1, source_target_pairs={{0,24},{1,25},{2,26},{3,27},{4,28},{5,29},{6,30},{7,31},{8,0},{9,1... | collective-permute-start | bytes 786440 | tf_op jit(solution)/shard_map/ppermute | solution.py:45
  19.1 3.6 %collective-permute-done.2.refs_2_ = bf16[2,2,256,128]{3,2,1,0:T(8,128)(2,1)S(1)} collective-permute-done((bf16[2,2,256,128]{3,2,1,0:T(8,128)(2,1)S(1)}, bf16[2,2,256,128]{3,2,1,0:T(8,128)(2,1)S(1)}, u32[]{:S(2)}, u32[]{:S(2)}) %collective-permute-start.2) | collective-permute-done | bytes 262176 | tf_op jit(solution)/shard_map/ppermute | solution.py:45
  26.5 3.2 %collective-permute-start.7 = (bf16[2,4,2,256,128]{4,3,2,1,0:T(8,128)(2,1)S(1)}, bf16[2,4,2,256,128]{4,3,2,1,0:T(8,128)(2,1)S(1)}, u32[]{:S(2)}, u32[]{:S(2)}) collective-permute-start(bf16[2,4,2,256,128]{4,3,2,1,0:T(8,128)(2,1)S(1)} %get-tuple-element.27.refs_3_), channel_id=1, source_target_pairs={{0,3},{1,0},{2,1},{3,2},{4,7},{5,4},{6,5},{7,6},{8,11},{9,8},{10,9... | collective-permute-start | bytes 3145736 | tf_op jit(solution)/shard_map/ppermute | solution.py:45
  32.9 18.9 %collective-permute-done.8.refs_1_.refs_5_ = bf16[2,4,2,256,128]{4,3,2,1,0:T(8,128)(2,1)S(1)} collective-permute-done((bf16[2,4,2,256,128]{4,3,2,1,0:T(8,128)(2,1)S(1)}, bf16[2,4,2,256,128]{4,3,2,1,0:T(8,128)(2,1)S(1)}, u32[]{:S(2)}, u32[]{:S(2)}) %collective-permute-start.8) | collective-permute-done | bytes 1048608 | tf_op jit(solution)/shard_map/ppermute | solution.py:45
  56.6 3.2 %collective-permute-start.12 = (bf16[4,2,256,128]{3,2,1,0:T(8,128)(2,1)}, bf16[4,2,256,128]{3,2,1,0:T(8,128)(2,1)}, u32[]{:S(2)}, u32[]{:S(2)}) collective-permute-start(bf16[4,2,256,128]{3,2,1,0:T(8,128)(2,1)} %get-tuple-element.30), channel_id=1, source_target_pairs={{0,3},{1,0},{2,1},{3,2},{4,7},{5,4},{6,5},{7,6},{8,11},{9,8},{10,9... | collective-permute-start | bytes 1572872 | tf_op jit(solution)/shard_map/ppermute | solution.py:45
  60.1 3.0 %collective-permute-start.14 = (bf16[4,2,256,128]{3,2,1,0:T(8,128)(2,1)}, bf16[4,2,256,128]{3,2,1,0:T(8,128)(2,1)}, u32[]{:S(2)}, u32[]{:S(2)}) collective-permute-start(bf16[4,2,256,128]{3,2,1,0:T(8,128)(2,1)} %get-tuple-element.32), channel_id=1, source_target_pairs={{0,24},{1,25},{2,26},{3,27},{4,28},{5,29},{6,30},{7,31},{8,0},{9,1... | collective-permute-start | bytes 1572872 | tf_op jit(solution)/shard_map/ppermute | solution.py:45
  63.2 8.6 %collective-permute-done.15.refs_0_ = bf16[2,2,4,2,256,128]{5,4,3,2,1,0:T(8,128)(2,1)S(1)} collective-permute-done((bf16[2,2,4,2,256,128]{5,4,3,2,1,0:T(8,128)(2,1)}, bf16[2,2,4,2,256,128]{5,4,3,2,1,0:T(8,128)(2,1)S(1)}, u32[]{:S(2)}, u32[]{:S(2)}) %collective-permute-start.15) | collective-permute-done | bytes 2097184 | tf_op jit(solution)/shard_map/ppermute | solution.py:45
  76.4 3.2 %collective-permute-start.16 = (bf16[2,4,2,256,128]{4,3,2,1,0:T(8,128)(2,1)S(1)}, bf16[2,4,2,256,128]{4,3,2,1,0:T(8,128)(2,1)}, u32[]{:S(2)}, u32[]{:S(2)}) collective-permute-start(bf16[2,4,2,256,128]{4,3,2,1,0:T(8,128)(2,1)S(1)} %get-tuple-element.34.refs_13_.refs_3_), channel_id=1, source_target_pairs={{0,3},{1,0},{2,1},{3,2},{4,7},{5,4},{6,5},{7,6},{8,11},{9,8},{10,9... | collective-permute-start | bytes 3145736 | tf_op jit(solution)/shard_map/ppermute | solution.py:45
  81.0 21.1 %columns.3 = (bf16[2,16,2,160,128]{4,3,2,1,0:T(8,128)(2,1)}, bf16[2,16,2,160,128]{4,3,2,1,0:T(8,128)(2,1)}) custom-call(s32[162]{0:T(256)} %pad_add_fusion.refs_0_, bf16[1,2,96,384,128]{4,3,2,1,0:T(8,128)(2,1)} %refs_1_.5, bf16[2,128,128]{2,1,0:T(8,128)(2,1)} %bitcast.80, bf16[2,4,2,256,128]{4,3,2,1,0:T(8,128)(2,1)} %copy-done.20, ...), custom_call_target="tpu_custom_call" | custom-call | flops 6442450944 | bytes 33554432 | tf_op jit(solution)/shard_map/columns/pallas_call | solution.py:257
  112.1 13.4 %columns.5 = (bf16[2,9,2,160,128]{4,3,2,1,0:T(8,128)(2,1)}, bf16[2,9,2,160,128]{4,3,2,1,0:T(8,128)(2,1)}) custom-call(s32[92]{0:T(128)} %pad_add_fusion.3.refs_0_, bf16[1,2,96,384,128]{4,3,2,1,0:T(8,128)(2,1)} %refs_1_.5, bf16[2,128,128]{2,1,0:T(8,128)(2,1)} %bitcast.81, bf16[2,4,2,256,128]{4,3,2,1,0:T(8,128)(2,1)} %copy-done.1, ...), custom_call_target="tpu_custom_call" | custom-call | flops 3623878656 | bytes 18874368 | tf_op jit(solution)/shard_map/columns/pallas_call | solution.py:257
  142.8 3.9 %pair_sums.3.refs_13_ = bf16[16,2,128,128]{3,2,1,0:T(8,128)(2,1)} custom-call(f32[2,4]{1,0:T(2,128)S(1)} %pad_maximum_fusion.refs_0_.coef, bf16[2,16,2,160,128]{4,3,2,1,0:T(8,128)(2,1)S(1)} %copy-done, bf16[2,16,2,160,128]{4,3,2,1,0:T(8,128)(2,1)} %collective-permute-done.20.refs_2_.other), custom_call_target="tpu_custom_call" | custom-call | bytes 1 | tf_op jit(solution)/shard_map/pair_sums/pallas_call | solution.py:311
  146.7 11.5 %columns.4 = (bf16[2,7,2,160,128]{4,3,2,1,0:T(8,128)(2,1)}, bf16[2,7,2,160,128]{4,3,2,1,0:T(8,128)(2,1)}) custom-call(s32[72]{0:T(128)} %pad_add_fusion.2.refs_0_, bf16[1,2,96,384,128]{4,3,2,1,0:T(8,128)(2,1)} %refs_1_.5, bf16[2,128,128]{2,1,0:T(8,128)(2,1)} %bitcast.82, bf16[2,4,2,256,128]{4,3,2,1,0:T(8,128)(2,1)} %copy-done.1, ...), custom_call_target="tpu_custom_call" | custom-call | flops 2818572288 | bytes 14680064 | tf_op jit(solution)/shard_map/columns/pallas_call | solution.py:257
  159.6 3.3 %pair_sums.5 = (bf16[9,2,128,128]{3,2,1,0:T(8,128)(2,1)}, bf16[9,2,128,128]{3,2,1,0:T(8,128)(2,1)S(1)}) custom-call(f32[2,4]{1,0:T(2,128)S(1)} %pad_maximum_fusion.refs_0_.coef, bf16[2,9,2,160,128]{4,3,2,1,0:T(8,128)(2,1)S(1)} %copy-done.16, bf16[2,9,2,160,128]{4,3,2,1,0:T(8,128)(2,1)} %collective-permute-done.26.refs_1_.refs_2_, ...), custom_call_target="tpu_custom_call" | custom-call | bytes 1 | tf_op jit(solution)/shard_map/pair_sums/pallas_call | solution.py:311
  163.7 3.7 %collective-permute-start.21 = (bf16[16,2,128,128]{3,2,1,0:T(8,128)(2,1)}, bf16[16,2,128,128]{3,2,1,0:T(8,128)(2,1)}, u32[]{:S(2)}, u32[]{:S(2)}) collective-permute-start(bf16[16,2,128,128]{3,2,1,0:T(8,128)(2,1)} %pair_sums.3.refs_13_), channel_id=1, source_target_pairs={{0,64},{32,96},{64,0},{96,32},{1,65},{33,97},{65,1},{97,33},{2,66}... | collective-permute-start | bytes 3145736 | tf_op jit(solution)/shard_map/ppermute | solution.py:456
  171.0 20.5 %collective-permute-done.21.refs_0_ = bf16[16,2,128,128]{3,2,1,0:T(8,128)(2,1)} collective-permute-done((bf16[16,2,128,128]{3,2,1,0:T(8,128)(2,1)}, bf16[16,2,128,128]{3,2,1,0:T(8,128)(2,1)}, u32[]{:S(2)}, u32[]{:S(2)}) %collective-permute-start.21) | collective-permute-done | bytes 1048608 | tf_op jit(solution)/shard_map/ppermute | solution.py:456
  191.6 3.3 %own_sums.1 = bf16[16,2,128,128]{3,2,1,0:T(8,128)(2,1)S(1)} custom-call(f32[2,4]{1,0:T(2,128)S(1)} %pad_maximum_fusion.refs_0_.coef, s32[16]{0:T(128)S(1)} %stack.222.order, bf16[2,16,2,160,128]{4,3,2,1,0:T(8,128)(2,1)S(1)} %copy-done, bf16[2,16,2,160,128]{4,3,2,1,0:T(8,128)(2,1)} %collective-permute-done.20.refs_2_.other, bf16[16,2,128,128]{3,2,1,0:T(8,128)(2,1)} %ordered.7.far), custom_call_target="tpu_custom_call" | custom-call | bytes 1 | tf_op jit(solution)/shard_map/own_sums/pallas_call | solution.py:337
  195.8 3.7 %all-to-all-start = ((bf16[16,2,128,128]{3,2,1,0:T(8,128)(2,1)}), bf16[16,2,128,128]{3,2,1,0:T(8,128)(2,1)S(1)}, u32[]{:S(2)}, u32[]{:S(2)}) async-start(bf16[16,2,128,128]{3,2,1,0:T(8,128)(2,1)} %copy-done.8), calls=%async_computation | async-start | bytes 2097152 | tf_op jit(solution)/shard_map/all_to_all | solution.py:403
  205.6 10.3 %collective-permute-done.28.refs_0_ = bf16[9,2,128,128]{3,2,1,0:T(8,128)(2,1)S(1)} collective-permute-done((bf16[9,2,128,128]{3,2,1,0:T(8,128)(2,1)}, bf16[9,2,128,128]{3,2,1,0:T(8,128)(2,1)S(1)}, u32[]{:S(2)}, u32[]{:S(2)}) %collective-permute-start.28) | collective-permute-done | bytes 589856 | tf_op jit(solution)/shard_map/ppermute | solution.py:45
  216.0 3.1 %collective-permute-done.29.refs_1_ = bf16[9,2,128,128]{3,2,1,0:T(8,128)(2,1)S(1)} collective-permute-done((bf16[9,2,128,128]{3,2,1,0:T(8,128)(2,1)}, bf16[9,2,128,128]{3,2,1,0:T(8,128)(2,1)S(1)}, u32[]{:S(2)}, u32[]{:S(2)}) %collective-permute-start.29) | collective-permute-done | bytes 589856 | tf_op jit(solution)/shard_map/ppermute | solution.py:465
  219.1 5.6 %collective-permute-done.30.refs_2_ = bf16[7,2,128,128]{3,2,1,0:T(8,128)(2,1)S(1)} collective-permute-done((bf16[7,2,128,128]{3,2,1,0:T(8,128)(2,1)}, bf16[7,2,128,128]{3,2,1,0:T(8,128)(2,1)S(1)}, u32[]{:S(2)}, u32[]{:S(2)}) %collective-permute-start.30) | collective-permute-done | bytes 458784 | tf_op jit(solution)/shard_map/ppermute | solution.py:45
  229.7 6.8 %all-to-all-start.1 = ((bf16[16,2,128,128]{3,2,1,0:T(8,128)(2,1)}), bf16[16,2,128,128]{3,2,1,0:T(8,128)(2,1)S(1)}, u32[]{:S(2)}, u32[]{:S(2)}) async-start(bf16[16,2,128,128]{3,2,1,0:T(8,128)(2,1)} %next_sums.1), calls=%async_computation.1 | async-start | bytes 2097152 | tf_op jit(solution)/shard_map/all_to_all | solution.py:403
  236.6 15.4 %all-to-all-done.1.other = bf16[16,2,128,128]{3,2,1,0:T(8,128)(2,1)S(1)} async-done(((bf16[16,2,128,128]{3,2,1,0:T(8,128)(2,1)}), bf16[16,2,128,128]{3,2,1,0:T(8,128)(2,1)S(1)}, u32[]{:S(2)}, u32[]{:S(2)}) %all-to-all-start.1) | async-done | bytes 1048608 | tf_op jit(solution)/shard_map/all_to_all | solution.py:403
  (154 shorter events, 69.9 us)
Async XLA Ops:
  24.5 47.4 %collective-permute-start.15 = (bf16[2,2,4,2,256,128]{5,4,3,2,1,0:T(8,128)(2,1)}, bf16[2,2,4,2,256,128]{5,4,3,2,1,0:T(8,128)(2,1)S(1)}, u32[]{:S(2)}, u32[]{:S(2)}) collective-permute-start(bf16[2,2,4,2,256,128]{5,4,3,2,1,0:T(8,128)(2,1)} %get-tuple-element.33), channel_id=1, source_target_pairs={{0,4},{1,5},{2,6},{3,7},{4,0},{5,1},{6,2},{7,3},{8,12},{9,13},{10,... | collective-permute-start | bytes 6291464 | tf_op jit(solution)/shard_map/ppermute | solution.py:45
  26.5 25.4 %collective-permute-start.8 = (bf16[2,4,2,256,128]{4,3,2,1,0:T(8,128)(2,1)S(1)}, bf16[2,4,2,256,128]{4,3,2,1,0:T(8,128)(2,1)S(1)}, u32[]{:S(2)}, u32[]{:S(2)}) collective-permute-start(bf16[2,4,2,256,128]{4,3,2,1,0:T(8,128)(2,1)S(1)} %get-tuple-element.27.refs_3_), channel_id=1, source_target_pairs={{0,1},{1,2},{2,3},{3,0},{4,5},{5,6},{6,7},{7,4},{8,9},{9,10},{10,1... | collective-permute-start | bytes 3145736 | tf_op jit(solution)/shard_map/ppermute | solution.py:45
  26.5 25.4 %collective-permute-start.7 = (bf16[2,4,2,256,128]{4,3,2,1,0:T(8,128)(2,1)S(1)}, bf16[2,4,2,256,128]{4,3,2,1,0:T(8,128)(2,1)S(1)}, u32[]{:S(2)}, u32[]{:S(2)}) collective-permute-start(bf16[2,4,2,256,128]{4,3,2,1,0:T(8,128)(2,1)S(1)} %get-tuple-element.27.refs_3_), channel_id=1, source_target_pairs={{0,3},{1,0},{2,1},{3,2},{4,7},{5,4},{6,5},{7,6},{8,11},{9,8},{10,9... | collective-permute-start | bytes 3145736 | tf_op jit(solution)/shard_map/ppermute | solution.py:45
  29.7 24.8 %collective-permute-start.10 = (bf16[2,4,2,256,128]{4,3,2,1,0:T(8,128)(2,1)S(1)}, bf16[2,4,2,256,128]{4,3,2,1,0:T(8,128)(2,1)S(1)}, u32[]{:S(2)}, u32[]{:S(2)}) collective-permute-start(bf16[2,4,2,256,128]{4,3,2,1,0:T(8,128)(2,1)S(1)} %get-tuple-element.28.refs_8_), channel_id=1, source_target_pairs={{0,8},{1,9},{2,10},{3,11},{4,12},{5,13},{6,14},{7,15},{8,16},{9,17... | collective-permute-start | bytes 3145736 | tf_op jit(solution)/shard_map/ppermute | solution.py:45
  31.2 23.4 %collective-permute-start.9 = (bf16[2,4,2,256,128]{4,3,2,1,0:T(8,128)(2,1)S(1)}, bf16[2,4,2,256,128]{4,3,2,1,0:T(8,128)(2,1)S(1)}, u32[]{:S(2)}, u32[]{:S(2)}) collective-permute-start(bf16[2,4,2,256,128]{4,3,2,1,0:T(8,128)(2,1)S(1)} %get-tuple-element.28.refs_8_), channel_id=1, source_target_pairs={{0,24},{1,25},{2,26},{3,27},{4,28},{5,29},{6,30},{7,31},{8,0},{9,1... | collective-permute-start | bytes 3145736 | tf_op jit(solution)/shard_map/ppermute | solution.py:45
  56.6 18.1 %collective-permute-start.11 = (bf16[4,2,256,128]{3,2,1,0:T(8,128)(2,1)}, bf16[4,2,256,128]{3,2,1,0:T(8,128)(2,1)}, u32[]{:S(2)}, u32[]{:S(2)}) collective-permute-start(bf16[4,2,256,128]{3,2,1,0:T(8,128)(2,1)} %get-tuple-element.29), channel_id=1, source_target_pairs={{0,1},{1,2},{2,3},{3,0},{4,5},{5,6},{6,7},{7,4},{8,9},{9,10},{10,1... | collective-permute-start | bytes 1572872 | tf_op jit(solution)/shard_map/ppermute | solution.py:45
  56.6 19.9 %collective-permute-start.12 = (bf16[4,2,256,128]{3,2,1,0:T(8,128)(2,1)}, bf16[4,2,256,128]{3,2,1,0:T(8,128)(2,1)}, u32[]{:S(2)}, u32[]{:S(2)}) collective-permute-start(bf16[4,2,256,128]{3,2,1,0:T(8,128)(2,1)} %get-tuple-element.30), channel_id=1, source_target_pairs={{0,3},{1,0},{2,1},{3,2},{4,7},{5,4},{6,5},{7,6},{8,11},{9,8},{10,9... | collective-permute-start | bytes 1572872 | tf_op jit(solution)/shard_map/ppermute | solution.py:45
  60.1 20.9 %collective-permute-start.14 = (bf16[4,2,256,128]{3,2,1,0:T(8,128)(2,1)}, bf16[4,2,256,128]{3,2,1,0:T(8,128)(2,1)}, u32[]{:S(2)}, u32[]{:S(2)}) collective-permute-start(bf16[4,2,256,128]{3,2,1,0:T(8,128)(2,1)} %get-tuple-element.32), channel_id=1, source_target_pairs={{0,24},{1,25},{2,26},{3,27},{4,28},{5,29},{6,30},{7,31},{8,0},{9,1... | collective-permute-start | bytes 1572872 | tf_op jit(solution)/shard_map/ppermute | solution.py:45
  73.1 29.0 %collective-permute-start.19 = (bf16[2,4,2,256,128]{4,3,2,1,0:T(8,128)(2,1)}, bf16[2,4,2,256,128]{4,3,2,1,0:T(8,128)(2,1)S(1)}, u32[]{:S(2)}, u32[]{:S(2)}) collective-permute-start(bf16[2,4,2,256,128]{4,3,2,1,0:T(8,128)(2,1)} %get-tuple-element.37.refs_8_.refs_6_), channel_id=1, source_target_pairs={{0,8},{1,9},{2,10},{3,11},{4,12},{5,13},{6,14},{7,15},{8,16},{9,17... | collective-permute-start | bytes 3145736 | tf_op jit(solution)/shard_map/ppermute | solution.py:45
  74.6 27.5 %collective-permute-start.18 = (bf16[2,4,2,256,128]{4,3,2,1,0:T(8,128)(2,1)}, bf16[2,4,2,256,128]{4,3,2,1,0:T(8,128)(2,1)S(1)}, u32[]{:S(2)}, u32[]{:S(2)}) collective-permute-start(bf16[2,4,2,256,128]{4,3,2,1,0:T(8,128)(2,1)} %get-tuple-element.37.refs_8_.refs_6_), channel_id=1, source_target_pairs={{0,24},{1,25},{2,26},{3,27},{4,28},{5,29},{6,30},{7,31},{8,0},{9,1... | collective-permute-start | bytes 3145736 | tf_op jit(solution)/shard_map/ppermute | solution.py:45
  76.4 25.7 %collective-permute-start.17 = (bf16[2,4,2,256,128]{4,3,2,1,0:T(8,128)(2,1)S(1)}, bf16[2,4,2,256,128]{4,3,2,1,0:T(8,128)(2,1)}, u32[]{:S(2)}, u32[]{:S(2)}) collective-permute-start(bf16[2,4,2,256,128]{4,3,2,1,0:T(8,128)(2,1)S(1)} %get-tuple-element.34.refs_13_.refs_3_), channel_id=1, source_target_pairs={{0,1},{1,2},{2,3},{3,0},{4,5},{5,6},{6,7},{7,4},{8,9},{9,10},{10,1... | collective-permute-start | bytes 3145736 | tf_op jit(solution)/shard_map/ppermute | solution.py:45
  76.4 25.7 %collective-permute-start.16 = (bf16[2,4,2,256,128]{4,3,2,1,0:T(8,128)(2,1)S(1)}, bf16[2,4,2,256,128]{4,3,2,1,0:T(8,128)(2,1)}, u32[]{:S(2)}, u32[]{:S(2)}) collective-permute-start(bf16[2,4,2,256,128]{4,3,2,1,0:T(8,128)(2,1)S(1)} %get-tuple-element.34.refs_13_.refs_3_), channel_id=1, source_target_pairs={{0,3},{1,0},{2,1},{3,2},{4,7},{5,4},{6,5},{7,6},{8,11},{9,8},{10,9... | collective-permute-start | bytes 3145736 | tf_op jit(solution)/shard_map/ppermute | solution.py:45
  105.5 37.3 %collective-permute-start.20 = (bf16[2,16,2,160,128]{4,3,2,1,0:T(8,128)(2,1)}, bf16[2,16,2,160,128]{4,3,2,1,0:T(8,128)(2,1)}, u32[]{:S(2)}, u32[]{:S(2)}) collective-permute-start(bf16[2,16,2,160,128]{4,3,2,1,0:T(8,128)(2,1)} %ordered.4), channel_id=1, source_target_pairs={{0,32},{32,0},{64,96},{96,64},{1,33},{33,1},{65,97},{97,65},{2,34}... | collective-permute-start | bytes 7864328 | tf_op jit(solution)/shard_map/ppermute | solution.py:448
  105.6 22.3 %collective-permute-start.23 = (bf16[4,2,256,128]{3,2,1,0:T(8,128)(2,1)S(1)}, bf16[4,2,256,128]{3,2,1,0:T(8,128)(2,1)S(1)}, u32[]{:S(2)}, u32[]{:S(2)}) collective-permute-start(bf16[4,2,256,128]{3,2,1,0:T(8,128)(2,1)S(1)} %get-tuple-element.38.refs_1_), channel_id=1, source_target_pairs={{0,3},{1,0},{2,1},{3,2},{4,7},{5,4},{6,5},{7,6},{8,11},{9,8},{10,9... | collective-permute-start | bytes 1572872 | tf_op jit(solution)/shard_map/ppermute | solution.py:45
  106.7 18.8 %collective-permute-start.22 = (bf16[4,2,256,128]{3,2,1,0:T(8,128)(2,1)}, bf16[4,2,256,128]{3,2,1,0:T(8,128)(2,1)S(1)}, u32[]{:S(2)}, u32[]{:S(2)}) collective-permute-start(bf16[4,2,256,128]{3,2,1,0:T(8,128)(2,1)} %copy-done.25), channel_id=1, source_target_pairs={{0,1},{1,2},{2,3},{3,0},{4,5},{5,6},{6,7},{7,4},{8,9},{9,10},{10,1... | collective-permute-start | bytes 1572872 | tf_op jit(solution)/shard_map/ppermute | solution.py:45
  107.7 18.7 %collective-permute-start.24 = (bf16[4,2,256,128]{3,2,1,0:T(8,128)(2,1)}, bf16[4,2,256,128]{3,2,1,0:T(8,128)(2,1)S(1)}, u32[]{:S(2)}, u32[]{:S(2)}) collective-permute-start(bf16[4,2,256,128]{3,2,1,0:T(8,128)(2,1)} %copy-done.24), channel_id=1, source_target_pairs={{0,8},{1,9},{2,10},{3,11},{4,12},{5,13},{6,14},{7,15},{8,16},{9,17... | collective-permute-start | bytes 1572872 | tf_op jit(solution)/shard_map/ppermute | solution.py:45
  109.1 18.0 %collective-permute-start.25 = (bf16[4,2,256,128]{3,2,1,0:T(8,128)(2,1)}, bf16[4,2,256,128]{3,2,1,0:T(8,128)(2,1)S(1)}, u32[]{:S(2)}, u32[]{:S(2)}) collective-permute-start(bf16[4,2,256,128]{3,2,1,0:T(8,128)(2,1)} %copy-done.23), channel_id=1, source_target_pairs={{0,24},{1,25},{2,26},{3,27},{4,28},{5,29},{6,30},{7,31},{8,0},{9,1... | collective-permute-start | bytes 1572872 | tf_op jit(solution)/shard_map/ppermute | solution.py:45
  133.8 24.4 %collective-permute-start.26 = (bf16[2,9,2,160,128]{4,3,2,1,0:T(8,128)(2,1)}, bf16[2,9,2,160,128]{4,3,2,1,0:T(8,128)(2,1)}, u32[]{:S(2)}, u32[]{:S(2)}) collective-permute-start(bf16[2,9,2,160,128]{4,3,2,1,0:T(8,128)(2,1)} %copy-done.18), channel_id=1, source_target_pairs={{0,32},{32,0},{64,96},{96,64},{1,33},{33,1},{65,97},{97,65},{2,34}... | collective-permute-start | bytes 4423688 | tf_op jit(solution)/shard_map/ppermute | solution.py:448
  163.7 27.8 %collective-permute-start.21 = (bf16[16,2,128,128]{3,2,1,0:T(8,128)(2,1)}, bf16[16,2,128,128]{3,2,1,0:T(8,128)(2,1)}, u32[]{:S(2)}, u32[]{:S(2)}) collective-permute-start(bf16[16,2,128,128]{3,2,1,0:T(8,128)(2,1)} %pair_sums.3.refs_13_), channel_id=1, source_target_pairs={{0,64},{32,96},{64,0},{96,32},{1,65},{33,97},{65,1},{97,33},{2,66}... | collective-permute-start | bytes 3145736 | tf_op jit(solution)/shard_map/ppermute | solution.py:456
  195.8 33.9 %all-to-all-start = ((bf16[16,2,128,128]{3,2,1,0:T(8,128)(2,1)}), bf16[16,2,128,128]{3,2,1,0:T(8,128)(2,1)S(1)}, u32[]{:S(2)}, u32[]{:S(2)}) async-start(bf16[16,2,128,128]{3,2,1,0:T(8,128)(2,1)} %copy-done.8), calls=%async_computation | async-start | bytes 2097152 | tf_op jit(solution)/shard_map/all_to_all | solution.py:403
  201.4 17.7 %collective-permute-start.29 = (bf16[9,2,128,128]{3,2,1,0:T(8,128)(2,1)}, bf16[9,2,128,128]{3,2,1,0:T(8,128)(2,1)S(1)}, u32[]{:S(2)}, u32[]{:S(2)}) collective-permute-start(bf16[9,2,128,128]{3,2,1,0:T(8,128)(2,1)} %copy-done.22), channel_id=1, source_target_pairs={{0,68},{1,69},{2,70},{3,71},{4,64},{5,65},{6,66},{7,67},{8,76},{9,... | collective-permute-start | bytes 1769480 | tf_op jit(solution)/shard_map/ppermute | solution.py:465
  203.6 21.1 %collective-permute-start.30 = (bf16[7,2,128,128]{3,2,1,0:T(8,128)(2,1)}, bf16[7,2,128,128]{3,2,1,0:T(8,128)(2,1)S(1)}, u32[]{:S(2)}, u32[]{:S(2)}) collective-permute-start(bf16[7,2,128,128]{3,2,1,0:T(8,128)(2,1)} %copy-done.26), channel_id=1, source_target_pairs={{0,4},{1,5},{2,6},{3,7},{4,0},{5,1},{6,2},{7,3},{8,12},{9,13},{10,... | collective-permute-start | bytes 1376264 | tf_op jit(solution)/shard_map/ppermute | solution.py:45
  204.9 22.4 %collective-permute-start.31 = (bf16[7,2,128,128]{3,2,1,0:T(8,128)(2,1)S(1)}, bf16[7,2,128,128]{3,2,1,0:T(8,128)(2,1)}, u32[]{:S(2)}, u32[]{:S(2)}) collective-permute-start(bf16[7,2,128,128]{3,2,1,0:T(8,128)(2,1)S(1)} %get-tuple-element.45.refs_1_), channel_id=1, source_target_pairs={{0,68},{1,69},{2,70},{3,71},{4,64},{5,65},{6,66},{7,67},{8,76},{9,... | collective-permute-start | bytes 1376264 | tf_op jit(solution)/shard_map/ppermute | solution.py:465
  229.7 22.3 %all-to-all-start.1 = ((bf16[16,2,128,128]{3,2,1,0:T(8,128)(2,1)}), bf16[16,2,128,128]{3,2,1,0:T(8,128)(2,1)S(1)}, u32[]{:S(2)}, u32[]{:S(2)}) async-start(bf16[16,2,128,128]{3,2,1,0:T(8,128)(2,1)} %next_sums.1), calls=%async_computation.1 | async-start | bytes 2097152 | tf_op jit(solution)/shard_map/all_to_all | solution.py:403
  (43 other events, 322.0 us)

commit v2 on v1

--- a/solution.py
+++ b/solution.py
@@ -450,22 +450,24 @@
     own_keep, own_give, own_order = chunk(0, ALL, left, right, (next_left,))
     left, right, halves = crossed(next_left, next_right)
     own_got = swapped(own_give, halves[0])
-    inner_keep, inner_give, inner = chunk(1, INNER, left, right, ())
-    inner_got = swapped(inner_give, left[3], left[4], right[3], right[4])
     (own_away,) = pair_sums((1,), coef, own_keep, own_got, ())
     own_far = lax.ppermute(own_away, "pole", Z_HI)
-    outer_keep, outer_give, outer = chunk(1, OUTER, left, right, (own_away,))
-    outer_got = swapped(outer_give, inner_got)
+    inner_keep, inner_give, inner = chunk(1, INNER, left, right, (own_away,))
+    outer_keep, outer_give, outer = chunk(1, OUTER, left, right, (inner_give,))
+    inner_got = swapped(inner_give, own_far, outer_give)
+    outer_got = swapped(outer_give, own_far)
+    sums = own_sums(coef, own_order, own_keep, own_got, own_far)
+    own = in_plane(sums)
     pairs = [
-        pair_sums((0, 1), coef, inner_keep, inner_got, (outer_give,)),
+        pair_sums((0, 1), coef, inner_keep, inner_got, (sums,)),
         pair_sums((0, 1), coef, outer_keep, outer_got, ()),
     ]
-    own = in_plane(own_sums(coef, own_order, own_keep, own_got, ordered(own_far, pairs[1][1])))
-    pairs = [
+    (near, away), outer_pair = [
         (send(near, dz=1), lax.ppermute(away, ("pole", "snode"), across()))
         for near, away in pairs
     ]
-    other = in_plane(next_sums(jnp.concatenate([inner, outer]), pairs))
+    inner_pair = (ordered(near, own), away)
+    other = in_plane(next_sums(jnp.concatenate([inner, outer]), [inner_pair, outer_pair]))
     rows_out, diag_out = placed(jnp.stack([z, 1 - z]).astype(jnp.int32), own, other)
     return rows_out[:, None], diag_out[:, None]
 

time: 256 us -> 227 us (0.89)
  waiting for transfers between devices: 95.9 us -> 73.4 us
  local copies, waits for them, and re-layouts: 18.3 us -> 11.4 us
    ppermute x1, waiting for transfers between devices: 20.5 us -> 0.01 us  [on_device(): own_far = lax.ppermute(own_away, 'pole', Z_HI)]
    unnamed x67 -> x57, local copies, waits for them, and re-layouts: 14.1 us -> 7.22 us
    all_to_all x2, waiting for transfers between devices: 15.4 us -> 21.3 us  [in_plane(): lax.all_to_all(value, 'snode', split_axis=0, concat_axis=0, axis_index_gr...]
    ppermute x2, waiting for transfers between devices: 5.75 us -> 1.22 us  [on_device(): lax.ppermute(away, ('pole', 'snode'), across())]
    ppermute x25, waiting for transfers between devices: 54.2 us -> 50.2 us  [send(): return lax.ppermute(value, 'snode', shift(**by))]
  transfers between devices with their start and end apart: 34 -> 34, of which waited for: 15 -> 15; matrix products, arithmetic and copies ran while one was open for 3% -> 3% of each run, Pallas kernels for 22% -> 26%
where the time goes in v2:
time: 227 us; the launch traced here: 226 us
  waiting for transfers between devices  73.4 us (32%)
  Pallas kernels  71.5 us (31%)
  starting transfers between devices  59.9 us (26%)
  local copies, waits for them, and re-layouts  11.4 us (5%)
  between operations  6.29 us (3%)
  other arithmetic  3.41 us (2%)
    ppermute x25, waiting for transfers between devices, send(): return lax.ppermute(value, 'snode', shift(**by))  50.2 us
    pallas_call x3, Pallas kernels, columns_of(): pl.pallas_call(lambda *refs: column_body(places, with_own, *refs), out_sh...  46.3 us
    ppermute x25, starting transfers between devices, send(): return lax.ppermute(value, 'snode', shift(**by))  41.4 us
    all_to_all x2, waiting for transfers between devices, in_plane(): lax.all_to_all(value, 'snode', split_axis=0, concat_axis=0, axis_index_gr...  21.3 us
    all_to_all x2, starting transfers between devices, in_plane(): lax.all_to_all(value, 'snode', split_axis=0, concat_axis=0, axis_index_gr...  10.6 us
    pallas_call x3, Pallas kernels, pair_sums(): pl.pallas_call(lambda *refs: pair_body(parts, *refs), out_shape=[jax.Shap...  10.6 us
    unnamed x57, local copies, waits for them, and re-layouts  7.22 us
    pallas_call x4, Pallas kernels, copied(): pl.pallas_call(lambda *refs: copies_body(plan, len(arrays), len(shapes),...  6.69 us
  transfers between devices with their start and end apart: 34, of which 15 were waited for; matrix products, arithmetic and copies ran while one was open for 3% of the time, Pallas kernels for 26%

profile of v2, /device:TPU:0, one launch (start us, length us, event | category | flops | bytes accessed | tf_op | source)
XLA Modules:
  0.0 225.9 jit_solution(620226149196739482)
XLA Ops:
  1.8 3.4 %collective-permute-start.6 = (bf16[2,2,256,128]{3,2,1,0:T(8,128)(2,1)S(1)}, bf16[2,2,256,128]{3,2,1,0:T(8,128)(2,1)S(1)}, u32[]{:S(2)}, u32[]{:S(2)}) collective-permute-start(bf16[2,2,256,128]{3,2,1,0:T(8,128)(2,1)S(1)} %get-tuple-element.56.refs_4_), channel_id=1, source_target_pairs={{0,2},{1,3},{2,0},{3,1},{4,6},{5,7},{6,4},{7,5},{8,10},{9,11},{10,... | collective-permute-start | bytes 786440 | tf_op jit(solution)/shard_map/ppermute | solution.py:45
  8.3 3.0 %collective-permute-start.3 = (bf16[2,2,256,128]{3,2,1,0:T(8,128)(2,1)S(1)}, bf16[2,2,256,128]{3,2,1,0:T(8,128)(2,1)S(1)}, u32[]{:S(2)}, u32[]{:S(2)}) collective-permute-start(bf16[2,2,256,128]{3,2,1,0:T(8,128)(2,1)S(1)} %get-tuple-element.57.refs_0_), channel_id=1, source_target_pairs={{0,16},{1,17},{2,18},{3,19},{4,20},{5,21},{6,22},{7,23},{8,24},{9,... | collective-permute-start | bytes 786440 | tf_op jit(solution)/shard_map/ppermute | solution.py:45
  12.6 2.8 %collective-permute-start.1 = (bf16[2,2,256,128]{3,2,1,0:T(8,128)(2,1)S(1)}, bf16[2,2,256,128]{3,2,1,0:T(8,128)(2,1)S(1)}, u32[]{:S(2)}, u32[]{:S(2)}) collective-permute-start(bf16[2,2,256,128]{3,2,1,0:T(8,128)(2,1)S(1)} %get-tuple-element.57.refs_0_), channel_id=1, source_target_pairs={{0,24},{1,25},{2,26},{3,27},{4,28},{5,29},{6,30},{7,31},{8,0},{9,1... | collective-permute-start | bytes 786440 | tf_op jit(solution)/shard_map/ppermute | solution.py:45
  19.1 3.6 %collective-permute-done.2.refs_2_ = bf16[2,2,256,128]{3,2,1,0:T(8,128)(2,1)S(1)} collective-permute-done((bf16[2,2,256,128]{3,2,1,0:T(8,128)(2,1)S(1)}, bf16[2,2,256,128]{3,2,1,0:T(8,128)(2,1)S(1)}, u32[]{:S(2)}, u32[]{:S(2)}) %collective-permute-start.2) | collective-permute-done | bytes 262176 | tf_op jit(solution)/shard_map/ppermute | solution.py:45
  26.5 3.2 %collective-permute-start.7 = (bf16[2,4,2,256,128]{4,3,2,1,0:T(8,128)(2,1)S(1)}, bf16[2,4,2,256,128]{4,3,2,1,0:T(8,128)(2,1)S(1)}, u32[]{:S(2)}, u32[]{:S(2)}) collective-permute-start(bf16[2,4,2,256,128]{4,3,2,1,0:T(8,128)(2,1)S(1)} %get-tuple-element.27.refs_3_), channel_id=1, source_target_pairs={{0,3},{1,0},{2,1},{3,2},{4,7},{5,4},{6,5},{7,6},{8,11},{9,8},{10,9... | collective-permute-start | bytes 3145736 | tf_op jit(solution)/shard_map/ppermute | solution.py:45
  32.9 18.9 %collective-permute-done.8.refs_1_.refs_5_ = bf16[2,4,2,256,128]{4,3,2,1,0:T(8,128)(2,1)S(1)} collective-permute-done((bf16[2,4,2,256,128]{4,3,2,1,0:T(8,128)(2,1)S(1)}, bf16[2,4,2,256,128]{4,3,2,1,0:T(8,128)(2,1)S(1)}, u32[]{:S(2)}, u32[]{:S(2)}) %collective-permute-start.8) | collective-permute-done | bytes 1048608 | tf_op jit(solution)/shard_map/ppermute | solution.py:45
  56.6 3.2 %collective-permute-start.12 = (bf16[4,2,256,128]{3,2,1,0:T(8,128)(2,1)}, bf16[4,2,256,128]{3,2,1,0:T(8,128)(2,1)}, u32[]{:S(2)}, u32[]{:S(2)}) collective-permute-start(bf16[4,2,256,128]{3,2,1,0:T(8,128)(2,1)} %get-tuple-element.30), channel_id=1, source_target_pairs={{0,3},{1,0},{2,1},{3,2},{4,7},{5,4},{6,5},{7,6},{8,11},{9,8},{10,9... | collective-permute-start | bytes 1572872 | tf_op jit(solution)/shard_map/ppermute | solution.py:45
  60.0 3.0 %collective-permute-start.14 = (bf16[4,2,256,128]{3,2,1,0:T(8,128)(2,1)}, bf16[4,2,256,128]{3,2,1,0:T(8,128)(2,1)}, u32[]{:S(2)}, u32[]{:S(2)}) collective-permute-start(bf16[4,2,256,128]{3,2,1,0:T(8,128)(2,1)} %get-tuple-element.32), channel_id=1, source_target_pairs={{0,24},{1,25},{2,26},{3,27},{4,28},{5,29},{6,30},{7,31},{8,0},{9,1... | collective-permute-start | bytes 1572872 | tf_op jit(solution)/shard_map/ppermute | solution.py:45
  63.2 8.6 %collective-permute-done.15.refs_0_ = bf16[2,2,4,2,256,128]{5,4,3,2,1,0:T(8,128)(2,1)S(1)} collective-permute-done((bf16[2,2,4,2,256,128]{5,4,3,2,1,0:T(8,128)(2,1)}, bf16[2,2,4,2,256,128]{5,4,3,2,1,0:T(8,128)(2,1)S(1)}, u32[]{:S(2)}, u32[]{:S(2)}) %collective-permute-start.15) | collective-permute-done | bytes 2097184 | tf_op jit(solution)/shard_map/ppermute | solution.py:45
  76.4 3.2 %collective-permute-start.16 = (bf16[2,4,2,256,128]{4,3,2,1,0:T(8,128)(2,1)S(1)}, bf16[2,4,2,256,128]{4,3,2,1,0:T(8,128)(2,1)}, u32[]{:S(2)}, u32[]{:S(2)}) collective-permute-start(bf16[2,4,2,256,128]{4,3,2,1,0:T(8,128)(2,1)S(1)} %get-tuple-element.34.refs_13_.refs_3_), channel_id=1, source_target_pairs={{0,3},{1,0},{2,1},{3,2},{4,7},{5,4},{6,5},{7,6},{8,11},{9,8},{10,9... | collective-permute-start | bytes 3145736 | tf_op jit(solution)/shard_map/ppermute | solution.py:45
  81.0 21.8 %columns.3 = (bf16[2,16,2,160,128]{4,3,2,1,0:T(8,128)(2,1)}, bf16[2,16,2,160,128]{4,3,2,1,0:T(8,128)(2,1)}) custom-call(s32[162]{0:T(256)} %pad_add_fusion.refs_0_, bf16[1,2,96,384,128]{4,3,2,1,0:T(8,128)(2,1)} %refs_1_.5, bf16[2,128,128]{2,1,0:T(8,128)(2,1)} %bitcast.80, bf16[2,4,2,256,128]{4,3,2,1,0:T(8,128)(2,1)} %copy-done.14, ...), custom_call_target="tpu_custom_call" | custom-call | flops 6442450944 | bytes 33554432 | tf_op jit(solution)/shard_map/columns/pallas_call | solution.py:257
  115.0 3.9 %pair_sums.3.refs_9_ = bf16[16,2,128,128]{3,2,1,0:T(8,128)(2,1)} custom-call(f32[2,4]{1,0:T(2,128)S(1)} %pad_maximum_fusion.refs_0_.coef, bf16[2,16,2,160,128]{4,3,2,1,0:T(8,128)(2,1)S(1)} %copy-done, bf16[2,16,2,160,128]{4,3,2,1,0:T(8,128)(2,1)} %collective-permute-done.20.refs_2_.other), custom_call_target="tpu_custom_call" | custom-call | bytes 1 | tf_op jit(solution)/shard_map/pair_sums/pallas_call | solution.py:311
  118.9 3.7 %collective-permute-start.21 = (bf16[16,2,128,128]{3,2,1,0:T(8,128)(2,1)}, bf16[16,2,128,128]{3,2,1,0:T(8,128)(2,1)}, u32[]{:S(2)}, u32[]{:S(2)}) collective-permute-start(bf16[16,2,128,128]{3,2,1,0:T(8,128)(2,1)} %pair_sums.3.refs_9_), channel_id=1, source_target_pairs={{0,64},{32,96},{64,0},{96,32},{1,65},{33,97},{65,1},{97,33},{2,66}... | collective-permute-start | bytes 3145736 | tf_op jit(solution)/shard_map/ppermute | solution.py:454
  130.4 13.2 %columns.4 = (bf16[2,9,2,160,128]{4,3,2,1,0:T(8,128)(2,1)}, bf16[2,9,2,160,128]{4,3,2,1,0:T(8,128)(2,1)}) custom-call(s32[92]{0:T(128)} %pad_add_fusion.2.refs_0_, bf16[1,2,96,384,128]{4,3,2,1,0:T(8,128)(2,1)} %refs_1_.5, bf16[2,128,128]{2,1,0:T(8,128)(2,1)} %bitcast.81, bf16[2,4,2,256,128]{4,3,2,1,0:T(8,128)(2,1)} %copy-done.1, ...), custom_call_target="tpu_custom_call" | custom-call | flops 3623878656 | bytes 18874368 | tf_op jit(solution)/shard_map/columns/pallas_call | solution.py:257
  144.5 11.3 %columns.5 = (bf16[2,7,2,160,128]{4,3,2,1,0:T(8,128)(2,1)}, bf16[2,7,2,160,128]{4,3,2,1,0:T(8,128)(2,1)}) custom-call(s32[72]{0:T(128)} %pad_add_fusion.3.refs_0_, bf16[1,2,96,384,128]{4,3,2,1,0:T(8,128)(2,1)} %refs_1_.5, bf16[2,128,128]{2,1,0:T(8,128)(2,1)} %bitcast.82, bf16[2,4,2,256,128]{4,3,2,1,0:T(8,128)(2,1)} %copy-done.1, ...), custom_call_target="tpu_custom_call" | custom-call | flops 2818572288 | bytes 14680064 | tf_op jit(solution)/shard_map/columns/pallas_call | solution.py:257
  158.9 3.3 %own_sums.1.refs_3_ = bf16[16,2,128,128]{3,2,1,0:T(8,128)(2,1)S(1)} custom-call(f32[2,4]{1,0:T(2,128)S(1)} %pad_maximum_fusion.refs_0_.coef, s32[16]{0:T(128)S(1)} %stack.222.order, bf16[2,16,2,160,128]{4,3,2,1,0:T(8,128)(2,1)S(1)} %copy-done, bf16[2,16,2,160,128]{4,3,2,1,0:T(8,128)(2,1)} %collective-permute-done.20.refs_2_.other, ...), custom_call_target="tpu_custom_call" | custom-call | bytes 1 | tf_op jit(solution)/shard_map/own_sums/pallas_call | solution.py:337
  163.2 3.8 %all-to-all-start = ((bf16[16,2,128,128]{3,2,1,0:T(8,128)(2,1)}), bf16[16,2,128,128]{3,2,1,0:T(8,128)(2,1)S(1)}, u32[]{:S(2)}, u32[]{:S(2)}) async-start(bf16[16,2,128,128]{3,2,1,0:T(8,128)(2,1)} %copy-done.4), calls=%async_computation | async-start | bytes 2097152 | tf_op jit(solution)/shard_map/all_to_all | solution.py:403
  168.3 3.6 %pair_sums.4 = (bf16[9,2,128,128]{3,2,1,0:T(8,128)(2,1)}, bf16[9,2,128,128]{3,2,1,0:T(8,128)(2,1)}) custom-call(f32[2,4]{1,0:T(2,128)S(1)} %pad_maximum_fusion.refs_0_.coef, bf16[2,9,2,160,128]{4,3,2,1,0:T(8,128)(2,1)S(1)} %copy-done.12, bf16[2,9,2,160,128]{4,3,2,1,0:T(8,128)(2,1)} %collective-permute-done.26.refs_2_, bf16[16,2,128,128]{3,2,1,0:T(8,128)(2,1)S(1)} %copy-done.5), custom_call_target="tpu_custom_call" | custom-call | bytes 1 | tf_op jit(solution)/shard_map/pair_sums/pallas_call | solution.py:311
  172.5 3.1 %pair_sums.5 = (bf16[7,2,128,128]{3,2,1,0:T(8,128)(2,1)}, bf16[7,2,128,128]{3,2,1,0:T(8,128)(2,1)}) custom-call(f32[2,4]{1,0:T(2,128)S(1)} %pad_maximum_fusion.refs_0_.coef, bf16[2,7,2,160,128]{4,3,2,1,0:T(8,128)(2,1)S(1)} %copy-done.13, bf16[2,7,2,160,128]{4,3,2,1,0:T(8,128)(2,1)} %collective-permute-done.29.refs_2_), custom_call_target="tpu_custom_call" | custom-call | bytes 1 | tf_op jit(solution)/shard_map/pair_sums/pallas_call | solution.py:311
  179.7 5.4 %all-to-all-done.refs_1_.own = bf16[16,2,128,128]{3,2,1,0:T(8,128)(2,1)S(1)} async-done(((bf16[16,2,128,128]{3,2,1,0:T(8,128)(2,1)}), bf16[16,2,128,128]{3,2,1,0:T(8,128)(2,1)S(1)}, u32[]{:S(2)}, u32[]{:S(2)}) %all-to-all-start) | async-done | bytes 1048608 | tf_op jit(solution)/shard_map/all_to_all | solution.py:403
  185.2 3.2 %collective-permute-done.27.refs_0_ = bf16[9,2,128,128]{3,2,1,0:T(8,128)(2,1)S(1)} collective-permute-done((bf16[9,2,128,128]{3,2,1,0:T(8,128)(2,1)}, bf16[9,2,128,128]{3,2,1,0:T(8,128)(2,1)S(1)}, u32[]{:S(2)}, u32[]{:S(2)}) %collective-permute-start.27) | collective-permute-done | bytes 589856 | tf_op jit(solution)/shard_map/ppermute | solution.py:45
  188.3 8.9 %collective-permute-done.30.refs_2_ = bf16[7,2,128,128]{3,2,1,0:T(8,128)(2,1)S(1)} collective-permute-done((bf16[7,2,128,128]{3,2,1,0:T(8,128)(2,1)}, bf16[7,2,128,128]{3,2,1,0:T(8,128)(2,1)S(1)}, u32[]{:S(2)}, u32[]{:S(2)}) %collective-permute-start.30) | collective-permute-done | bytes 458784 | tf_op jit(solution)/shard_map/ppermute | solution.py:45
  200.2 6.9 %all-to-all-start.1 = ((bf16[16,2,128,128]{3,2,1,0:T(8,128)(2,1)}), bf16[16,2,128,128]{3,2,1,0:T(8,128)(2,1)S(1)}, u32[]{:S(2)}, u32[]{:S(2)}) async-start(bf16[16,2,128,128]{3,2,1,0:T(8,128)(2,1)} %next_sums.1), calls=%async_computation.1 | async-start | bytes 2097152 | tf_op jit(solution)/shard_map/all_to_all | solution.py:403
  207.2 15.9 %all-to-all-done.1.other = bf16[16,2,128,128]{3,2,1,0:T(8,128)(2,1)S(1)} async-done(((bf16[16,2,128,128]{3,2,1,0:T(8,128)(2,1)}), bf16[16,2,128,128]{3,2,1,0:T(8,128)(2,1)S(1)}, u32[]{:S(2)}, u32[]{:S(2)}) %all-to-all-start.1) | async-done | bytes 1048608 | tf_op jit(solution)/shard_map/all_to_all | solution.py:403
  (144 shorter events, 58.7 us)
Async XLA Ops:
  24.5 47.4 %collective-permute-start.15 = (bf16[2,2,4,2,256,128]{5,4,3,2,1,0:T(8,128)(2,1)}, bf16[2,2,4,2,256,128]{5,4,3,2,1,0:T(8,128)(2,1)S(1)}, u32[]{:S(2)}, u32[]{:S(2)}) collective-permute-start(bf16[2,2,4,2,256,128]{5,4,3,2,1,0:T(8,128)(2,1)} %get-tuple-element.33), channel_id=1, source_target_pairs={{0,4},{1,5},{2,6},{3,7},{4,0},{5,1},{6,2},{7,3},{8,12},{9,13},{10,... | collective-permute-start | bytes 6291464 | tf_op jit(solution)/shard_map/ppermute | solution.py:45
  26.5 25.4 %collective-permute-start.8 = (bf16[2,4,2,256,128]{4,3,2,1,0:T(8,128)(2,1)S(1)}, bf16[2,4,2,256,128]{4,3,2,1,0:T(8,128)(2,1)S(1)}, u32[]{:S(2)}, u32[]{:S(2)}) collective-permute-start(bf16[2,4,2,256,128]{4,3,2,1,0:T(8,128)(2,1)S(1)} %get-tuple-element.27.refs_3_), channel_id=1, source_target_pairs={{0,1},{1,2},{2,3},{3,0},{4,5},{5,6},{6,7},{7,4},{8,9},{9,10},{10,1... | collective-permute-start | bytes 3145736 | tf_op jit(solution)/shard_map/ppermute | solution.py:45
  26.5 25.4 %collective-permute-start.7 = (bf16[2,4,2,256,128]{4,3,2,1,0:T(8,128)(2,1)S(1)}, bf16[2,4,2,256,128]{4,3,2,1,0:T(8,128)(2,1)S(1)}, u32[]{:S(2)}, u32[]{:S(2)}) collective-permute-start(bf16[2,4,2,256,128]{4,3,2,1,0:T(8,128)(2,1)S(1)} %get-tuple-element.27.refs_3_), channel_id=1, source_target_pairs={{0,3},{1,0},{2,1},{3,2},{4,7},{5,4},{6,5},{7,6},{8,11},{9,8},{10,9... | collective-permute-start | bytes 3145736 | tf_op jit(solution)/shard_map/ppermute | solution.py:45
  29.7 24.8 %collective-permute-start.10 = (bf16[2,4,2,256,128]{4,3,2,1,0:T(8,128)(2,1)S(1)}, bf16[2,4,2,256,128]{4,3,2,1,0:T(8,128)(2,1)S(1)}, u32[]{:S(2)}, u32[]{:S(2)}) collective-permute-start(bf16[2,4,2,256,128]{4,3,2,1,0:T(8,128)(2,1)S(1)} %get-tuple-element.28.refs_8_), channel_id=1, source_target_pairs={{0,8},{1,9},{2,10},{3,11},{4,12},{5,13},{6,14},{7,15},{8,16},{9,17... | collective-permute-start | bytes 3145736 | tf_op jit(solution)/shard_map/ppermute | solution.py:45
  31.2 23.4 %collective-permute-start.9 = (bf16[2,4,2,256,128]{4,3,2,1,0:T(8,128)(2,1)S(1)}, bf16[2,4,2,256,128]{4,3,2,1,0:T(8,128)(2,1)S(1)}, u32[]{:S(2)}, u32[]{:S(2)}) collective-permute-start(bf16[2,4,2,256,128]{4,3,2,1,0:T(8,128)(2,1)S(1)} %get-tuple-element.28.refs_8_), channel_id=1, source_target_pairs={{0,24},{1,25},{2,26},{3,27},{4,28},{5,29},{6,30},{7,31},{8,0},{9,1... | collective-permute-start | bytes 3145736 | tf_op jit(solution)/shard_map/ppermute | solution.py:45
  56.6 18.0 %collective-permute-start.11 = (bf16[4,2,256,128]{3,2,1,0:T(8,128)(2,1)}, bf16[4,2,256,128]{3,2,1,0:T(8,128)(2,1)}, u32[]{:S(2)}, u32[]{:S(2)}) collective-permute-start(bf16[4,2,256,128]{3,2,1,0:T(8,128)(2,1)} %get-tuple-element.29), channel_id=1, source_target_pairs={{0,1},{1,2},{2,3},{3,0},{4,5},{5,6},{6,7},{7,4},{8,9},{9,10},{10,1... | collective-permute-start | bytes 1572872 | tf_op jit(solution)/shard_map/ppermute | solution.py:45
  56.6 19.9 %collective-permute-start.12 = (bf16[4,2,256,128]{3,2,1,0:T(8,128)(2,1)}, bf16[4,2,256,128]{3,2,1,0:T(8,128)(2,1)}, u32[]{:S(2)}, u32[]{:S(2)}) collective-permute-start(bf16[4,2,256,128]{3,2,1,0:T(8,128)(2,1)} %get-tuple-element.30), channel_id=1, source_target_pairs={{0,3},{1,0},{2,1},{3,2},{4,7},{5,4},{6,5},{7,6},{8,11},{9,8},{10,9... | collective-permute-start | bytes 1572872 | tf_op jit(solution)/shard_map/ppermute | solution.py:45
  59.8 16.6 %collective-permute-start.13 = (bf16[4,2,256,128]{3,2,1,0:T(8,128)(2,1)}, bf16[4,2,256,128]{3,2,1,0:T(8,128)(2,1)}, u32[]{:S(2)}, u32[]{:S(2)}) collective-permute-start(bf16[4,2,256,128]{3,2,1,0:T(8,128)(2,1)} %get-tuple-element.31), channel_id=1, source_target_pairs={{0,8},{1,9},{2,10},{3,11},{4,12},{5,13},{6,14},{7,15},{8,16},{9,17... | collective-permute-start | bytes 1572872 | tf_op jit(solution)/shard_map/ppermute | solution.py:45
  60.0 21.0 %collective-permute-start.14 = (bf16[4,2,256,128]{3,2,1,0:T(8,128)(2,1)}, bf16[4,2,256,128]{3,2,1,0:T(8,128)(2,1)}, u32[]{:S(2)}, u32[]{:S(2)}) collective-permute-start(bf16[4,2,256,128]{3,2,1,0:T(8,128)(2,1)} %get-tuple-element.32), channel_id=1, source_target_pairs={{0,24},{1,25},{2,26},{3,27},{4,28},{5,29},{6,30},{7,31},{8,0},{9,1... | collective-permute-start | bytes 1572872 | tf_op jit(solution)/shard_map/ppermute | solution.py:45
  73.1 29.7 %collective-permute-start.19 = (bf16[2,4,2,256,128]{4,3,2,1,0:T(8,128)(2,1)}, bf16[2,4,2,256,128]{4,3,2,1,0:T(8,128)(2,1)S(1)}, u32[]{:S(2)}, u32[]{:S(2)}) collective-permute-start(bf16[2,4,2,256,128]{4,3,2,1,0:T(8,128)(2,1)} %get-tuple-element.37.refs_6_.refs_8_), channel_id=1, source_target_pairs={{0,8},{1,9},{2,10},{3,11},{4,12},{5,13},{6,14},{7,15},{8,16},{9,17... | collective-permute-start | bytes 3145736 | tf_op jit(solution)/shard_map/ppermute | solution.py:45
  74.6 28.2 %collective-permute-start.18 = (bf16[2,4,2,256,128]{4,3,2,1,0:T(8,128)(2,1)}, bf16[2,4,2,256,128]{4,3,2,1,0:T(8,128)(2,1)S(1)}, u32[]{:S(2)}, u32[]{:S(2)}) collective-permute-start(bf16[2,4,2,256,128]{4,3,2,1,0:T(8,128)(2,1)} %get-tuple-element.37.refs_6_.refs_8_), channel_id=1, source_target_pairs={{0,24},{1,25},{2,26},{3,27},{4,28},{5,29},{6,30},{7,31},{8,0},{9,1... | collective-permute-start | bytes 3145736 | tf_op jit(solution)/shard_map/ppermute | solution.py:45
  76.4 26.4 %collective-permute-start.17 = (bf16[2,4,2,256,128]{4,3,2,1,0:T(8,128)(2,1)S(1)}, bf16[2,4,2,256,128]{4,3,2,1,0:T(8,128)(2,1)}, u32[]{:S(2)}, u32[]{:S(2)}) collective-permute-start(bf16[2,4,2,256,128]{4,3,2,1,0:T(8,128)(2,1)S(1)} %get-tuple-element.34.refs_13_.refs_3_), channel_id=1, source_target_pairs={{0,1},{1,2},{2,3},{3,0},{4,5},{5,6},{6,7},{7,4},{8,9},{9,10},{10,1... | collective-permute-start | bytes 3145736 | tf_op jit(solution)/shard_map/ppermute | solution.py:45
  76.4 26.4 %collective-permute-start.16 = (bf16[2,4,2,256,128]{4,3,2,1,0:T(8,128)(2,1)S(1)}, bf16[2,4,2,256,128]{4,3,2,1,0:T(8,128)(2,1)}, u32[]{:S(2)}, u32[]{:S(2)}) collective-permute-start(bf16[2,4,2,256,128]{4,3,2,1,0:T(8,128)(2,1)S(1)} %get-tuple-element.34.refs_13_.refs_3_), channel_id=1, source_target_pairs={{0,3},{1,0},{2,1},{3,2},{4,7},{5,4},{6,5},{7,6},{8,11},{9,8},{10,9... | collective-permute-start | bytes 3145736 | tf_op jit(solution)/shard_map/ppermute | solution.py:45
  118.9 36.9 %collective-permute-start.21 = (bf16[16,2,128,128]{3,2,1,0:T(8,128)(2,1)}, bf16[16,2,128,128]{3,2,1,0:T(8,128)(2,1)}, u32[]{:S(2)}, u32[]{:S(2)}) collective-permute-start(bf16[16,2,128,128]{3,2,1,0:T(8,128)(2,1)} %pair_sums.3.refs_9_), channel_id=1, source_target_pairs={{0,64},{32,96},{64,0},{96,32},{1,65},{33,97},{65,1},{97,33},{2,66}... | collective-permute-start | bytes 3145736 | tf_op jit(solution)/shard_map/ppermute | solution.py:454
  123.9 19.8 %collective-permute-start.23 = (bf16[4,2,256,128]{3,2,1,0:T(8,128)(2,1)S(1)}, bf16[4,2,256,128]{3,2,1,0:T(8,128)(2,1)S(1)}, u32[]{:S(2)}, u32[]{:S(2)}) collective-permute-start(bf16[4,2,256,128]{3,2,1,0:T(8,128)(2,1)S(1)} %copy-done.17), channel_id=1, source_target_pairs={{0,3},{1,0},{2,1},{3,2},{4,7},{5,4},{6,5},{7,6},{8,11},{9,8},{10,9... | collective-permute-start | bytes 1572872 | tf_op jit(solution)/shard_map/ppermute | solution.py:45
  124.2 19.5 %collective-permute-start.22 = (bf16[4,2,256,128]{3,2,1,0:T(8,128)(2,1)}, bf16[4,2,256,128]{3,2,1,0:T(8,128)(2,1)}, u32[]{:S(2)}, u32[]{:S(2)}) collective-permute-start(bf16[4,2,256,128]{3,2,1,0:T(8,128)(2,1)} %copy-done.20), channel_id=1, source_target_pairs={{0,1},{1,2},{2,3},{3,0},{4,5},{5,6},{6,7},{7,4},{8,9},{9,10},{10,1... | collective-permute-start | bytes 1572872 | tf_op jit(solution)/shard_map/ppermute | solution.py:45
  126.0 17.7 %collective-permute-start.24 = (bf16[4,2,256,128]{3,2,1,0:T(8,128)(2,1)}, bf16[4,2,256,128]{3,2,1,0:T(8,128)(2,1)}, u32[]{:S(2)}, u32[]{:S(2)}) collective-permute-start(bf16[4,2,256,128]{3,2,1,0:T(8,128)(2,1)} %copy-done.19), channel_id=1, source_target_pairs={{0,8},{1,9},{2,10},{3,11},{4,12},{5,13},{6,14},{7,15},{8,16},{9,17... | collective-permute-start | bytes 1572872 | tf_op jit(solution)/shard_map/ppermute | solution.py:45
  127.0 16.7 %collective-permute-start.25 = (bf16[4,2,256,128]{3,2,1,0:T(8,128)(2,1)}, bf16[4,2,256,128]{3,2,1,0:T(8,128)(2,1)}, u32[]{:S(2)}, u32[]{:S(2)}) collective-permute-start(bf16[4,2,256,128]{3,2,1,0:T(8,128)(2,1)} %copy-done.18), channel_id=1, source_target_pairs={{0,24},{1,25},{2,26},{3,27},{4,28},{5,29},{6,30},{7,31},{8,0},{9,1... | collective-permute-start | bytes 1572872 | tf_op jit(solution)/shard_map/ppermute | solution.py:45
  163.2 22.0 %all-to-all-start = ((bf16[16,2,128,128]{3,2,1,0:T(8,128)(2,1)}), bf16[16,2,128,128]{3,2,1,0:T(8,128)(2,1)S(1)}, u32[]{:S(2)}, u32[]{:S(2)}) async-start(bf16[16,2,128,128]{3,2,1,0:T(8,128)(2,1)} %copy-done.4), calls=%async_computation | async-start | bytes 2097152 | tf_op jit(solution)/shard_map/all_to_all | solution.py:403
  171.9 16.4 %collective-permute-start.27 = (bf16[9,2,128,128]{3,2,1,0:T(8,128)(2,1)}, bf16[9,2,128,128]{3,2,1,0:T(8,128)(2,1)S(1)}, u32[]{:S(2)}, u32[]{:S(2)}) collective-permute-start(bf16[9,2,128,128]{3,2,1,0:T(8,128)(2,1)} %get-tuple-element.45), channel_id=1, source_target_pairs={{0,4},{1,5},{2,6},{3,7},{4,0},{5,1},{6,2},{7,3},{8,12},{9,13},{10,... | collective-permute-start | bytes 1769480 | tf_op jit(solution)/shard_map/ppermute | solution.py:45
  172.0 26.4 %collective-permute-start.28 = (bf16[9,2,128,128]{3,2,1,0:T(8,128)(2,1)}, bf16[9,2,128,128]{3,2,1,0:T(8,128)(2,1)S(1)}, u32[]{:S(2)}, u32[]{:S(2)}) collective-permute-start(bf16[9,2,128,128]{3,2,1,0:T(8,128)(2,1)} %get-tuple-element.46), channel_id=1, source_target_pairs={{0,68},{1,69},{2,70},{3,71},{4,64},{5,65},{6,66},{7,67},{8,76},{9,... | collective-permute-start | bytes 1769480 | tf_op jit(solution)/shard_map/ppermute | solution.py:466
  175.5 21.6 %collective-permute-start.30 = (bf16[7,2,128,128]{3,2,1,0:T(8,128)(2,1)}, bf16[7,2,128,128]{3,2,1,0:T(8,128)(2,1)S(1)}, u32[]{:S(2)}, u32[]{:S(2)}) collective-permute-start(bf16[7,2,128,128]{3,2,1,0:T(8,128)(2,1)} %get-tuple-element.48), channel_id=1, source_target_pairs={{0,4},{1,5},{2,6},{3,7},{4,0},{5,1},{6,2},{7,3},{8,12},{9,13},{10,... | collective-permute-start | bytes 1376264 | tf_op jit(solution)/shard_map/ppermute | solution.py:45
  177.0 21.4 %collective-permute-start.31 = (bf16[7,2,128,128]{3,2,1,0:T(8,128)(2,1)}, bf16[7,2,128,128]{3,2,1,0:T(8,128)(2,1)S(1)}, u32[]{:S(2)}, u32[]{:S(2)}) collective-permute-start(bf16[7,2,128,128]{3,2,1,0:T(8,128)(2,1)} %get-tuple-element.49), channel_id=1, source_target_pairs={{0,68},{1,69},{2,70},{3,71},{4,64},{5,65},{6,66},{7,67},{8,76},{9,... | collective-permute-start | bytes 1376264 | tf_op jit(solution)/shard_map/ppermute | solution.py:466
  200.2 22.8 %all-to-all-start.1 = ((bf16[16,2,128,128]{3,2,1,0:T(8,128)(2,1)}), bf16[16,2,128,128]{3,2,1,0:T(8,128)(2,1)S(1)}, u32[]{:S(2)}, u32[]{:S(2)}) async-start(bf16[16,2,128,128]{3,2,1,0:T(8,128)(2,1)} %next_sums.1), calls=%async_computation.1 | async-start | bytes 2097152 | tf_op jit(solution)/shard_map/all_to_all | solution.py:403
  (38 other events, 314.3 us)

commit v3 on v2

--- a/solution.py
+++ b/solution.py
@@ -272,7 +272,7 @@
             pltpu.SemaphoreType.DMA((AHEAD,)),
             pltpu.SemaphoreType.DMA((n_copies,)),
         ],
-        compiler_params=pltpu.CompilerParams(vmem_limit_bytes=60 * 2**20),
+        compiler_params=pltpu.CompilerParams(vmem_limit_bytes=28 * 2**20),
         cost_estimate=pl.CostEstimate(
             flops=2 * count * ROWS * 2 * M * B * 2 * B,
             bytes_accessed=count * (2 * M * B * B * 2 + 2 * M * ROWS * B * 2),

time: 227 us -> 227 us (level)
  local copies, waits for them, and re-layouts: 11.4 us -> 21.1 us
  Pallas kernels: 71.5 us -> 64.4 us
    unnamed x57 -> x61, local copies, waits for them, and re-layouts: 7.22 us -> 17 us
    pallas_call x3, Pallas kernels: 46.3 us -> 39.4 us  [columns_of(): pl.pallas_call(lambda *refs: column_body(places, with_own, *refs), out_sh...]
  transfers between devices with their start and end apart: 34 -> 34, of which waited for: 15 -> 15; matrix products, arithmetic and copies ran while one was open for 3% -> 2% of each run, Pallas kernels for 26% -> 23%
where the time goes in v3:
time: 227 us
  waiting for transfers between devices  72.4 us (32%)
  Pallas kernels  64.4 us (28%)
  starting transfers between devices  61.8 us (27%)
  local copies, waits for them, and re-layouts  21.1 us (9%)
  between operations  5.96 us (3%)
    ppermute x25, waiting for transfers between devices, send(): return lax.ppermute(value, 'snode', shift(**by))  49 us
    ppermute x25, starting transfers between devices, send(): return lax.ppermute(value, 'snode', shift(**by))  43.2 us
    pallas_call x3, Pallas kernels, columns_of(): pl.pallas_call(lambda *refs: column_body(places, with_own, *refs), out_sh...  39.4 us
    all_to_all x2, waiting for transfers between devices, in_plane(): lax.all_to_all(value, 'snode', split_axis=0, concat_axis=0, axis_index_gr...  20.1 us
    unnamed x61, local copies, waits for them, and re-layouts  17 us
    all_to_all x2, starting transfers between devices, in_plane(): lax.all_to_all(value, 'snode', split_axis=0, concat_axis=0, axis_index_gr...  11.7 us
    pallas_call x3, Pallas kernels, pair_sums(): pl.pallas_call(lambda *refs: pair_body(parts, *refs), out_shape=[jax.Shap...  10.5 us
    pallas_call x4, Pallas kernels, copied(): pl.pallas_call(lambda *refs: copies_body(plan, len(arrays), len(shapes),...  6.52 us
  transfers between devices with their start and end apart: 34, of which 15 were waited for; matrix products, arithmetic and copies ran while one was open for 2% of the time, Pallas kernels for 23%

profile of v3, /device:TPU:0, one launch (start us, length us, event | category | flops | bytes accessed | tf_op | source)
XLA Modules:
  0.0 227.3 jit_solution(13104808482354822237)
XLA Ops:
  1.8 3.4 %collective-permute-start.6 = (bf16[2,2,256,128]{3,2,1,0:T(8,128)(2,1)S(1)}, bf16[2,2,256,128]{3,2,1,0:T(8,128)(2,1)S(1)}, u32[]{:S(2)}, u32[]{:S(2)}) collective-permute-start(bf16[2,2,256,128]{3,2,1,0:T(8,128)(2,1)S(1)} %get-tuple-element.56.refs_4_), channel_id=1, source_target_pairs={{0,2},{1,3},{2,0},{3,1},{4,6},{5,7},{6,4},{7,5},{8,10},{9,11},{10,... | collective-permute-start | bytes 786440 | tf_op jit(solution)/shard_map/ppermute | solution.py:45
  8.3 3.0 %collective-permute-start.3 = (bf16[2,2,256,128]{3,2,1,0:T(8,128)(2,1)S(1)}, bf16[2,2,256,128]{3,2,1,0:T(8,128)(2,1)S(1)}, u32[]{:S(2)}, u32[]{:S(2)}) collective-permute-start(bf16[2,2,256,128]{3,2,1,0:T(8,128)(2,1)S(1)} %get-tuple-element.57.refs_0_), channel_id=1, source_target_pairs={{0,16},{1,17},{2,18},{3,19},{4,20},{5,21},{6,22},{7,23},{8,24},{9,... | collective-permute-start | bytes 786440 | tf_op jit(solution)/shard_map/ppermute | solution.py:45
  19.1 3.6 %collective-permute-done.2.refs_2_ = bf16[2,2,256,128]{3,2,1,0:T(8,128)(2,1)S(1)} collective-permute-done((bf16[2,2,256,128]{3,2,1,0:T(8,128)(2,1)S(1)}, bf16[2,2,256,128]{3,2,1,0:T(8,128)(2,1)S(1)}, u32[]{:S(2)}, u32[]{:S(2)}) %collective-permute-start.2) | collective-permute-done | bytes 262176 | tf_op jit(solution)/shard_map/ppermute | solution.py:45
  26.5 3.2 %collective-permute-start.7 = (bf16[2,4,2,256,128]{4,3,2,1,0:T(8,128)(2,1)S(1)}, bf16[2,4,2,256,128]{4,3,2,1,0:T(8,128)(2,1)S(1)}, u32[]{:S(2)}, u32[]{:S(2)}) collective-permute-start(bf16[2,4,2,256,128]{4,3,2,1,0:T(8,128)(2,1)S(1)} %get-tuple-element.27.refs_3_), channel_id=1, source_target_pairs={{0,3},{1,0},{2,1},{3,2},{4,7},{5,4},{6,5},{7,6},{8,11},{9,8},{10,9... | collective-permute-start | bytes 3145736 | tf_op jit(solution)/shard_map/ppermute | solution.py:45
  34.9 17.0 %collective-permute-done.8.refs_1_.refs_5_ = bf16[2,4,2,256,128]{4,3,2,1,0:T(8,128)(2,1)S(1)} collective-permute-done((bf16[2,4,2,256,128]{4,3,2,1,0:T(8,128)(2,1)S(1)}, bf16[2,4,2,256,128]{4,3,2,1,0:T(8,128)(2,1)S(1)}, u32[]{:S(2)}, u32[]{:S(2)}) %collective-permute-start.8) | collective-permute-done | bytes 1048608 | tf_op jit(solution)/shard_map/ppermute | solution.py:45
  51.9 3.7 %collective-permute-done.10.refs_3_.refs_10_ = bf16[2,4,2,256,128]{4,3,2,1,0:T(8,128)(2,1)S(1)} collective-permute-done((bf16[2,4,2,256,128]{4,3,2,1,0:T(8,128)(2,1)S(1)}, bf16[2,4,2,256,128]{4,3,2,1,0:T(8,128)(2,1)S(1)}, u32[]{:S(2)}, u32[]{:S(2)}) %collective-permute-start.10) | collective-permute-done | bytes 1048608 | tf_op jit(solution)/shard_map/ppermute | solution.py:45
  57.5 3.2 %collective-permute-start.12 = (bf16[4,2,256,128]{3,2,1,0:T(8,128)(2,1)}, bf16[4,2,256,128]{3,2,1,0:T(8,128)(2,1)S(1)}, u32[]{:S(2)}, u32[]{:S(2)}) collective-permute-start(bf16[4,2,256,128]{3,2,1,0:T(8,128)(2,1)} %get-tuple-element.30), channel_id=1, source_target_pairs={{0,3},{1,0},{2,1},{3,2},{4,7},{5,4},{6,5},{7,6},{8,11},{9,8},{10,9... | collective-permute-start | bytes 1572872 | tf_op jit(solution)/shard_map/ppermute | solution.py:45
  61.0 3.0 %collective-permute-start.14 = (bf16[4,2,256,128]{3,2,1,0:T(8,128)(2,1)}, bf16[4,2,256,128]{3,2,1,0:T(8,128)(2,1)}, u32[]{:S(2)}, u32[]{:S(2)}) collective-permute-start(bf16[4,2,256,128]{3,2,1,0:T(8,128)(2,1)} %get-tuple-element.32), channel_id=1, source_target_pairs={{0,24},{1,25},{2,26},{3,27},{4,28},{5,29},{6,30},{7,31},{8,0},{9,1... | collective-permute-start | bytes 1572872 | tf_op jit(solution)/shard_map/ppermute | solution.py:45
  64.2 7.7 %collective-permute-done.15.refs_0_ = bf16[2,2,4,2,256,128]{5,4,3,2,1,0:T(8,128)(2,1)S(1)} collective-permute-done((bf16[2,2,4,2,256,128]{5,4,3,2,1,0:T(8,128)(2,1)}, bf16[2,2,4,2,256,128]{5,4,3,2,1,0:T(8,128)(2,1)S(1)}, u32[]{:S(2)}, u32[]{:S(2)}) %collective-permute-start.15) | collective-permute-done | bytes 2097184 | tf_op jit(solution)/shard_map/ppermute | solution.py:45
  77.5 3.2 %collective-permute-start.16 = (bf16[2,4,2,256,128]{4,3,2,1,0:T(8,128)(2,1)}, bf16[2,4,2,256,128]{4,3,2,1,0:T(8,128)(2,1)}, u32[]{:S(2)}, u32[]{:S(2)}) collective-permute-start(bf16[2,4,2,256,128]{4,3,2,1,0:T(8,128)(2,1)} %get-tuple-element.34.refs_13_.refs_3_), channel_id=1, source_target_pairs={{0,3},{1,0},{2,1},{3,2},{4,7},{5,4},{6,5},{7,6},{8,11},{9,8},{10,9... | collective-permute-start | bytes 3145736 | tf_op jit(solution)/shard_map/ppermute | solution.py:45
  89.9 17.1 %columns.3 = (bf16[2,16,2,160,128]{4,3,2,1,0:T(8,128)(2,1)S(1)}, bf16[2,16,2,160,128]{4,3,2,1,0:T(8,128)(2,1)}) custom-call(s32[162]{0:T(256)S(1)} %pad_add_fusion.refs_0_, bf16[1,2,96,384,128]{4,3,2,1,0:T(8,128)(2,1)} %refs_1_.5, bf16[2,128,128]{2,1,0:T(8,128)(2,1)S(1)} %bitcast.79, bf16[2,4,2,256,128]{4,3,2,1,0:T(8,128)(2,1)S(1)} %copy-done.15, ...), custom_call_target="tpu_custom_call" | custom-call | flops 6442450944 | bytes 33554432 | tf_op jit(solution)/shard_map/columns/pallas_call | solution.py:257
  118.2 3.9 %pair_sums.3.refs_9_ = bf16[16,2,128,128]{3,2,1,0:T(8,128)(2,1)} custom-call(f32[2,4]{1,0:T(2,128)S(1)} %pad_maximum_fusion.refs_0_.coef, bf16[2,16,2,160,128]{4,3,2,1,0:T(8,128)(2,1)S(1)} %get-tuple-element.35.refs_1_.mine, bf16[2,16,2,160,128]{4,3,2,1,0:T(8,128)(2,1)} %collective-permute-done.20.refs_2_.other), custom_call_target="tpu_custom_call" | custom-call | bytes 1 | tf_op jit(solution)/shard_map/pair_sums/pallas_call | solution.py:311
  122.0 3.7 %collective-permute-start.21 = (bf16[16,2,128,128]{3,2,1,0:T(8,128)(2,1)}, bf16[16,2,128,128]{3,2,1,0:T(8,128)(2,1)}, u32[]{:S(2)}, u32[]{:S(2)}) collective-permute-start(bf16[16,2,128,128]{3,2,1,0:T(8,128)(2,1)} %pair_sums.3.refs_9_), channel_id=1, source_target_pairs={{0,64},{32,96},{64,0},{96,32},{1,65},{33,97},{65,1},{97,33},{2,66}... | collective-permute-start | bytes 3145736 | tf_op jit(solution)/shard_map/ppermute | solution.py:454
  132.4 12.7 %columns.4 = (bf16[2,9,2,160,128]{4,3,2,1,0:T(8,128)(2,1)S(1)}, bf16[2,9,2,160,128]{4,3,2,1,0:T(8,128)(2,1)}) custom-call(s32[92]{0:T(128)S(1)} %pad_add_fusion.2.refs_0_, bf16[1,2,96,384,128]{4,3,2,1,0:T(8,128)(2,1)} %refs_1_.5, bf16[2,128,128]{2,1,0:T(8,128)(2,1)S(1)} %bitcast.80, bf16[2,4,2,256,128]{4,3,2,1,0:T(8,128)(2,1)} %get-tuple-element.34.refs_13_.refs_3_, ...), custom_call_target="tpu_custom_call" | custom-call | flops 3623878656 | bytes 18874368 | tf_op jit(solution)/shard_map/columns/pallas_call | solution.py:257
  146.3 9.6 %columns.5 = (bf16[2,7,2,160,128]{4,3,2,1,0:T(8,128)(2,1)S(1)}, bf16[2,7,2,160,128]{4,3,2,1,0:T(8,128)(2,1)}) custom-call(s32[72]{0:T(128)S(1)} %pad_add_fusion.3.refs_0_, bf16[1,2,96,384,128]{4,3,2,1,0:T(8,128)(2,1)} %refs_1_.5, bf16[2,128,128]{2,1,0:T(8,128)(2,1)S(1)} %bitcast.81, bf16[2,4,2,256,128]{4,3,2,1,0:T(8,128)(2,1)} %get-tuple-element.34.refs_13_.refs_3_, ...), custom_call_target="tpu_custom_call" | custom-call | flops 2818572288 | bytes 14680064 | tf_op jit(solution)/shard_map/columns/pallas_call | solution.py:257
  157.5 3.3 %own_sums.1.refs_3_ = bf16[16,2,128,128]{3,2,1,0:T(8,128)(2,1)S(1)} custom-call(f32[2,4]{1,0:T(2,128)S(1)} %pad_maximum_fusion.refs_0_.coef, s32[16]{0:T(128)S(1)} %stack.222.order, bf16[2,16,2,160,128]{4,3,2,1,0:T(8,128)(2,1)S(1)} %get-tuple-element.35.refs_1_.mine, bf16[2,16,2,160,128]{4,3,2,1,0:T(8,128)(2,1)} %collective-permute-done.20.refs_2_.other, ...), custom_call_target="tpu_custom_call" | custom-call | bytes 1 | tf_op jit(solution)/shard_map/own_sums/pallas_call | solution.py:337
  161.7 4.9 %all-to-all-start = ((bf16[16,2,128,128]{3,2,1,0:T(8,128)(2,1)}), bf16[16,2,128,128]{3,2,1,0:T(8,128)(2,1)S(1)}, u32[]{:S(2)}, u32[]{:S(2)}) async-start(bf16[16,2,128,128]{3,2,1,0:T(8,128)(2,1)} %copy-done), calls=%async_computation | async-start | bytes 2097152 | tf_op jit(solution)/shard_map/all_to_all | solution.py:403
  167.9 3.6 %pair_sums.4 = (bf16[9,2,128,128]{3,2,1,0:T(8,128)(2,1)}, bf16[9,2,128,128]{3,2,1,0:T(8,128)(2,1)}) custom-call(f32[2,4]{1,0:T(2,128)S(1)} %pad_maximum_fusion.refs_0_.coef, bf16[2,9,2,160,128]{4,3,2,1,0:T(8,128)(2,1)S(1)} %copy-done.11, bf16[2,9,2,160,128]{4,3,2,1,0:T(8,128)(2,1)} %collective-permute-done.26.refs_2_, bf16[16,2,128,128]{3,2,1,0:T(8,128)(2,1)S(1)} %copy-done.1), custom_call_target="tpu_custom_call" | custom-call | bytes 1 | tf_op jit(solution)/shard_map/pair_sums/pallas_call | solution.py:311
  173.8 3.1 %pair_sums.5 = (bf16[7,2,128,128]{3,2,1,0:T(8,128)(2,1)}, bf16[7,2,128,128]{3,2,1,0:T(8,128)(2,1)}) custom-call(f32[2,4]{1,0:T(2,128)S(1)} %pad_maximum_fusion.refs_0_.coef, bf16[2,7,2,160,128]{4,3,2,1,0:T(8,128)(2,1)S(1)} %copy-done.13, bf16[2,7,2,160,128]{4,3,2,1,0:T(8,128)(2,1)} %collective-permute-done.29.refs_2_), custom_call_target="tpu_custom_call" | custom-call | bytes 1 | tf_op jit(solution)/shard_map/pair_sums/pallas_call | solution.py:311
  180.2 4.4 %all-to-all-done.refs_1_.own = bf16[16,2,128,128]{3,2,1,0:T(8,128)(2,1)S(1)} async-done(((bf16[16,2,128,128]{3,2,1,0:T(8,128)(2,1)}), bf16[16,2,128,128]{3,2,1,0:T(8,128)(2,1)S(1)}, u32[]{:S(2)}, u32[]{:S(2)}) %all-to-all-start) | async-done | bytes 1048608 | tf_op jit(solution)/shard_map/all_to_all | solution.py:403
  184.6 3.5 %collective-permute-done.27.refs_0_ = bf16[9,2,128,128]{3,2,1,0:T(8,128)(2,1)S(1)} collective-permute-done((bf16[9,2,128,128]{3,2,1,0:T(8,128)(2,1)}, bf16[9,2,128,128]{3,2,1,0:T(8,128)(2,1)S(1)}, u32[]{:S(2)}, u32[]{:S(2)}) %collective-permute-start.27) | collective-permute-done | bytes 589856 | tf_op jit(solution)/shard_map/ppermute | solution.py:45
  188.1 9.2 %collective-permute-done.30.refs_2_ = bf16[7,2,128,128]{3,2,1,0:T(8,128)(2,1)S(1)} collective-permute-done((bf16[7,2,128,128]{3,2,1,0:T(8,128)(2,1)}, bf16[7,2,128,128]{3,2,1,0:T(8,128)(2,1)S(1)}, u32[]{:S(2)}, u32[]{:S(2)}) %collective-permute-start.30) | collective-permute-done | bytes 458784 | tf_op jit(solution)/shard_map/ppermute | solution.py:45
  201.8 6.9 %all-to-all-start.1 = ((bf16[16,2,128,128]{3,2,1,0:T(8,128)(2,1)}), bf16[16,2,128,128]{3,2,1,0:T(8,128)(2,1)S(1)}, u32[]{:S(2)}, u32[]{:S(2)}) async-start(bf16[16,2,128,128]{3,2,1,0:T(8,128)(2,1)} %next_sums.1), calls=%async_computation.1 | async-start | bytes 2097152 | tf_op jit(solution)/shard_map/all_to_all | solution.py:403
  208.8 15.7 %all-to-all-done.1.other = bf16[16,2,128,128]{3,2,1,0:T(8,128)(2,1)S(1)} async-done(((bf16[16,2,128,128]{3,2,1,0:T(8,128)(2,1)}), bf16[16,2,128,128]{3,2,1,0:T(8,128)(2,1)S(1)}, u32[]{:S(2)}, u32[]{:S(2)}) %all-to-all-start.1) | async-done | bytes 1048608 | tf_op jit(solution)/shard_map/all_to_all | solution.py:403
  (148 shorter events, 68.9 us)
Async XLA Ops:
  24.5 47.4 %collective-permute-start.15 = (bf16[2,2,4,2,256,128]{5,4,3,2,1,0:T(8,128)(2,1)}, bf16[2,2,4,2,256,128]{5,4,3,2,1,0:T(8,128)(2,1)S(1)}, u32[]{:S(2)}, u32[]{:S(2)}) collective-permute-start(bf16[2,2,4,2,256,128]{5,4,3,2,1,0:T(8,128)(2,1)} %get-tuple-element.33), channel_id=1, source_target_pairs={{0,4},{1,5},{2,6},{3,7},{4,0},{5,1},{6,2},{7,3},{8,12},{9,13},{10,... | collective-permute-start | bytes 6291464 | tf_op jit(solution)/shard_map/ppermute | solution.py:45
  26.4 25.4 %collective-permute-start.8 = (bf16[2,4,2,256,128]{4,3,2,1,0:T(8,128)(2,1)S(1)}, bf16[2,4,2,256,128]{4,3,2,1,0:T(8,128)(2,1)S(1)}, u32[]{:S(2)}, u32[]{:S(2)}) collective-permute-start(bf16[2,4,2,256,128]{4,3,2,1,0:T(8,128)(2,1)S(1)} %get-tuple-element.27.refs_3_), channel_id=1, source_target_pairs={{0,1},{1,2},{2,3},{3,0},{4,5},{5,6},{6,7},{7,4},{8,9},{9,10},{10,1... | collective-permute-start | bytes 3145736 | tf_op jit(solution)/shard_map/ppermute | solution.py:45
  26.5 25.4 %collective-permute-start.7 = (bf16[2,4,2,256,128]{4,3,2,1,0:T(8,128)(2,1)S(1)}, bf16[2,4,2,256,128]{4,3,2,1,0:T(8,128)(2,1)S(1)}, u32[]{:S(2)}, u32[]{:S(2)}) collective-permute-start(bf16[2,4,2,256,128]{4,3,2,1,0:T(8,128)(2,1)S(1)} %get-tuple-element.27.refs_3_), channel_id=1, source_target_pairs={{0,3},{1,0},{2,1},{3,2},{4,7},{5,4},{6,5},{7,6},{8,11},{9,8},{10,9... | collective-permute-start | bytes 3145736 | tf_op jit(solution)/shard_map/ppermute | solution.py:45
  30.7 24.8 %collective-permute-start.10 = (bf16[2,4,2,256,128]{4,3,2,1,0:T(8,128)(2,1)S(1)}, bf16[2,4,2,256,128]{4,3,2,1,0:T(8,128)(2,1)S(1)}, u32[]{:S(2)}, u32[]{:S(2)}) collective-permute-start(bf16[2,4,2,256,128]{4,3,2,1,0:T(8,128)(2,1)S(1)} %get-tuple-element.28.refs_8_), channel_id=1, source_target_pairs={{0,8},{1,9},{2,10},{3,11},{4,12},{5,13},{6,14},{7,15},{8,16},{9,17... | collective-permute-start | bytes 3145736 | tf_op jit(solution)/shard_map/ppermute | solution.py:45
  32.2 23.4 %collective-permute-start.9 = (bf16[2,4,2,256,128]{4,3,2,1,0:T(8,128)(2,1)S(1)}, bf16[2,4,2,256,128]{4,3,2,1,0:T(8,128)(2,1)S(1)}, u32[]{:S(2)}, u32[]{:S(2)}) collective-permute-start(bf16[2,4,2,256,128]{4,3,2,1,0:T(8,128)(2,1)S(1)} %get-tuple-element.28.refs_8_), channel_id=1, source_target_pairs={{0,24},{1,25},{2,26},{3,27},{4,28},{5,29},{6,30},{7,31},{8,0},{9,1... | collective-permute-start | bytes 3145736 | tf_op jit(solution)/shard_map/ppermute | solution.py:45
  57.5 17.3 %collective-permute-start.11 = (bf16[4,2,256,128]{3,2,1,0:T(8,128)(2,1)}, bf16[4,2,256,128]{3,2,1,0:T(8,128)(2,1)S(1)}, u32[]{:S(2)}, u32[]{:S(2)}) collective-permute-start(bf16[4,2,256,128]{3,2,1,0:T(8,128)(2,1)} %get-tuple-element.29), channel_id=1, source_target_pairs={{0,1},{1,2},{2,3},{3,0},{4,5},{5,6},{6,7},{7,4},{8,9},{9,10},{10,1... | collective-permute-start | bytes 1572872 | tf_op jit(solution)/shard_map/ppermute | solution.py:45
  57.5 19.2 %collective-permute-start.12 = (bf16[4,2,256,128]{3,2,1,0:T(8,128)(2,1)}, bf16[4,2,256,128]{3,2,1,0:T(8,128)(2,1)S(1)}, u32[]{:S(2)}, u32[]{:S(2)}) collective-permute-start(bf16[4,2,256,128]{3,2,1,0:T(8,128)(2,1)} %get-tuple-element.30), channel_id=1, source_target_pairs={{0,3},{1,0},{2,1},{3,2},{4,7},{5,4},{6,5},{7,6},{8,11},{9,8},{10,9... | collective-permute-start | bytes 1572872 | tf_op jit(solution)/shard_map/ppermute | solution.py:45
  60.8 16.7 %collective-permute-start.13 = (bf16[4,2,256,128]{3,2,1,0:T(8,128)(2,1)}, bf16[4,2,256,128]{3,2,1,0:T(8,128)(2,1)}, u32[]{:S(2)}, u32[]{:S(2)}) collective-permute-start(bf16[4,2,256,128]{3,2,1,0:T(8,128)(2,1)} %get-tuple-element.31), channel_id=1, source_target_pairs={{0,8},{1,9},{2,10},{3,11},{4,12},{5,13},{6,14},{7,15},{8,16},{9,17... | collective-permute-start | bytes 1572872 | tf_op jit(solution)/shard_map/ppermute | solution.py:45
  61.0 20.5 %collective-permute-start.14 = (bf16[4,2,256,128]{3,2,1,0:T(8,128)(2,1)}, bf16[4,2,256,128]{3,2,1,0:T(8,128)(2,1)}, u32[]{:S(2)}, u32[]{:S(2)}) collective-permute-start(bf16[4,2,256,128]{3,2,1,0:T(8,128)(2,1)} %get-tuple-element.32), channel_id=1, source_target_pairs={{0,24},{1,25},{2,26},{3,27},{4,28},{5,29},{6,30},{7,31},{8,0},{9,1... | collective-permute-start | bytes 1572872 | tf_op jit(solution)/shard_map/ppermute | solution.py:45
  73.4 33.7 %collective-permute-start.19 = (bf16[2,4,2,256,128]{4,3,2,1,0:T(8,128)(2,1)}, bf16[2,4,2,256,128]{4,3,2,1,0:T(8,128)(2,1)}, u32[]{:S(2)}, u32[]{:S(2)}) collective-permute-start(bf16[2,4,2,256,128]{4,3,2,1,0:T(8,128)(2,1)} %get-tuple-element.37.refs_6_.refs_8_), channel_id=1, source_target_pairs={{0,8},{1,9},{2,10},{3,11},{4,12},{5,13},{6,14},{7,15},{8,16},{9,17... | collective-permute-start | bytes 3145736 | tf_op jit(solution)/shard_map/ppermute | solution.py:45
  74.9 32.2 %collective-permute-start.18 = (bf16[2,4,2,256,128]{4,3,2,1,0:T(8,128)(2,1)}, bf16[2,4,2,256,128]{4,3,2,1,0:T(8,128)(2,1)}, u32[]{:S(2)}, u32[]{:S(2)}) collective-permute-start(bf16[2,4,2,256,128]{4,3,2,1,0:T(8,128)(2,1)} %get-tuple-element.37.refs_6_.refs_8_), channel_id=1, source_target_pairs={{0,24},{1,25},{2,26},{3,27},{4,28},{5,29},{6,30},{7,31},{8,0},{9,1... | collective-permute-start | bytes 3145736 | tf_op jit(solution)/shard_map/ppermute | solution.py:45
  77.5 29.6 %collective-permute-start.17 = (bf16[2,4,2,256,128]{4,3,2,1,0:T(8,128)(2,1)}, bf16[2,4,2,256,128]{4,3,2,1,0:T(8,128)(2,1)}, u32[]{:S(2)}, u32[]{:S(2)}) collective-permute-start(bf16[2,4,2,256,128]{4,3,2,1,0:T(8,128)(2,1)} %get-tuple-element.34.refs_13_.refs_3_), channel_id=1, source_target_pairs={{0,1},{1,2},{2,3},{3,0},{4,5},{5,6},{6,7},{7,4},{8,9},{9,10},{10,1... | collective-permute-start | bytes 3145736 | tf_op jit(solution)/shard_map/ppermute | solution.py:45
  77.5 29.6 %collective-permute-start.16 = (bf16[2,4,2,256,128]{4,3,2,1,0:T(8,128)(2,1)}, bf16[2,4,2,256,128]{4,3,2,1,0:T(8,128)(2,1)}, u32[]{:S(2)}, u32[]{:S(2)}) collective-permute-start(bf16[2,4,2,256,128]{4,3,2,1,0:T(8,128)(2,1)} %get-tuple-element.34.refs_13_.refs_3_), channel_id=1, source_target_pairs={{0,3},{1,0},{2,1},{3,2},{4,7},{5,4},{6,5},{7,6},{8,11},{9,8},{10,9... | collective-permute-start | bytes 3145736 | tf_op jit(solution)/shard_map/ppermute | solution.py:45
  122.0 33.8 %collective-permute-start.21 = (bf16[16,2,128,128]{3,2,1,0:T(8,128)(2,1)}, bf16[16,2,128,128]{3,2,1,0:T(8,128)(2,1)}, u32[]{:S(2)}, u32[]{:S(2)}) collective-permute-start(bf16[16,2,128,128]{3,2,1,0:T(8,128)(2,1)} %pair_sums.3.refs_9_), channel_id=1, source_target_pairs={{0,64},{32,96},{64,0},{96,32},{1,65},{33,97},{65,1},{97,33},{2,66}... | collective-permute-start | bytes 3145736 | tf_op jit(solution)/shard_map/ppermute | solution.py:454
  127.0 19.3 %collective-permute-start.23 = (bf16[4,2,256,128]{3,2,1,0:T(8,128)(2,1)S(1)}, bf16[4,2,256,128]{3,2,1,0:T(8,128)(2,1)S(1)}, u32[]{:S(2)}, u32[]{:S(2)}) collective-permute-start(bf16[4,2,256,128]{3,2,1,0:T(8,128)(2,1)S(1)} %get-tuple-element.38.refs_1_), channel_id=1, source_target_pairs={{0,3},{1,0},{2,1},{3,2},{4,7},{5,4},{6,5},{7,6},{8,11},{9,8},{10,9... | collective-permute-start | bytes 1572872 | tf_op jit(solution)/shard_map/ppermute | solution.py:45
  128.4 17.8 %collective-permute-start.22 = (bf16[4,2,256,128]{3,2,1,0:T(8,128)(2,1)}, bf16[4,2,256,128]{3,2,1,0:T(8,128)(2,1)S(1)}, u32[]{:S(2)}, u32[]{:S(2)}) collective-permute-start(bf16[4,2,256,128]{3,2,1,0:T(8,128)(2,1)} %copy-done.23), channel_id=1, source_target_pairs={{0,1},{1,2},{2,3},{3,0},{4,5},{5,6},{6,7},{7,4},{8,9},{9,10},{10,1... | collective-permute-start | bytes 1572872 | tf_op jit(solution)/shard_map/ppermute | solution.py:45
  129.0 17.2 %collective-permute-start.24 = (bf16[4,2,256,128]{3,2,1,0:T(8,128)(2,1)}, bf16[4,2,256,128]{3,2,1,0:T(8,128)(2,1)S(1)}, u32[]{:S(2)}, u32[]{:S(2)}) collective-permute-start(bf16[4,2,256,128]{3,2,1,0:T(8,128)(2,1)} %copy-done.22), channel_id=1, source_target_pairs={{0,8},{1,9},{2,10},{3,11},{4,12},{5,13},{6,14},{7,15},{8,16},{9,17... | collective-permute-start | bytes 1572872 | tf_op jit(solution)/shard_map/ppermute | solution.py:45
  156.9 16.9 %collective-permute-start.29 = (bf16[2,7,2,160,128]{4,3,2,1,0:T(8,128)(2,1)}, bf16[2,7,2,160,128]{4,3,2,1,0:T(8,128)(2,1)}, u32[]{:S(2)}, u32[]{:S(2)}) collective-permute-start(bf16[2,7,2,160,128]{4,3,2,1,0:T(8,128)(2,1)} %ordered.7), channel_id=1, source_target_pairs={{0,32},{32,0},{64,96},{96,64},{1,33},{33,1},{65,97},{97,65},{2,34}... | collective-permute-start | bytes 3440648 | tf_op jit(solution)/shard_map/ppermute | solution.py:448
  161.7 22.8 %all-to-all-start = ((bf16[16,2,128,128]{3,2,1,0:T(8,128)(2,1)}), bf16[16,2,128,128]{3,2,1,0:T(8,128)(2,1)S(1)}, u32[]{:S(2)}, u32[]{:S(2)}) async-start(bf16[16,2,128,128]{3,2,1,0:T(8,128)(2,1)} %copy-done), calls=%async_computation | async-start | bytes 2097152 | tf_op jit(solution)/shard_map/all_to_all | solution.py:403
  171.5 16.6 %collective-permute-start.27 = (bf16[9,2,128,128]{3,2,1,0:T(8,128)(2,1)}, bf16[9,2,128,128]{3,2,1,0:T(8,128)(2,1)S(1)}, u32[]{:S(2)}, u32[]{:S(2)}) collective-permute-start(bf16[9,2,128,128]{3,2,1,0:T(8,128)(2,1)} %get-tuple-element.45), channel_id=1, source_target_pairs={{0,4},{1,5},{2,6},{3,7},{4,0},{5,1},{6,2},{7,3},{8,12},{9,13},{10,... | collective-permute-start | bytes 1769480 | tf_op jit(solution)/shard_map/ppermute | solution.py:45
  173.8 26.2 %collective-permute-start.28 = (bf16[9,2,128,128]{3,2,1,0:T(8,128)(2,1)}, bf16[9,2,128,128]{3,2,1,0:T(8,128)(2,1)S(1)}, u32[]{:S(2)}, u32[]{:S(2)}) collective-permute-start(bf16[9,2,128,128]{3,2,1,0:T(8,128)(2,1)} %get-tuple-element.46), channel_id=1, source_target_pairs={{0,68},{1,69},{2,70},{3,71},{4,64},{5,65},{6,66},{7,67},{8,76},{9,... | collective-permute-start | bytes 1769480 | tf_op jit(solution)/shard_map/ppermute | solution.py:466
  176.9 20.5 %collective-permute-start.30 = (bf16[7,2,128,128]{3,2,1,0:T(8,128)(2,1)}, bf16[7,2,128,128]{3,2,1,0:T(8,128)(2,1)S(1)}, u32[]{:S(2)}, u32[]{:S(2)}) collective-permute-start(bf16[7,2,128,128]{3,2,1,0:T(8,128)(2,1)} %get-tuple-element.48), channel_id=1, source_target_pairs={{0,4},{1,5},{2,6},{3,7},{4,0},{5,1},{6,2},{7,3},{8,12},{9,13},{10,... | collective-permute-start | bytes 1376264 | tf_op jit(solution)/shard_map/ppermute | solution.py:45
  178.0 22.0 %collective-permute-start.31 = (bf16[7,2,128,128]{3,2,1,0:T(8,128)(2,1)}, bf16[7,2,128,128]{3,2,1,0:T(8,128)(2,1)S(1)}, u32[]{:S(2)}, u32[]{:S(2)}) collective-permute-start(bf16[7,2,128,128]{3,2,1,0:T(8,128)(2,1)} %get-tuple-element.49), channel_id=1, source_target_pairs={{0,68},{1,69},{2,70},{3,71},{4,64},{5,65},{6,66},{7,67},{8,76},{9,... | collective-permute-start | bytes 1376264 | tf_op jit(solution)/shard_map/ppermute | solution.py:466
  201.8 22.7 %all-to-all-start.1 = ((bf16[16,2,128,128]{3,2,1,0:T(8,128)(2,1)}), bf16[16,2,128,128]{3,2,1,0:T(8,128)(2,1)S(1)}, u32[]{:S(2)}, u32[]{:S(2)}) async-start(bf16[16,2,128,128]{3,2,1,0:T(8,128)(2,1)} %next_sums.1), calls=%async_computation.1 | async-start | bytes 2097152 | tf_op jit(solution)/shard_map/all_to_all | solution.py:403
  (40 other events, 258.0 us)

commit v4 on v2

--- a/solution.py
+++ b/solution.py
@@ -93,7 +93,7 @@
 CROSS = (2, 4, 2, 2 * B, B)
 
 
-def own_rings(factor):
+def own_rings(factor, after):
     parts = factor.reshape(2, 2, 2, 2 * B, B).transpose(1, 2, 0, 3, 4)
     arrays = [parts[0]] + [send(parts[0], dx=-d) for d in RING[1:]]
     arrays += [parts[1]] + [send(parts[1], dy=-d) for d in RING[1:]]
@@ -105,7 +105,7 @@
             lambda outs, s=side, at=at: outs[2].at[s, :, at],
         ]
         plan.append((lambda ins, n=n: ins[n], targets))
-    return copied("own_rings", plan, CROSS[:1] + CROSS[2:], arrays, [CROSS, CROSS, (2,) + CROSS])
+    return copied("own_rings", plan, CROSS[:1] + CROSS[2:], [*arrays, after], [CROSS, CROSS, (2,) + CROSS])
 
 
 def crossed(left, right):
@@ -420,7 +420,7 @@
         ]
     )[None]
     coef = jnp.concatenate([own_coef, lax.ppermute(own_coef, "pole", CORE)])
-    left, right, both = own_rings(factor_columns[0, 0])
+    left, right, both = own_rings(factor_columns[0, 0], coef)
     both = send(both, dz=1)
     left, right, _ = crossed(left, right)
     plan = [(lambda ins, n=n: ins[0].at[n], [lambda outs, n=n: outs[n]]) for n in range(2)]

time: 227 us -> 233 us (1.026)
  waiting for transfers between devices: 73.4 us -> 80.3 us
    ppermute x3, waiting for transfers between devices: 0.01 us -> 5.04 us  [swapped(): return lax.ppermute(ordered(give, *after), 'pole', CORE)]
  transfers between devices with their start and end apart: 34 -> 34, of which waited for: 15 -> 12; matrix products, arithmetic and copies ran while one was open for 3% -> 3% of each run, Pallas kernels for 26% -> 26%
where the time goes in v4:
time: 233 us
  waiting for transfers between devices  80.3 us (34%)
  Pallas kernels  72.2 us (31%)
  starting transfers between devices  59.3 us (25%)
  local copies, waits for them, and re-layouts  11.4 us (5%)
  between operations  6.21 us (3%)
  other arithmetic  3.28 us (1%)
    ppermute x25, waiting for transfers between devices, send(): return lax.ppermute(value, 'snode', shift(**by))  52.5 us
    pallas_call x3, Pallas kernels, columns_of(): pl.pallas_call(lambda *refs: column_body(places, with_own, *refs), out_sh...  47 us
    ppermute x25, starting transfers between devices, send(): return lax.ppermute(value, 'snode', shift(**by))  41.8 us
    all_to_all x2, waiting for transfers between devices, in_plane(): lax.all_to_all(value, 'snode', split_axis=0, concat_axis=0, axis_index_gr...  21.1 us
    all_to_all x2, starting transfers between devices, in_plane(): lax.all_to_all(value, 'snode', split_axis=0, concat_axis=0, axis_index_gr...  10.6 us
    pallas_call x3, Pallas kernels, pair_sums(): pl.pallas_call(lambda *refs: pair_body(parts, *refs), out_shape=[jax.Shap...  10.6 us
    unnamed x57, local copies, waits for them, and re-layouts  7.2 us
    pallas_call x4, Pallas kernels, copied(): pl.pallas_call(lambda *refs: copies_body(plan, len(arrays), len(shapes),...  6.69 us
  transfers between devices with their start and end apart: 34, of which 12 were waited for; matrix products, arithmetic and copies ran while one was open for 3% of the time, Pallas kernels for 26%

profile of v4, /device:TPU:0, one launch (start us, length us, event | category | flops | bytes accessed | tf_op | source)
XLA Modules:
  0.0 232.6 jit_solution(7526268514941283079)
XLA Ops:
  1.8 3.4 %collective-permute-start.6 = (bf16[2,2,256,128]{3,2,1,0:T(8,128)(2,1)S(1)}, bf16[2,2,256,128]{3,2,1,0:T(8,128)(2,1)S(1)}, u32[]{:S(2)}, u32[]{:S(2)}) collective-permute-start(bf16[2,2,256,128]{3,2,1,0:T(8,128)(2,1)S(1)} %get-tuple-element.56.refs_4_), channel_id=1, source_target_pairs={{0,2},{1,3},{2,0},{3,1},{4,6},{5,7},{6,4},{7,5},{8,10},{9,11},{10,... | collective-permute-start | bytes 786440 | tf_op jit(solution)/shard_map/ppermute | solution.py:45
  15.5 3.1 %collective-permute-start.3 = (bf16[2,2,256,128]{3,2,1,0:T(8,128)(2,1)S(1)}, bf16[2,2,256,128]{3,2,1,0:T(8,128)(2,1)S(1)}, u32[]{:S(2)}, u32[]{:S(2)}) collective-permute-start(bf16[2,2,256,128]{3,2,1,0:T(8,128)(2,1)S(1)} %get-tuple-element.57.refs_0_), channel_id=1, source_target_pairs={{0,16},{1,17},{2,18},{3,19},{4,20},{5,21},{6,22},{7,23},{8,24},{9,... | collective-permute-start | bytes 786440 | tf_op jit(solution)/shard_map/ppermute | solution.py:45
  21.9 4.4 %collective-permute-done.3.refs_3_ = bf16[2,2,256,128]{3,2,1,0:T(8,128)(2,1)S(1)} collective-permute-done((bf16[2,2,256,128]{3,2,1,0:T(8,128)(2,1)S(1)}, bf16[2,2,256,128]{3,2,1,0:T(8,128)(2,1)S(1)}, u32[]{:S(2)}, u32[]{:S(2)}) %collective-permute-start.3) | collective-permute-done | bytes 262176 | tf_op jit(solution)/shard_map/ppermute | solution.py:45
  26.3 5.1 %collective-permute-done.2.refs_2_ = bf16[2,2,256,128]{3,2,1,0:T(8,128)(2,1)S(1)} collective-permute-done((bf16[2,2,256,128]{3,2,1,0:T(8,128)(2,1)S(1)}, bf16[2,2,256,128]{3,2,1,0:T(8,128)(2,1)S(1)}, u32[]{:S(2)}, u32[]{:S(2)}) %collective-permute-start.2) | collective-permute-done | bytes 262176 | tf_op jit(solution)/shard_map/ppermute | solution.py:45
  35.2 3.2 %collective-permute-start.7 = (bf16[2,4,2,256,128]{4,3,2,1,0:T(8,128)(2,1)S(1)}, bf16[2,4,2,256,128]{4,3,2,1,0:T(8,128)(2,1)S(1)}, u32[]{:S(2)}, u32[]{:S(2)}) collective-permute-start(bf16[2,4,2,256,128]{4,3,2,1,0:T(8,128)(2,1)S(1)} %get-tuple-element.27.refs_3_), channel_id=1, source_target_pairs={{0,3},{1,0},{2,1},{3,2},{4,7},{5,4},{6,5},{7,6},{8,11},{9,8},{10,9... | collective-permute-start | bytes 3145736 | tf_op jit(solution)/shard_map/ppermute | solution.py:45
  41.7 19.4 %collective-permute-done.8.refs_1_.refs_5_ = bf16[2,4,2,256,128]{4,3,2,1,0:T(8,128)(2,1)S(1)} collective-permute-done((bf16[2,4,2,256,128]{4,3,2,1,0:T(8,128)(2,1)S(1)}, bf16[2,4,2,256,128]{4,3,2,1,0:T(8,128)(2,1)S(1)}, u32[]{:S(2)}, u32[]{:S(2)}) %collective-permute-start.8) | collective-permute-done | bytes 1048608 | tf_op jit(solution)/shard_map/ppermute | solution.py:45
  65.7 3.2 %collective-permute-start.12 = (bf16[4,2,256,128]{3,2,1,0:T(8,128)(2,1)}, bf16[4,2,256,128]{3,2,1,0:T(8,128)(2,1)}, u32[]{:S(2)}, u32[]{:S(2)}) collective-permute-start(bf16[4,2,256,128]{3,2,1,0:T(8,128)(2,1)} %get-tuple-element.30), channel_id=1, source_target_pairs={{0,3},{1,0},{2,1},{3,2},{4,7},{5,4},{6,5},{7,6},{8,11},{9,8},{10,9... | collective-permute-start | bytes 1572872 | tf_op jit(solution)/shard_map/ppermute | solution.py:45
  72.4 8.7 %collective-permute-done.15.refs_0_ = bf16[2,2,4,2,256,128]{5,4,3,2,1,0:T(8,128)(2,1)S(1)} collective-permute-done((bf16[2,2,4,2,256,128]{5,4,3,2,1,0:T(8,128)(2,1)}, bf16[2,2,4,2,256,128]{5,4,3,2,1,0:T(8,128)(2,1)S(1)}, u32[]{:S(2)}, u32[]{:S(2)}) %collective-permute-start.15) | collective-permute-done | bytes 2097184 | tf_op jit(solution)/shard_map/ppermute | solution.py:45
  85.7 3.2 %collective-permute-start.16 = (bf16[2,4,2,256,128]{4,3,2,1,0:T(8,128)(2,1)S(1)}, bf16[2,4,2,256,128]{4,3,2,1,0:T(8,128)(2,1)}, u32[]{:S(2)}, u32[]{:S(2)}) collective-permute-start(bf16[2,4,2,256,128]{4,3,2,1,0:T(8,128)(2,1)S(1)} %get-tuple-element.34.refs_13_.refs_3_), channel_id=1, source_target_pairs={{0,3},{1,0},{2,1},{3,2},{4,7},{5,4},{6,5},{7,6},{8,11},{9,8},{10,9... | collective-permute-start | bytes 3145736 | tf_op jit(solution)/shard_map/ppermute | solution.py:45
  90.2 21.5 %columns.3 = (bf16[2,16,2,160,128]{4,3,2,1,0:T(8,128)(2,1)}, bf16[2,16,2,160,128]{4,3,2,1,0:T(8,128)(2,1)}) custom-call(s32[162]{0:T(256)} %pad_add_fusion.refs_0_, bf16[1,2,96,384,128]{4,3,2,1,0:T(8,128)(2,1)} %refs_1_.5, bf16[2,128,128]{2,1,0:T(8,128)(2,1)} %bitcast.80, bf16[2,4,2,256,128]{4,3,2,1,0:T(8,128)(2,1)} %copy-done.14, ...), custom_call_target="tpu_custom_call" | custom-call | flops 6442450944 | bytes 33554432 | tf_op jit(solution)/shard_map/columns/pallas_call | solution.py:257
  115.5 5.0 %collective-permute-done.20.refs_2_.other = bf16[2,16,2,160,128]{4,3,2,1,0:T(8,128)(2,1)} collective-permute-done((bf16[2,16,2,160,128]{4,3,2,1,0:T(8,128)(2,1)}, bf16[2,16,2,160,128]{4,3,2,1,0:T(8,128)(2,1)}, u32[]{:S(2)}, u32[]{:S(2)}) %collective-permute-start.20) | collective-permute-done | bytes 2621472 | tf_op jit(solution)/shard_map/ppermute | solution.py:448
  120.6 3.9 %pair_sums.3.refs_9_ = bf16[16,2,128,128]{3,2,1,0:T(8,128)(2,1)} custom-call(f32[2,4]{1,0:T(2,128)S(1)} %pad_maximum_fusion.refs_8_.refs_0_.coef, bf16[2,16,2,160,128]{4,3,2,1,0:T(8,128)(2,1)S(1)} %copy-done, bf16[2,16,2,160,128]{4,3,2,1,0:T(8,128)(2,1)} %collective-permute-done.20.refs_2_.other), custom_call_target="tpu_custom_call" | custom-call | bytes 1 | tf_op jit(solution)/shard_map/pair_sums/pallas_call | solution.py:311
  124.5 3.7 %collective-permute-start.21 = (bf16[16,2,128,128]{3,2,1,0:T(8,128)(2,1)}, bf16[16,2,128,128]{3,2,1,0:T(8,128)(2,1)}, u32[]{:S(2)}, u32[]{:S(2)}) collective-permute-start(bf16[16,2,128,128]{3,2,1,0:T(8,128)(2,1)} %pair_sums.3.refs_9_), channel_id=1, source_target_pairs={{0,64},{32,96},{64,0},{96,32},{1,65},{33,97},{65,1},{97,33},{2,66}... | collective-permute-start | bytes 3145736 | tf_op jit(solution)/shard_map/ppermute | solution.py:454
  131.6 3.2 %collective-permute-start.25 = (bf16[4,2,256,128]{3,2,1,0:T(8,128)(2,1)}, bf16[4,2,256,128]{3,2,1,0:T(8,128)(2,1)}, u32[]{:S(2)}, u32[]{:S(2)}) collective-permute-start(bf16[4,2,256,128]{3,2,1,0:T(8,128)(2,1)} %copy-done.18), channel_id=1, source_target_pairs={{0,24},{1,25},{2,26},{3,27},{4,28},{5,29},{6,30},{7,31},{8,0},{9,1... | collective-permute-start | bytes 1572872 | tf_op jit(solution)/shard_map/ppermute | solution.py:45
  136.0 14.0 %columns.4 = (bf16[2,9,2,160,128]{4,3,2,1,0:T(8,128)(2,1)}, bf16[2,9,2,160,128]{4,3,2,1,0:T(8,128)(2,1)}) custom-call(s32[92]{0:T(128)} %pad_add_fusion.2.refs_0_, bf16[1,2,96,384,128]{4,3,2,1,0:T(8,128)(2,1)} %refs_1_.5, bf16[2,128,128]{2,1,0:T(8,128)(2,1)} %bitcast.81, bf16[2,4,2,256,128]{4,3,2,1,0:T(8,128)(2,1)} %copy-done.1, ...), custom_call_target="tpu_custom_call" | custom-call | flops 3623878656 | bytes 18874368 | tf_op jit(solution)/shard_map/columns/pallas_call | solution.py:257
  150.8 11.5 %columns.5 = (bf16[2,7,2,160,128]{4,3,2,1,0:T(8,128)(2,1)}, bf16[2,7,2,160,128]{4,3,2,1,0:T(8,128)(2,1)}) custom-call(s32[72]{0:T(128)} %pad_add_fusion.3.refs_0_, bf16[1,2,96,384,128]{4,3,2,1,0:T(8,128)(2,1)} %refs_1_.5, bf16[2,128,128]{2,1,0:T(8,128)(2,1)} %bitcast.82, bf16[2,4,2,256,128]{4,3,2,1,0:T(8,128)(2,1)} %copy-done.1, ...), custom_call_target="tpu_custom_call" | custom-call | flops 2818572288 | bytes 14680064 | tf_op jit(solution)/shard_map/columns/pallas_call | solution.py:257
  165.4 3.3 %own_sums.1.refs_3_ = bf16[16,2,128,128]{3,2,1,0:T(8,128)(2,1)S(1)} custom-call(f32[2,4]{1,0:T(2,128)S(1)} %pad_maximum_fusion.refs_8_.refs_0_.coef, s32[16]{0:T(128)S(1)} %stack.222.order, bf16[2,16,2,160,128]{4,3,2,1,0:T(8,128)(2,1)S(1)} %copy-done, bf16[2,16,2,160,128]{4,3,2,1,0:T(8,128)(2,1)} %collective-permute-done.20.refs_2_.other, ...), custom_call_target="tpu_custom_call" | custom-call | bytes 1 | tf_op jit(solution)/shard_map/own_sums/pallas_call | solution.py:337
  169.7 3.8 %all-to-all-start = ((bf16[16,2,128,128]{3,2,1,0:T(8,128)(2,1)}), bf16[16,2,128,128]{3,2,1,0:T(8,128)(2,1)S(1)}, u32[]{:S(2)}, u32[]{:S(2)}) async-start(bf16[16,2,128,128]{3,2,1,0:T(8,128)(2,1)} %copy-done.4), calls=%async_computation | async-start | bytes 2097152 | tf_op jit(solution)/shard_map/all_to_all | solution.py:403
  174.8 3.6 %pair_sums.4 = (bf16[9,2,128,128]{3,2,1,0:T(8,128)(2,1)}, bf16[9,2,128,128]{3,2,1,0:T(8,128)(2,1)}) custom-call(f32[2,4]{1,0:T(2,128)S(1)} %pad_maximum_fusion.refs_8_.refs_0_.coef, bf16[2,9,2,160,128]{4,3,2,1,0:T(8,128)(2,1)S(1)} %copy-done.12, bf16[2,9,2,160,128]{4,3,2,1,0:T(8,128)(2,1)} %collective-permute-done.26.refs_2_, ...), custom_call_target="tpu_custom_call" | custom-call | bytes 1 | tf_op jit(solution)/shard_map/pair_sums/pallas_call | solution.py:311
  186.2 5.4 %all-to-all-done.refs_1_.own = bf16[16,2,128,128]{3,2,1,0:T(8,128)(2,1)S(1)} async-done(((bf16[16,2,128,128]{3,2,1,0:T(8,128)(2,1)}), bf16[16,2,128,128]{3,2,1,0:T(8,128)(2,1)S(1)}, u32[]{:S(2)}, u32[]{:S(2)}) %all-to-all-start) | async-done | bytes 1048608 | tf_op jit(solution)/shard_map/all_to_all | solution.py:403
  191.7 3.2 %collective-permute-done.27.refs_0_ = bf16[9,2,128,128]{3,2,1,0:T(8,128)(2,1)S(1)} collective-permute-done((bf16[9,2,128,128]{3,2,1,0:T(8,128)(2,1)}, bf16[9,2,128,128]{3,2,1,0:T(8,128)(2,1)S(1)}, u32[]{:S(2)}, u32[]{:S(2)}) %collective-permute-start.27) | collective-permute-done | bytes 589856 | tf_op jit(solution)/shard_map/ppermute | solution.py:45
  194.8 8.9 %collective-permute-done.30.refs_2_ = bf16[7,2,128,128]{3,2,1,0:T(8,128)(2,1)S(1)} collective-permute-done((bf16[7,2,128,128]{3,2,1,0:T(8,128)(2,1)}, bf16[7,2,128,128]{3,2,1,0:T(8,128)(2,1)S(1)}, u32[]{:S(2)}, u32[]{:S(2)}) %collective-permute-start.30) | collective-permute-done | bytes 458784 | tf_op jit(solution)/shard_map/ppermute | solution.py:45
  207.1 6.9 %all-to-all-start.1 = ((bf16[16,2,128,128]{3,2,1,0:T(8,128)(2,1)}), bf16[16,2,128,128]{3,2,1,0:T(8,128)(2,1)S(1)}, u32[]{:S(2)}, u32[]{:S(2)}) async-start(bf16[16,2,128,128]{3,2,1,0:T(8,128)(2,1)} %next_sums.1), calls=%async_computation.1 | async-start | bytes 2097152 | tf_op jit(solution)/shard_map/all_to_all | solution.py:403
  214.1 15.7 %all-to-all-done.1.other = bf16[16,2,128,128]{3,2,1,0:T(8,128)(2,1)S(1)} async-done(((bf16[16,2,128,128]{3,2,1,0:T(8,128)(2,1)}), bf16[16,2,128,128]{3,2,1,0:T(8,128)(2,1)S(1)}, u32[]{:S(2)}, u32[]{:S(2)}) %all-to-all-start.1) | async-done | bytes 1048608 | tf_op jit(solution)/shard_map/all_to_all | solution.py:403
  (144 shorter events, 59.1 us)
Async XLA Ops:
  1.8 17.4 %collective-permute-start.6 = (bf16[2,2,256,128]{3,2,1,0:T(8,128)(2,1)S(1)}, bf16[2,2,256,128]{3,2,1,0:T(8,128)(2,1)S(1)}, u32[]{:S(2)}, u32[]{:S(2)}) collective-permute-start(bf16[2,2,256,128]{3,2,1,0:T(8,128)(2,1)S(1)} %get-tuple-element.56.refs_4_), channel_id=1, source_target_pairs={{0,2},{1,3},{2,0},{3,1},{4,6},{5,7},{6,4},{7,5},{8,10},{9,11},{10,... | collective-permute-start | bytes 786440 | tf_op jit(solution)/shard_map/ppermute | solution.py:45
  5.1 16.7 %collective-permute-start.5 = (bf16[2,2,256,128]{3,2,1,0:T(8,128)(2,1)S(1)}, bf16[2,2,256,128]{3,2,1,0:T(8,128)(2,1)S(1)}, u32[]{:S(2)}, u32[]{:S(2)}) collective-permute-start(bf16[2,2,256,128]{3,2,1,0:T(8,128)(2,1)S(1)} %get-tuple-element.56.refs_4_), channel_id=1, source_target_pairs={{0,1},{1,2},{2,3},{3,0},{4,5},{5,6},{6,7},{7,4},{8,9},{9,10},{10,1... | collective-permute-start | bytes 786440 | tf_op jit(solution)/shard_map/ppermute | solution.py:45
  33.2 47.9 %collective-permute-start.15 = (bf16[2,2,4,2,256,128]{5,4,3,2,1,0:T(8,128)(2,1)}, bf16[2,2,4,2,256,128]{5,4,3,2,1,0:T(8,128)(2,1)S(1)}, u32[]{:S(2)}, u32[]{:S(2)}) collective-permute-start(bf16[2,2,4,2,256,128]{5,4,3,2,1,0:T(8,128)(2,1)} %get-tuple-element.33), channel_id=1, source_target_pairs={{0,4},{1,5},{2,6},{3,7},{4,0},{5,1},{6,2},{7,3},{8,12},{9,13},{10,... | collective-permute-start | bytes 6291464 | tf_op jit(solution)/shard_map/ppermute | solution.py:45
  35.2 25.9 %collective-permute-start.8 = (bf16[2,4,2,256,128]{4,3,2,1,0:T(8,128)(2,1)S(1)}, bf16[2,4,2,256,128]{4,3,2,1,0:T(8,128)(2,1)S(1)}, u32[]{:S(2)}, u32[]{:S(2)}) collective-permute-start(bf16[2,4,2,256,128]{4,3,2,1,0:T(8,128)(2,1)S(1)} %get-tuple-element.27.refs_3_), channel_id=1, source_target_pairs={{0,1},{1,2},{2,3},{3,0},{4,5},{5,6},{6,7},{7,4},{8,9},{9,10},{10,1... | collective-permute-start | bytes 3145736 | tf_op jit(solution)/shard_map/ppermute | solution.py:45
  35.2 25.9 %collective-permute-start.7 = (bf16[2,4,2,256,128]{4,3,2,1,0:T(8,128)(2,1)S(1)}, bf16[2,4,2,256,128]{4,3,2,1,0:T(8,128)(2,1)S(1)}, u32[]{:S(2)}, u32[]{:S(2)}) collective-permute-start(bf16[2,4,2,256,128]{4,3,2,1,0:T(8,128)(2,1)S(1)} %get-tuple-element.27.refs_3_), channel_id=1, source_target_pairs={{0,3},{1,0},{2,1},{3,2},{4,7},{5,4},{6,5},{7,6},{8,11},{9,8},{10,9... | collective-permute-start | bytes 3145736 | tf_op jit(solution)/shard_map/ppermute | solution.py:45
  38.4 25.3 %collective-permute-start.10 = (bf16[2,4,2,256,128]{4,3,2,1,0:T(8,128)(2,1)S(1)}, bf16[2,4,2,256,128]{4,3,2,1,0:T(8,128)(2,1)S(1)}, u32[]{:S(2)}, u32[]{:S(2)}) collective-permute-start(bf16[2,4,2,256,128]{4,3,2,1,0:T(8,128)(2,1)S(1)} %get-tuple-element.28.refs_8_), channel_id=1, source_target_pairs={{0,8},{1,9},{2,10},{3,11},{4,12},{5,13},{6,14},{7,15},{8,16},{9,17... | collective-permute-start | bytes 3145736 | tf_op jit(solution)/shard_map/ppermute | solution.py:45
  39.9 23.9 %collective-permute-start.9 = (bf16[2,4,2,256,128]{4,3,2,1,0:T(8,128)(2,1)S(1)}, bf16[2,4,2,256,128]{4,3,2,1,0:T(8,128)(2,1)S(1)}, u32[]{:S(2)}, u32[]{:S(2)}) collective-permute-start(bf16[2,4,2,256,128]{4,3,2,1,0:T(8,128)(2,1)S(1)} %get-tuple-element.28.refs_8_), channel_id=1, source_target_pairs={{0,24},{1,25},{2,26},{3,27},{4,28},{5,29},{6,30},{7,31},{8,0},{9,1... | collective-permute-start | bytes 3145736 | tf_op jit(solution)/shard_map/ppermute | solution.py:45
  65.7 18.2 %collective-permute-start.11 = (bf16[4,2,256,128]{3,2,1,0:T(8,128)(2,1)}, bf16[4,2,256,128]{3,2,1,0:T(8,128)(2,1)}, u32[]{:S(2)}, u32[]{:S(2)}) collective-permute-start(bf16[4,2,256,128]{3,2,1,0:T(8,128)(2,1)} %get-tuple-element.29), channel_id=1, source_target_pairs={{0,1},{1,2},{2,3},{3,0},{4,5},{5,6},{6,7},{7,4},{8,9},{9,10},{10,1... | collective-permute-start | bytes 1572872 | tf_op jit(solution)/shard_map/ppermute | solution.py:45
  65.7 19.9 %collective-permute-start.12 = (bf16[4,2,256,128]{3,2,1,0:T(8,128)(2,1)}, bf16[4,2,256,128]{3,2,1,0:T(8,128)(2,1)}, u32[]{:S(2)}, u32[]{:S(2)}) collective-permute-start(bf16[4,2,256,128]{3,2,1,0:T(8,128)(2,1)} %get-tuple-element.30), channel_id=1, source_target_pairs={{0,3},{1,0},{2,1},{3,2},{4,7},{5,4},{6,5},{7,6},{8,11},{9,8},{10,9... | collective-permute-start | bytes 1572872 | tf_op jit(solution)/shard_map/ppermute | solution.py:45
  69.7 20.5 %collective-permute-start.14 = (bf16[4,2,256,128]{3,2,1,0:T(8,128)(2,1)}, bf16[4,2,256,128]{3,2,1,0:T(8,128)(2,1)}, u32[]{:S(2)}, u32[]{:S(2)}) collective-permute-start(bf16[4,2,256,128]{3,2,1,0:T(8,128)(2,1)} %get-tuple-element.32), channel_id=1, source_target_pairs={{0,24},{1,25},{2,26},{3,27},{4,28},{5,29},{6,30},{7,31},{8,0},{9,1... | collective-permute-start | bytes 1572872 | tf_op jit(solution)/shard_map/ppermute | solution.py:45
  82.4 29.4 %collective-permute-start.19 = (bf16[2,4,2,256,128]{4,3,2,1,0:T(8,128)(2,1)}, bf16[2,4,2,256,128]{4,3,2,1,0:T(8,128)(2,1)S(1)}, u32[]{:S(2)}, u32[]{:S(2)}) collective-permute-start(bf16[2,4,2,256,128]{4,3,2,1,0:T(8,128)(2,1)} %get-tuple-element.37.refs_6_.refs_8_), channel_id=1, source_target_pairs={{0,8},{1,9},{2,10},{3,11},{4,12},{5,13},{6,14},{7,15},{8,16},{9,17... | collective-permute-start | bytes 3145736 | tf_op jit(solution)/shard_map/ppermute | solution.py:45
  83.9 27.9 %collective-permute-start.18 = (bf16[2,4,2,256,128]{4,3,2,1,0:T(8,128)(2,1)}, bf16[2,4,2,256,128]{4,3,2,1,0:T(8,128)(2,1)S(1)}, u32[]{:S(2)}, u32[]{:S(2)}) collective-permute-start(bf16[2,4,2,256,128]{4,3,2,1,0:T(8,128)(2,1)} %get-tuple-element.37.refs_6_.refs_8_), channel_id=1, source_target_pairs={{0,24},{1,25},{2,26},{3,27},{4,28},{5,29},{6,30},{7,31},{8,0},{9,1... | collective-permute-start | bytes 3145736 | tf_op jit(solution)/shard_map/ppermute | solution.py:45
  85.7 26.1 %collective-permute-start.17 = (bf16[2,4,2,256,128]{4,3,2,1,0:T(8,128)(2,1)S(1)}, bf16[2,4,2,256,128]{4,3,2,1,0:T(8,128)(2,1)}, u32[]{:S(2)}, u32[]{:S(2)}) collective-permute-start(bf16[2,4,2,256,128]{4,3,2,1,0:T(8,128)(2,1)S(1)} %get-tuple-element.34.refs_13_.refs_3_), channel_id=1, source_target_pairs={{0,1},{1,2},{2,3},{3,0},{4,5},{5,6},{6,7},{7,4},{8,9},{9,10},{10,1... | collective-permute-start | bytes 3145736 | tf_op jit(solution)/shard_map/ppermute | solution.py:45
  85.7 26.1 %collective-permute-start.16 = (bf16[2,4,2,256,128]{4,3,2,1,0:T(8,128)(2,1)S(1)}, bf16[2,4,2,256,128]{4,3,2,1,0:T(8,128)(2,1)}, u32[]{:S(2)}, u32[]{:S(2)}) collective-permute-start(bf16[2,4,2,256,128]{4,3,2,1,0:T(8,128)(2,1)S(1)} %get-tuple-element.34.refs_13_.refs_3_), channel_id=1, source_target_pairs={{0,3},{1,0},{2,1},{3,2},{4,7},{5,4},{6,5},{7,6},{8,11},{9,8},{10,9... | collective-permute-start | bytes 3145736 | tf_op jit(solution)/shard_map/ppermute | solution.py:45
  124.5 37.9 %collective-permute-start.21 = (bf16[16,2,128,128]{3,2,1,0:T(8,128)(2,1)}, bf16[16,2,128,128]{3,2,1,0:T(8,128)(2,1)}, u32[]{:S(2)}, u32[]{:S(2)}) collective-permute-start(bf16[16,2,128,128]{3,2,1,0:T(8,128)(2,1)} %pair_sums.3.refs_9_), channel_id=1, source_target_pairs={{0,64},{32,96},{64,0},{96,32},{1,65},{33,97},{65,1},{97,33},{2,66}... | collective-permute-start | bytes 3145736 | tf_op jit(solution)/shard_map/ppermute | solution.py:454
  129.5 20.6 %collective-permute-start.23 = (bf16[4,2,256,128]{3,2,1,0:T(8,128)(2,1)S(1)}, bf16[4,2,256,128]{3,2,1,0:T(8,128)(2,1)S(1)}, u32[]{:S(2)}, u32[]{:S(2)}) collective-permute-start(bf16[4,2,256,128]{3,2,1,0:T(8,128)(2,1)S(1)} %copy-done.17), channel_id=1, source_target_pairs={{0,3},{1,0},{2,1},{3,2},{4,7},{5,4},{6,5},{7,6},{8,11},{9,8},{10,9... | collective-permute-start | bytes 1572872 | tf_op jit(solution)/shard_map/ppermute | solution.py:45
  130.6 19.4 %collective-permute-start.22 = (bf16[4,2,256,128]{3,2,1,0:T(8,128)(2,1)}, bf16[4,2,256,128]{3,2,1,0:T(8,128)(2,1)}, u32[]{:S(2)}, u32[]{:S(2)}) collective-permute-start(bf16[4,2,256,128]{3,2,1,0:T(8,128)(2,1)} %copy-done.20), channel_id=1, source_target_pairs={{0,1},{1,2},{2,3},{3,0},{4,5},{5,6},{6,7},{7,4},{8,9},{9,10},{10,1... | collective-permute-start | bytes 1572872 | tf_op jit(solution)/shard_map/ppermute | solution.py:45
  131.6 18.4 %collective-permute-start.24 = (bf16[4,2,256,128]{3,2,1,0:T(8,128)(2,1)}, bf16[4,2,256,128]{3,2,1,0:T(8,128)(2,1)}, u32[]{:S(2)}, u32[]{:S(2)}) collective-permute-start(bf16[4,2,256,128]{3,2,1,0:T(8,128)(2,1)} %copy-done.19), channel_id=1, source_target_pairs={{0,8},{1,9},{2,10},{3,11},{4,12},{5,13},{6,14},{7,15},{8,16},{9,17... | collective-permute-start | bytes 1572872 | tf_op jit(solution)/shard_map/ppermute | solution.py:45
  131.6 18.4 %collective-permute-start.25 = (bf16[4,2,256,128]{3,2,1,0:T(8,128)(2,1)}, bf16[4,2,256,128]{3,2,1,0:T(8,128)(2,1)}, u32[]{:S(2)}, u32[]{:S(2)}) collective-permute-start(bf16[4,2,256,128]{3,2,1,0:T(8,128)(2,1)} %copy-done.18), channel_id=1, source_target_pairs={{0,24},{1,25},{2,26},{3,27},{4,28},{5,29},{6,30},{7,31},{8,0},{9,1... | collective-permute-start | bytes 1572872 | tf_op jit(solution)/shard_map/ppermute | solution.py:45
  169.7 22.0 %all-to-all-start = ((bf16[16,2,128,128]{3,2,1,0:T(8,128)(2,1)}), bf16[16,2,128,128]{3,2,1,0:T(8,128)(2,1)S(1)}, u32[]{:S(2)}, u32[]{:S(2)}) async-start(bf16[16,2,128,128]{3,2,1,0:T(8,128)(2,1)} %copy-done.4), calls=%async_computation | async-start | bytes 2097152 | tf_op jit(solution)/shard_map/all_to_all | solution.py:403
  179.1 26.2 %collective-permute-start.28 = (bf16[9,2,128,128]{3,2,1,0:T(8,128)(2,1)}, bf16[9,2,128,128]{3,2,1,0:T(8,128)(2,1)S(1)}, u32[]{:S(2)}, u32[]{:S(2)}) collective-permute-start(bf16[9,2,128,128]{3,2,1,0:T(8,128)(2,1)} %get-tuple-element.46), channel_id=1, source_target_pairs={{0,68},{1,69},{2,70},{3,71},{4,64},{5,65},{6,66},{7,67},{8,76},{9,... | collective-permute-start | bytes 1769480 | tf_op jit(solution)/shard_map/ppermute | solution.py:466
  182.2 21.5 %collective-permute-start.30 = (bf16[7,2,128,128]{3,2,1,0:T(8,128)(2,1)}, bf16[7,2,128,128]{3,2,1,0:T(8,128)(2,1)S(1)}, u32[]{:S(2)}, u32[]{:S(2)}) collective-permute-start(bf16[7,2,128,128]{3,2,1,0:T(8,128)(2,1)} %get-tuple-element.48), channel_id=1, source_target_pairs={{0,4},{1,5},{2,6},{3,7},{4,0},{5,1},{6,2},{7,3},{8,12},{9,13},{10,... | collective-permute-start | bytes 1376264 | tf_op jit(solution)/shard_map/ppermute | solution.py:45
  183.5 21.8 %collective-permute-start.31 = (bf16[7,2,128,128]{3,2,1,0:T(8,128)(2,1)}, bf16[7,2,128,128]{3,2,1,0:T(8,128)(2,1)S(1)}, u32[]{:S(2)}, u32[]{:S(2)}) collective-permute-start(bf16[7,2,128,128]{3,2,1,0:T(8,128)(2,1)} %get-tuple-element.49), channel_id=1, source_target_pairs={{0,68},{1,69},{2,70},{3,71},{4,64},{5,65},{6,66},{7,67},{8,76},{9,... | collective-permute-start | bytes 1376264 | tf_op jit(solution)/shard_map/ppermute | solution.py:466
  207.1 22.7 %all-to-all-start.1 = ((bf16[16,2,128,128]{3,2,1,0:T(8,128)(2,1)}), bf16[16,2,128,128]{3,2,1,0:T(8,128)(2,1)S(1)}, u32[]{:S(2)}, u32[]{:S(2)}) async-start(bf16[16,2,128,128]{3,2,1,0:T(8,128)(2,1)} %next_sums.1), calls=%async_computation.1 | async-start | bytes 2097152 | tf_op jit(solution)/shard_map/all_to_all | solution.py:403
  (38 other events, 341.9 us)
